TPU v7x, 256 devices: a whole 4x4x8 slice. The times are simulated.
256 devices in a mesh: seq: 32 (over z, y_lo, core), head: 8 (over y_hi, x).
Axes of the slice: x: 4, y: 4 (y_hi: 2, y_lo: 2; y = y_hi * 2 + y_lo), z: 8, core: 2. Of those that a mesh axis runs over, the one named last changes fastest.
Arguments:
- comp_q: bfloat16 [32, 192, 8, 640], P('seq', 'head'), may hold values from -8 to 8
- comp_k: bfloat16 [32, 192, 8, 128], P('seq', 'head'), may hold values from -6 to 6
- comp_v: bfloat16 [32, 192, 8, 128], P('seq', 'head'), may hold values from -24 to 24
- comp_grad: bfloat16 [32, 192, 8, 640], P('seq', 'head'), may hold values from -24 to 24
- prefix_k: bfloat16 [8192, 8, 128], P('seq', 'head'), may hold values from -8 to 8
- prefix_v: bfloat16 [8192, 8, 128], P('seq', 'head'), may hold values from -24 to 24
- comp_len: int32 [32], replicated, may hold values from 1 to 192, 3072 in all
Outputs:
- attn_out: bfloat16 [32, 192, 8, 640], P('seq', 'head')
- grad_q: bfloat16 [32, 192, 8, 640], P('seq', 'head')
- grad_k: bfloat16 [32, 192, 8, 128], P('seq', 'head')
- grad_v: bfloat16 [32, 192, 8, 128], P('seq', 'head')
- grad_prefix_k: float32 [8192, 8, 128], P('seq', 'head')
- grad_prefix_v: float32 [8192, 8, 128], P('seq', 'head')
Inputs may be any that keep to these rules, and one draw needn't show every extreme that they name: `comp_len`: the lengths sum to 3072 and the largest is 192.
All inputs are finite; a program needn't handle non-finite values.
Results may differ from a plain program's by a relative error of at most 0.011.
Values may be sent and summed in bfloat16 or wider, within the bound.
No kernel may reach another device: no remote copies, remote signals or barrier semaphores. Data moves between devices by JAX's collectives and lax.ppermute only.
A program may use at most 128 MiB of HBM per device.

v0:
```python
import math

import jax
import jax.numpy as jnp
from jax import lax
from jax.sharding import PartitionSpec as P

PROMPTS = 4


masked_fill = -1e30


def slot_pass(queries, cotangent, keys, values, length, prefix_len, scale):
    cap = queries.shape[0]
    scores = jnp.einsum("thgd,khd->hgtk", queries, keys, preferred_element_type=jnp.float32) * scale
    rows = lax.broadcasted_iota(jnp.int32, (cap, keys.shape[0]), 0)
    cols = lax.broadcasted_iota(jnp.int32, (cap, keys.shape[0]), 1) - prefix_len
    allowed = (cols < 0) | (cols <= rows) & (cols < length)
    live_rows = rows < length
    masked = jnp.where(allowed, scores, masked_fill)
    top = jnp.max(masked, axis=3, keepdims=True)
    log_total = top + jnp.log(jnp.sum(jnp.exp(masked - top), axis=3, keepdims=True))
    probs = jnp.where(allowed & live_rows, jnp.exp(masked - log_total), 0.0)
    probs_half = probs.astype(jnp.bfloat16)
    output = jnp.einsum("hgtk,khd->thgd", probs_half, values, preferred_element_type=jnp.float32)
    prob_grad = jnp.einsum("thgd,khd->hgtk", cotangent, values, preferred_element_type=jnp.float32)
    delta = jnp.sum(probs * prob_grad, axis=3, keepdims=True)
    score_grad = (probs * (prob_grad - delta)).astype(jnp.bfloat16)
    query_grad = (
        jnp.einsum("hgtk,khd->thgd", score_grad, keys, preferred_element_type=jnp.float32) * scale
    )
    key_grad = (
        jnp.einsum("hgtk,thgd->khd", score_grad, queries, preferred_element_type=jnp.float32)
        * scale
    )
    value_grad = jnp.einsum(
        "hgtk,thgd->khd", probs_half, cotangent, preferred_element_type=jnp.float32
    )
    return (output, query_grad, key_grad, value_grad)


def on_device(comp_q, comp_k, comp_v, comp_grad, prefix_k, prefix_v, comp_len):
    queries_all, cotangent_all, keys_own, values_own = (
        lax.all_to_all(comp_q, "head", split_axis=2, concat_axis=1, tiled=True),
        lax.all_to_all(comp_grad, "head", split_axis=2, concat_axis=1, tiled=True),
        lax.all_to_all(comp_k, "head", split_axis=2, concat_axis=1, tiled=True),
        lax.all_to_all(comp_v, "head", split_axis=2, concat_axis=1, tiled=True),
    )
    slots, cap, heads, width = queries_all.shape
    head_dim = keys_own.shape[3]
    group = width // head_dim
    devices = lax.axis_size("seq")
    per_group = devices // PROMPTS
    position = lax.axis_index("seq")
    prompt_len = prefix_k.shape[0] * per_group
    scale = 1.0 / math.sqrt(head_dim)
    first = position * slots
    lengths = lax.dynamic_slice_in_dim(comp_len, first, slots, 0)
    prompt_here = position % PROMPTS
    prefix_keys, prefix_values = (
        lax.all_gather(prefix_k, "seq", axis=0, tiled=True),
        lax.all_gather(prefix_v, "seq", axis=0, tiled=True),
    )
    start = prompt_here * prompt_len
    outputs, query_grads, key_grads, value_grads = ([], [], [], [])
    key_rows = lax.dynamic_slice_in_dim(prefix_keys, start, prompt_len, 0)
    value_rows = lax.dynamic_slice_in_dim(prefix_values, start, prompt_len, 0)
    queries = queries_all[0].reshape(cap, heads, group, head_dim)
    cotangent = cotangent_all[0].reshape(cap, heads, group, head_dim)
    keys = jnp.concatenate([key_rows, keys_own[0]], 0)
    values = jnp.concatenate([value_rows, values_own[0]], 0)
    output, query_grad, key_grad, value_grad = slot_pass(
        queries, cotangent, keys, values, lengths[0], prompt_len, scale
    )
    prompt_term = jnp.concatenate([key_grad[:prompt_len], value_grad[:prompt_len]], 2)
    outputs.append(output.reshape(cap, heads, width).astype(jnp.bfloat16))
    query_grads.append(query_grad.reshape(cap, heads, width).astype(jnp.bfloat16))
    key_grads.append(key_grad[prompt_len:].astype(jnp.bfloat16))
    value_grads.append(value_grad[prompt_len:].astype(jnp.bfloat16))
    whole_term = jnp.zeros((prefix_keys.shape[0], heads, 2 * head_dim), jnp.float32)
    whole_term = lax.dynamic_update_slice_in_dim(whole_term, prompt_term, start, 0)
    summed = lax.psum_scatter(whole_term, "seq", scatter_dimension=0, tiled=True)
    returned = (
        lax.all_to_all(jnp.stack(outputs), "head", split_axis=1, concat_axis=2, tiled=True),
        lax.all_to_all(jnp.stack(query_grads), "head", split_axis=1, concat_axis=2, tiled=True),
        lax.all_to_all(jnp.stack(key_grads), "head", split_axis=1, concat_axis=2, tiled=True),
        lax.all_to_all(jnp.stack(value_grads), "head", split_axis=1, concat_axis=2, tiled=True),
    )
    return (
        returned[0],
        returned[1],
        returned[2],
        returned[3],
        summed[:, :, :head_dim],
        summed[:, :, head_dim:],
    )


def solution(mesh):
    placed = (
        P("seq", "head", None, None),
        P("seq", "head", None, None),
        P("seq", "head", None, None),
        P("seq", "head", None, None),
        P("seq", "head", None),
        P("seq", "head", None),
        P(),
    )
    return jax.shard_map(
        on_device,
        mesh=mesh,
        in_specs=placed,
        out_specs=(
            P("seq", "head", None, None),
            P("seq", "head", None, None),
            P("seq", "head", None, None),
            P("seq", "head", None, None),
            P("seq", "head", None),
            P("seq", "head", None),
        ),
        check_vma=False,
    )
```

profile of v0, /device:TPU:24, one launch (start us, length us, event | category | flops | bytes accessed | tf_op | source)
XLA Modules:
  0.0 432.3 jit_solution(15813540640573410146)
XLA Ops:
  7.2 0.7 all-gather.5.cloned.1.call-update
  7.9 0.7 all-gather.3.cloned.1.call-update
  8.6 1.7 copy.56
  10.3 7.3 %all-to-all-start.2 = ((bf16[1,24,8,640]{3,1,0,2:T(8,128)(2,1)}), bf16[1,24,8,640]{3,1,0,2:T(8,128)(2,1)S(1)}, u32[]{:S(2)}, u32[]{:S(2)}) async-start(bf16[1,24,8,640]{3,1,0,2:T(8,128)(2,1)} %copy.56), calls=%async_computation.2 | async-start | bytes 491520 | tf_op jit(solution)/shard_map/all_to_all | solution.py:45
  17.6 1.7 copy.60
  19.2 1.2 dynamic_slice.10
  21.8 1.5 all-to-all-done.2
  23.3 6.3 %all-to-all-start.4 = ((bf16[1,24,8,640]{3,1,0,2:T(8,128)(2,1)}), bf16[1,24,8,640]{3,1,0,2:T(8,128)(2,1)S(1)}, u32[]{:S(2)}, u32[]{:S(2)}) async-start(bf16[1,24,8,640]{3,1,0,2:T(8,128)(2,1)} %copy.60), calls=%async_computation.4 | async-start | bytes 491520 | tf_op jit(solution)/shard_map/all_to_all | solution.py:46
  30.2 1.4 copy.54
  31.6 1.4 copy.55
  33.4 2.0 all-to-all-done.4
  35.4 6.2 %all-to-all-start.1 = ((bf16[1,24,8,128]{3,1,0,2:T(8,128)(2,1)}), bf16[1,24,8,128]{3,1,0,2:T(8,128)(2,1)S(1)}, u32[]{:S(2)}, u32[]{:S(2)}) async-start(bf16[1,24,8,128]{3,1,0,2:T(8,128)(2,1)} %copy.55), calls=%async_computation.1 | async-start | bytes 98304 | tf_op jit(solution)/shard_map/all_to_all | solution.py:47
  41.9 34.9 %all-gather.5.cloned.1.call-done = bf16[8192,1,128]{2,0,1:T(8,128)(2,1)} async-done(((bf16[256,1,128]{2,0,1:T(8,128)(2,1)}), bf16[8192,1,128]{2,0,1:T(8,128)(2,1)}) %all-gather.5.cloned.1.call-update) | async-done | bytes 2097168 | tf_op jit(solution)/shard_map/all_gather | solution.py:62
  76.8 1.1 constant_dynamic-slice_fusion
  77.9 7.1 %all-to-all-start = ((bf16[1,24,8,128]{3,1,0,2:T(8,128)(2,1)}), bf16[1,24,8,128]{3,1,0,2:T(8,128)(2,1)}, u32[]{:S(2)}, u32[]{:S(2)}) async-start(bf16[1,24,8,128]{3,1,0,2:T(8,128)(2,1)} %copy.54), calls=%async_computation | async-start | bytes 98304 | tf_op jit(solution)/shard_map/all_to_all | solution.py:48
  85.0 1.9 fusion.3
  86.9 2.4 exponential_reduce_fusion
  89.3 1.0 copy-done
  90.4 3.0 fusion.9
  93.4 49.7 %all-gather.3.cloned.1.call-done = bf16[8192,1,128]{2,0,1:T(8,128)(2,1)} async-done(((bf16[256,1,128]{2,0,1:T(8,128)(2,1)}), bf16[8192,1,128]{2,0,1:T(8,128)(2,1)}) %all-gather.3.cloned.1.call-update) | async-done | bytes 2097168 | tf_op jit(solution)/shard_map/all_gather | solution.py:63
  143.1 1.1 constant_dynamic-slice_fusion.1
  144.3 7.3 %fusion = (f32[5,192]{1,0:T(8,128)S(1)}, f32[2240,192,5]{0,1,2:T(8,128)S(1)}) fusion(f32[5,192]{1,0:T(8,128)S(1)} %log_add_fusion, f32[2240,192,5]{0,1,2:T(8,128)} %copy-done, pred[192,2240]{1,0:T(8,128)(4,1)S(1)} %get-tuple-element.27, pred[192,2240]{1,0:T(8,128)(4,1)S(1)} %get-tuple-element.26, bf16[192,5,128]{2,1,0:T(8,128)(2,1)} %copy-done.5, ...), kind=kOutput, calls=%fused_computation.3 | convolution fusion | flops 564550720 | bytes 18890240 | tf_op jit(solution)/shard_map/thgd,khd->hgtk/dot_general | solution.py:27
  151.7 3.5 fusion.4
  155.2 1.5 fusion.13
  157.0 0.7 copy-done.2
  157.7 5.5 %broadcast_in_dim.24 = f32[8192,1,256]{2,1,0:T(1,128)} broadcast(f32[]{:T(128)} %constant.40.clone.1), dimensions={} | broadcast | bytes 8388612 | tf_op jit(solution)/shard_map/broadcast_in_dim | solution.py:81
  163.2 9.9 %copy_dynamic-update-slice_fusion = f32[8192,1,256]{2,1,0:T(1,128)} fusion(f32[8192,1,256]{2,1,0:T(1,128)} %broadcast_in_dim.24, s32[]{:T(128)S(6)} %select_n.23, f32[2048,1,256]{2,0,1:T(8,128)S(1)} %pad_maximum_fusion), kind=kLoop, calls=%fused_computation.20 | loop fusion | bytes 4194308 | tf_op jit(solution)/shard_map/dynamic_update_slice | solution.py:82
  173.1 0.9 fusion.31
  174.6 0.9 reduce.5
  176.2 7.2 %all-to-all-start.6 = ((bf16[8,2,1536]{2,1,0:T(2,128)(2,1)}), bf16[8,2,1536]{2,1,0:T(2,128)(2,1)S(1)}, u32[]{:S(2)}, u32[]{:S(2)}) async-start(bf16[8,2,1536]{2,1,0:T(2,128)(2,1)} %reshape.128), calls=%async_computation.6 | async-start | bytes 98304 | tf_op jit(solution)/shard_map/all_to_all | solution.py:87
  183.5 0.9 reduce.6
  185.0 3.2 all-to-all-done.6
  188.9 6.2 %all-to-all-start.7 = ((bf16[8,2,1536]{2,1,0:T(2,128)(2,1)}), bf16[8,2,1536]{2,1,0:T(2,128)(2,1)S(1)}, u32[]{:S(2)}, u32[]{:S(2)}) async-start(bf16[8,2,1536]{2,1,0:T(2,128)(2,1)} %reshape.130), calls=%async_computation.7 | async-start | bytes 98304 | tf_op jit(solution)/shard_map/all_to_all | solution.py:88
  195.1 6.1 %fusion.21 = bf16[192,1,5,128]{3,0,2,1:T(8,128)(2,1)S(1)} fusion(bf16[192,1,128]{2,0,1:T(8,128)(2,1)} %bitcast.2, bf16[2048,1,128]{2,0,1:T(8,128)(2,1)S(1)} %constant_dynamic-slice_fusion.1, f32[5,192]{1,0:T(8,128)S(1)} %log_add_fusion, f32[2240,192,5]{0,1,2:T(8,128)} %copy-done, pred[192,2240]{1,0:T(8,128)(4,1)S(1)} %get-tuple-element.27, ...), kind=kOutput, calls=%fused_computation.27 | convolution fusion | flops 562524160 | bytes 10284800 | tf_op jit(solution)/shard_map/hgtk,khd->thgd/dot_general | solution.py:26
  201.4 0.9 copy.59
  202.3 2.1 reduce.3
  204.4 0.8 reshape.124
  205.1 7.2 %all-to-all-start.3 = ((bf16[8,2,7680]{2,1,0:T(2,128)(2,1)}), bf16[8,2,7680]{2,1,0:T(2,128)(2,1)S(1)}, u32[]{:S(2)}, u32[]{:S(2)}) async-start(bf16[8,2,7680]{2,1,0:T(2,128)(2,1)} %reshape.124), calls=%async_computation.3 | async-start | bytes 491520 | tf_op jit(solution)/shard_map/all_to_all | solution.py:85
  212.4 3.6 fusion.24
  216.2 0.9 copy.63
  217.0 2.1 reduce.4
  219.1 0.8 reshape.126
  219.9 7.2 %all-to-all-start.5 = ((bf16[8,2,7680]{2,1,0:T(2,128)(2,1)}), bf16[8,2,7680]{2,1,0:T(2,128)(2,1)S(1)}, u32[]{:S(2)}, u32[]{:S(2)}) async-start(bf16[8,2,7680]{2,1,0:T(2,128)(2,1)} %reshape.126), calls=%async_computation.5 | async-start | bytes 491520 | tf_op jit(solution)/shard_map/all_to_all | solution.py:86
  230.0 0.7 copy.69
  230.7 2.2 all-to-all-done.5
  233.1 0.7 copy.70
  233.8 189.9 %all-reduce.3.cloned.1.call-done = f32[8192,1,256]{2,1,0:T(1,128)} async-done(((f32[8192,1,256]{2,1,0:T(1,128)}), f32[8192,1,256]{2,1,0:T(1,128)}) %all-reduce.3.cloned.1.call-update) | async-done | bytes 8388624
  423.8 2.0 constant_dynamic-slice_fusion.3
  (64 shorter events, 8.3 us)
Async XLA Ops:
  7.2 69.7 %all-gather.5.cloned.1.call-start = ((), (), s32[]{:S(2)}) async-start(), calls=%async_computation.9 | async-start | bytes 2162688 | tf_op jit(solution)/shard_map/all_gather | solution.py:62
  7.9 135.2 %all-gather.3.cloned.1.call-start = ((), (), s32[]{:S(2)}) async-start(), calls=%async_computation.8 | async-start | bytes 2162688 | tf_op jit(solution)/shard_map/all_gather | solution.py:63
  10.3 13.0 %all-to-all-start.2 = ((bf16[1,24,8,640]{3,1,0,2:T(8,128)(2,1)}), bf16[1,24,8,640]{3,1,0,2:T(8,128)(2,1)S(1)}, u32[]{:S(2)}, u32[]{:S(2)}) async-start(bf16[1,24,8,640]{3,1,0,2:T(8,128)(2,1)} %copy.56), calls=%async_computation.2 | async-start | bytes 491520 | tf_op jit(solution)/shard_map/all_to_all | solution.py:45
  23.3 12.1 %all-to-all-start.4 = ((bf16[1,24,8,640]{3,1,0,2:T(8,128)(2,1)}), bf16[1,24,8,640]{3,1,0,2:T(8,128)(2,1)S(1)}, u32[]{:S(2)}, u32[]{:S(2)}) async-start(bf16[1,24,8,640]{3,1,0,2:T(8,128)(2,1)} %copy.60), calls=%async_computation.4 | async-start | bytes 491520 | tf_op jit(solution)/shard_map/all_to_all | solution.py:46
  33.4 53.6 %copy-start.3 = (bf16[192,5,128]{2,1,0:T(8,128)(2,1)}, bf16[192,5,128]{2,1,0:T(8,128)(2,1)S(1)}, u32[]{:S(2)}) copy-start(bf16[192,5,128]{2,1,0:T(8,128)(2,1)S(1)} %reshape.115) | copy-start | bytes 737284
  35.4 42.5 %all-to-all-start.1 = ((bf16[1,24,8,128]{3,1,0,2:T(8,128)(2,1)}), bf16[1,24,8,128]{3,1,0,2:T(8,128)(2,1)S(1)}, u32[]{:S(2)}, u32[]{:S(2)}) async-start(bf16[1,24,8,128]{3,1,0,2:T(8,128)(2,1)} %copy.55), calls=%async_computation.1 | async-start | bytes 98304 | tf_op jit(solution)/shard_map/all_to_all | solution.py:47
  41.9 51.5 %copy-start.5 = (bf16[192,5,128]{2,1,0:T(8,128)(2,1)}, bf16[192,5,128]{2,1,0:T(8,128)(2,1)S(1)}, u32[]{:S(2)}) copy-start(bf16[192,5,128]{2,1,0:T(8,128)(2,1)S(1)} %reshape.117) | copy-start | bytes 737284
  77.9 11.4 %copy-start.6 = (bf16[1,24,8,128]{3,1,0,2:T(8,128)(2,1)}, bf16[1,24,8,128]{3,1,0,2:T(8,128)(2,1)S(1)}, u32[]{:S(2)}) copy-start(bf16[1,24,8,128]{3,1,0,2:T(8,128)(2,1)S(1)} %all-to-all-done.1) | copy-start | bytes 147460
  77.9 66.3 %all-to-all-start = ((bf16[1,24,8,128]{3,1,0,2:T(8,128)(2,1)}), bf16[1,24,8,128]{3,1,0,2:T(8,128)(2,1)}, u32[]{:S(2)}, u32[]{:S(2)}) async-start(bf16[1,24,8,128]{3,1,0,2:T(8,128)(2,1)} %copy.54), calls=%async_computation | async-start | bytes 98304 | tf_op jit(solution)/shard_map/all_to_all | solution.py:48
  85.0 338.7 %all-reduce.3.cloned.1.call-start = ((), (), s32[]{:S(2)}) async-start(), calls=%async_computation.10 | async-start | bytes 16777216
  86.9 3.4 copy-start
  143.1 8.5 %slice-start = ((s8[8847360]{0:T(1024)(128)(4,1)}), s8[458752]{0:T(1024)(128)(4,1)S(1)}, s32[]{:S(2)}) async-start(s8[8847360]{0:T(1024)(128)(4,1)} %bitcast.156), calls=%async_computation.11 | async-start | bytes 917504
  144.3 7.4 %slice-start.1 = ((s8[8847360]{0:T(1024)(128)(4,1)}), s8[4194304]{0:T(1024)(128)(4,1)S(1)}, s32[]{:S(2)}) async-start(s8[8847360]{0:T(1024)(128)(4,1)} %bitcast.156), calls=%async_computation.12 | async-start | bytes 8388608
  144.3 7.4 %slice-start.2 = ((s8[8847360]{0:T(1024)(128)(4,1)}), s8[4194304]{0:T(1024)(128)(4,1)S(1)}, s32[]{:S(2)}) async-start(s8[8847360]{0:T(1024)(128)(4,1)} %bitcast.156), calls=%async_computation.13 | async-start | bytes 8388608
  151.7 3.5 copy-start.4
  155.2 7.9 %copy-start.1 = (bf16[5,192,2240]{2,1,0:T(8,128)(2,1)}, bf16[5,192,2240]{2,1,0:T(8,128)(2,1)S(1)}, u32[]{:S(2)}) copy-start(bf16[5,192,2240]{2,1,0:T(8,128)(2,1)S(1)} %fusion.4) | copy-start | bytes 12902404
  156.7 1.0 copy-start.2
  176.2 12.1 %all-to-all-start.6 = ((bf16[8,2,1536]{2,1,0:T(2,128)(2,1)}), bf16[8,2,1536]{2,1,0:T(2,128)(2,1)S(1)}, u32[]{:S(2)}, u32[]{:S(2)}) async-start(bf16[8,2,1536]{2,1,0:T(2,128)(2,1)} %reshape.128), calls=%async_computation.6 | async-start | bytes 98304 | tf_op jit(solution)/shard_map/all_to_all | solution.py:87
  188.2 0.6 copy-start.8
  188.9 16.3 %all-to-all-start.7 = ((bf16[8,2,1536]{2,1,0:T(2,128)(2,1)}), bf16[8,2,1536]{2,1,0:T(2,128)(2,1)S(1)}, u32[]{:S(2)}, u32[]{:S(2)}) async-start(bf16[8,2,1536]{2,1,0:T(2,128)(2,1)} %reshape.130), calls=%async_computation.7 | async-start | bytes 98304 | tf_op jit(solution)/shard_map/all_to_all | solution.py:88
  195.1 17.3 %copy-start.7 = (bf16[1,24,8,128]{3,1,0,2:T(8,128)(2,1)S(1)}, bf16[1,24,8,128]{3,1,0,2:T(8,128)(2,1)}, u32[]{:S(2)}) copy-start(bf16[1,24,8,128]{3,1,0,2:T(8,128)(2,1)} %copy-done.6) | copy-start | bytes 147460
  201.2 25.9 %copy-start.10 = (u32[256]{0:T(256)S(1)}, u32[256]{0:T(256)}, u32[]{:S(2)}) copy-start(u32[256]{0:T(256)} %constant.49) | copy-start | bytes 3076
  201.2 27.1 %copy-start.9 = (bf16[8,2,1536]{2,1,0:T(2,128)(2,1)S(1)}, bf16[8,2,1536]{2,1,0:T(2,128)(2,1)}, u32[]{:S(2)}) copy-start(bf16[8,2,1536]{2,1,0:T(2,128)(2,1)} %copy-done.8) | copy-start | bytes 147460
  205.1 14.8 %all-to-all-start.3 = ((bf16[8,2,7680]{2,1,0:T(2,128)(2,1)}), bf16[8,2,7680]{2,1,0:T(2,128)(2,1)S(1)}, u32[]{:S(2)}, u32[]{:S(2)}) async-start(bf16[8,2,7680]{2,1,0:T(2,128)(2,1)} %reshape.124), calls=%async_computation.3 | async-start | bytes 491520 | tf_op jit(solution)/shard_map/all_to_all | solution.py:85
  219.9 13.0 %all-to-all-start.5 = ((bf16[8,2,7680]{2,1,0:T(2,128)(2,1)}), bf16[8,2,7680]{2,1,0:T(2,128)(2,1)S(1)}, u32[]{:S(2)}, u32[]{:S(2)}) async-start(bf16[8,2,7680]{2,1,0:T(2,128)(2,1)} %reshape.126), calls=%async_computation.5 | async-start | bytes 491520 | tf_op jit(solution)/shard_map/all_to_all | solution.py:86
Sparse Core Ops, SparseCore 0:
  9.9 66.9 all-gather.4
  78.7 64.3 all-gather.2
  173.2 250.4 all-reduce.2
where the time goes:
time: 438 us; the launch traced here: 432 us
  waiting for transfers between devices  285 us (65%)
  starting transfers between devices  54.8 us (13%)
  local copies, waits for them, and re-layouts  40.5 us (9%)
  matrix products  23.4 us (5%)
  between operations  14.8 us (3%)
  other arithmetic  13.9 us (3%)
    unnamed x4, waiting for transfers between devices  191 us
    all_gather x1, waiting for transfers between devices, on_device(): lax.all_gather(prefix_v, 'seq', axis=0, tiled=True)  49.7 us
    all_gather x1, waiting for transfers between devices, on_device(): lax.all_gather(prefix_k, 'seq', axis=0, tiled=True)  34.9 us
    unnamed x50, local copies, waits for them, and re-layouts  15.8 us
    dynamic_update_slice x1, local copies, waits for them, and re-layouts, on_device(): lax.dynamic_update_slice_in_dim(whole_term, prompt_term, start, 0)  9.94 us
  transfers between devices with their start and end apart: 11, of which 7 were waited for; matrix products, arithmetic and copies ran while one was open for 11% of the time, Pallas kernels for 0%

commit v1 on v0

v1 whole, which is shorter than its diff:
```python
import functools
import math

import jax
import jax.numpy as jnp
from jax import lax
from jax.experimental import pallas as pl
from jax.experimental.pallas import tpu as pltpu
from jax.sharding import PartitionSpec as P

PROMPTS = 4
FILL = -1e30
VMEM = pltpu.VMEM
LIMIT = 8 * 1024 * 1024
f32 = jnp.float32
bf16 = jnp.bfloat16


def dot(a, b):
    return jnp.dot(a, b, preferred_element_type=f32)


def dot_t(a, b):
    return lax.dot_general(a, b, (((1,), (1,)), ((), ())), preferred_element_type=f32)


def pack_kernel(heads, q_ref, g_ref, k_ref, v_ref, out_ref, wide):
    rows, width = q_ref.shape
    slots = rows // heads
    head_dim = k_ref.shape[1]
    group = width // head_dim
    for i in range(group):
        wide[i] = q_ref[:, i * head_dim:(i + 1) * head_dim].astype(f32)
        wide[group + i] = g_ref[:, i * head_dim:(i + 1) * head_dim].astype(f32)
    wide[2 * group] = k_ref[...].astype(f32)
    wide[2 * group + 1] = v_ref[...].astype(f32)
    for i in range(2 * group + 2):
        parts = [wide[i, pl.ds(h, slots, stride=heads), :] for h in range(heads)]
        out_ref[:, i * head_dim:(i + 1) * head_dim] = jnp.concatenate(parts, 0).astype(bf16)


def pack(q, g, k, v):
    _, slots, heads, width = q.shape
    head_dim = k.shape[3]
    rows = slots * heads
    total = 2 * width + 2 * head_dim
    return pl.pallas_call(
        functools.partial(pack_kernel, heads),
        out_shape=jax.ShapeDtypeStruct((rows, total), bf16),
        scratch_shapes=[VMEM((total // head_dim, rows, head_dim), f32)],
        compiler_params=pltpu.CompilerParams(vmem_limit_bytes=LIMIT),
        cost_estimate=pl.CostEstimate(
            flops=rows * total, bytes_accessed=4 * rows * total, transcendentals=0
        ),
    )(
        q.reshape(rows, width),
        g.reshape(rows, width),
        k.reshape(rows, head_dim),
        v.reshape(rows, head_dim),
    )


def unpack_kernel(heads, x_ref, o_ref, dq_ref, dk_ref, dv_ref, wide):
    rows, total = x_ref.shape
    slots = rows // heads
    width, head_dim = o_ref.shape[1], dk_ref.shape[1]
    for col in range(0, total, head_dim):
        wide[col // head_dim] = x_ref[:, col:col + head_dim].astype(f32)
    for col in range(0, total, head_dim):
        parts = [
            wide[col // head_dim, pl.ds(t, heads, stride=slots), :] for t in range(slots)
        ]
        block = jnp.concatenate(parts, 0).astype(bf16)
        if col < width:
            o_ref[:, col:col + head_dim] = block
        elif col < 2 * width:
            dq_ref[:, col - width:col - width + head_dim] = block
        elif col == 2 * width:
            dk_ref[...] = block
        else:
            dv_ref[...] = block


def unpack(x, heads, width, head_dim):
    rows, total = x.shape
    slots = rows // heads
    outs = pl.pallas_call(
        functools.partial(unpack_kernel, heads),
        out_shape=[
            jax.ShapeDtypeStruct((rows, width), bf16),
            jax.ShapeDtypeStruct((rows, width), bf16),
            jax.ShapeDtypeStruct((rows, head_dim), bf16),
            jax.ShapeDtypeStruct((rows, head_dim), bf16),
        ],
        scratch_shapes=[VMEM((total // head_dim, rows, head_dim), f32)],
        compiler_params=pltpu.CompilerParams(vmem_limit_bytes=LIMIT),
        cost_estimate=pl.CostEstimate(
            flops=rows * total, bytes_accessed=4 * rows * total, transcendentals=0
        ),
    )(x)
    return [piece.reshape(1, slots, heads, piece.shape[1]) for piece in outs]


def stack_rows(x_ref, q_s, g_s, group):
    cap, head_dim = x_ref.shape[0], q_s.shape[1]
    width = group * head_dim
    for i in range(group):
        q_s[i * cap:(i + 1) * cap, :] = x_ref[:, i * head_dim:(i + 1) * head_dim]
        g_s[i * cap:(i + 1) * cap, :] = x_ref[:, width + i * head_dim:width + (i + 1) * head_dim]


def blocks_of(rows, cap):
    for start in range(0, rows, 256):
        stop = min(start + 256, rows)
        token = (lax.broadcasted_iota(jnp.int32, (1, stop - start), 1) + start) % cap
        yield start, stop, token


def causal(token, length, cap):
    key = lax.broadcasted_iota(jnp.int32, (cap, token.shape[1]), 0)
    return (key <= token) & (key < length)


def merge(state, s, d, turn, seen=None):
    if seen is not None:
        s = jnp.where(seen, s, FILL)
    high = jnp.max(s, axis=0, keepdims=True) * turn
    new = high if state is None else jnp.maximum(state[0], high)
    e = jnp.exp2(s * turn - new)
    if seen is not None:
        e = jnp.where(seen, e, 0.0)
    norm = jnp.sum(e, axis=0, keepdims=True)
    delta = jnp.sum(e * d, axis=0, keepdims=True)
    if state is not None:
        drop = jnp.exp2(state[0] - new)
        norm = norm + state[1] * drop
        delta = delta + state[2] * drop
    return e, (new, norm, delta)


def transposed(x):
    return x.astype(f32).T.astype(bf16)


def near_stats_kernel(group, chunks, scale, len_ref, x_ref, *refs):
    kv_refs, stats_ref, q_s, g_s = refs[:chunks], refs[chunks], refs[chunks + 1], refs[chunks + 2]
    cap, head_dim = x_ref.shape[0], q_s.shape[1]
    width = group * head_dim
    length = len_ref[lax.axis_index("seq")]
    turn = scale * math.log2(math.e)
    stack_rows(x_ref, q_s, g_s, group)
    for start, stop, token in blocks_of(group * cap, cap):
        q, g = q_s[start:stop, :], g_s[start:stop, :]
        state = None
        for kv in kv_refs:
            _, state = merge(state, dot_t(kv[0], q), dot_t(kv[1], g), turn)
        own_k = x_ref[:, 2 * width:2 * width + head_dim]
        own_v = x_ref[:, 2 * width + head_dim:]
        seen = causal(token, length, cap)
        _, state = merge(state, dot_t(own_k, q), dot_t(own_v, g), turn, seen)
        for i in range(3):
            stats_ref[i:i + 1, start:stop] = state[i]


def far_kernel(group, chunks, scale, len_ref, x_ref, stats_ref, *refs):
    count = chunks + 1
    shard_refs, grad_refs = refs[:count], refs[count:2 * count]
    k_refs = [shard_refs[0]] + [r.at[0] for r in shard_refs[2:]]
    v_refs = [shard_refs[1]] + [r.at[1] for r in shard_refs[2:]]
    dk_refs = [grad_refs[0]] + [r.at[0] for r in grad_refs[2:]]
    dv_refs = [grad_refs[1]] + [r.at[1] for r in grad_refs[2:]]
    (total_ref, ot_ref, qt_ref,
     q_s, g_s, keys_t, values_t, e_s, d_s, pb_s, sb_s, dk_s, dv_s) = refs[2 * count:]
    cap = x_ref.shape[0]
    span, head_dim = shard_refs[0].shape
    length = len_ref[lax.axis_index("seq")]
    turn = scale * math.log2(math.e)
    stack_rows(x_ref, q_s, g_s, group)
    for i in range(chunks):
        keys_t[:, i * span:(i + 1) * span] = transposed(k_refs[i][...])
        values_t[:, i * span:(i + 1) * span] = transposed(v_refs[i][...])
    for start, stop, token in blocks_of(group * cap, cap):
        size = stop - start
        q, g = q_s[start:stop, :], g_s[start:stop, :]
        state = tuple(stats_ref[i:i + 1, start:stop] for i in range(3))
        tops = []
        for i in range(chunks):
            d = dot_t(v_refs[i][...], g)
            e, state = merge(state, dot_t(k_refs[i][...], q), d, turn)
            e_s[i * span:(i + 1) * span, :size] = e
            d_s[i * span:(i + 1) * span, :size] = d
            tops.append(state[0])
        top, norm, delta = state
        delta = delta / norm
        live = token < length
        total_ref[0:1, start:stop] = jnp.where(live, top + jnp.log2(norm), -FILL)
        total_ref[1:2, start:stop] = delta
        inverse = jnp.where(live, 1.0 / norm, 0.0)
        for i in range(chunks):
            lo, hi = i * span, (i + 1) * span
            p = e_s[lo:hi, :size] * (jnp.exp2(tops[i] - top) * inverse)
            pb = p.astype(bf16)
            sb = (p * (d_s[lo:hi, :size] - delta)).astype(bf16)
            pb_s[lo:hi, :size] = pb
            sb_s[lo:hi, :size] = sb
            dv, dk = dot(pb, g), dot(sb, q)
            if start == 0:
                dv_s[lo:hi, :] = dv
                dk_s[lo:hi, :] = dk
            else:
                dv_s[lo:hi, :] += dv
                dk_s[lo:hi, :] += dk
        ot_ref[:, start:stop] = dot(values_t[...], pb_s[:, :size])
        qt_ref[:, start:stop] = dot(keys_t[...], sb_s[:, :size])
    for i in range(chunks):
        dk_refs[i][...] = (dk_s[i * span:(i + 1) * span, :] * scale).astype(bf16)
        dv_refs[i][...] = dv_s[i * span:(i + 1) * span, :].astype(bf16)


def near_kernel(group, chunks, scale, len_ref, x_ref, total_ref, ot_ref, qt_ref, *refs):
    kv_refs = refs[:chunks]
    out_ref = refs[chunks]
    grad_refs = refs[chunks + 1:2 * chunks + 1]
    q_s, g_s, keys_t, values_t, pb_s, sb_s, ot_s, qt_s, dk_s, dv_s = refs[2 * chunks + 1:]
    cap = x_ref.shape[0]
    span, head_dim = kv_refs[0].shape[1:]
    width = group * head_dim
    prefix = chunks * span
    length = len_ref[lax.axis_index("seq")]
    turn = scale * math.log2(math.e)
    stack_rows(x_ref, q_s, g_s, group)

    def pair(i):
        if i < chunks:
            return kv_refs[i][0], kv_refs[i][1]
        return x_ref[:, 2 * width:2 * width + head_dim], x_ref[:, 2 * width + head_dim:]

    bounds = [(i * span, (i + 1) * span) for i in range(chunks)] + [(prefix, prefix + cap)]
    for i, (lo, hi) in enumerate(bounds):
        k, v = pair(i)
        keys_t[:, lo:hi] = transposed(k)
        values_t[:, lo:hi] = transposed(v)
    for start, stop, token in blocks_of(group * cap, cap):
        size = stop - start
        q, g = q_s[start:stop, :], g_s[start:stop, :]
        total = total_ref[0:1, start:stop]
        delta = total_ref[1:2, start:stop]
        for i, (lo, hi) in enumerate(bounds):
            k, v = pair(i)
            p = jnp.exp2(dot_t(k, q) * turn - total)
            if i == chunks:
                p = jnp.where(causal(token, length, cap), p, 0.0)
            pb = p.astype(bf16)
            sb = (p * (dot_t(v, g) - delta)).astype(bf16)
            pb_s[lo:hi, :size] = pb
            sb_s[lo:hi, :size] = sb
            dv, dk = dot(pb, g), dot(sb, q)
            if start == 0:
                dv_s[lo:hi, :] = dv
                dk_s[lo:hi, :] = dk
            else:
                dv_s[lo:hi, :] += dv
                dk_s[lo:hi, :] += dk
        ot_s[:, start:stop] = ot_ref[:, start:stop] + dot(values_t[...], pb_s[:, :size])
        qt_s[:, start:stop] = qt_ref[:, start:stop] + dot(keys_t[...], sb_s[:, :size])
    for i in range(chunks):
        lo, hi = bounds[i]
        grad_refs[i][0] = dk_s[lo:hi, :] * scale
        grad_refs[i][1] = dv_s[lo:hi, :]
    out_ref[:, 2 * width:2 * width + head_dim] = (dk_s[prefix:, :] * scale).astype(bf16)
    out_ref[:, 2 * width + head_dim:] = dv_s[prefix:, :].astype(bf16)
    out = ot_s[...].T
    grad_q = (qt_s[...] * scale).T
    for i in range(group):
        out_ref[:, i * head_dim:(i + 1) * head_dim] = out[i * cap:(i + 1) * cap].astype(bf16)
        out_ref[:, width + i * head_dim:width + (i + 1) * head_dim] = (
            grad_q[i * cap:(i + 1) * cap].astype(bf16)
        )


def call(body, products, keys, rows, head_dim, ins, outs, scratch, limit):
    smem = pl.BlockSpec(memory_space=pltpu.SMEM)
    vmem = pl.BlockSpec(memory_space=pltpu.VMEM)
    return pl.pallas_call(
        body,
        out_shape=outs,
        in_specs=[smem] + [vmem] * (len(ins) - 1),
        out_specs=[vmem] * len(outs),
        scratch_shapes=scratch,
        compiler_params=pltpu.CompilerParams(vmem_limit_bytes=limit * 1024 * 1024),
        cost_estimate=pl.CostEstimate(
            flops=2 * products * rows * keys * head_dim,
            bytes_accessed=sum(x.size * x.dtype.itemsize for x in ins + outs),
            transcendentals=rows * keys,
        ),
    )(*ins)


def near_stats(lengths, x, shards, group, scale):
    cap = x.shape[0]
    _, span, head_dim = shards[0].shape
    rows, keys = group * cap, len(shards) * span + cap
    return call(
        functools.partial(near_stats_kernel, group, len(shards), scale),
        2, keys, rows, head_dim,
        [lengths, x, *shards],
        [jax.ShapeDtypeStruct((3, rows), f32)],
        [VMEM((rows, head_dim), bf16)] * 2,
        12,
    )[0]


def far_pass(lengths, x, stats, shards, group, scale):
    cap = x.shape[0]
    span, head_dim = shards[0].shape
    chunks = len(shards) - 1
    rows, keys = group * cap, chunks * span
    outs = call(
        functools.partial(far_kernel, group, chunks, scale),
        6, keys, rows, head_dim,
        [lengths, x, stats, *shards],
        [jax.ShapeDtypeStruct(shard.shape, bf16) for shard in shards]
        + [jax.ShapeDtypeStruct((2, rows), f32)]
        + [jax.ShapeDtypeStruct((head_dim, rows), f32)] * 2,
        [VMEM((rows, head_dim), bf16)] * 2
        + [VMEM((head_dim, keys), bf16)] * 2
        + [VMEM((keys, 256), f32)] * 2
        + [VMEM((keys, 256), bf16)] * 2
        + [VMEM((keys, head_dim), f32)] * 2,
        24,
    )
    return outs[:chunks + 1], outs[chunks + 1:]


def near_pass(lengths, x, totals, shards, group, scale):
    cap, packed = x.shape
    _, span, head_dim = shards[0].shape
    rows, keys = group * cap, len(shards) * span + cap
    outs = call(
        functools.partial(near_kernel, group, len(shards), scale),
        6, keys, rows, head_dim,
        [lengths, x, *totals, *shards],
        [jax.ShapeDtypeStruct((cap, packed), bf16)]
        + [jax.ShapeDtypeStruct((2, span, head_dim), f32)] * len(shards),
        [VMEM((rows, head_dim), bf16)] * 2
        + [VMEM((head_dim, keys), bf16)] * 2
        + [VMEM((keys, 256), bf16)] * 2
        + [VMEM((head_dim, rows), f32)] * 2
        + [VMEM((keys, head_dim), f32)] * 2,
        24,
    )
    return outs[0], outs[1:]


def on_device(comp_q, comp_k, comp_v, comp_grad, prefix_k, prefix_v, comp_len):
    _, slots, heads, width = comp_q.shape
    head_dim = comp_k.shape[3]
    group = width // head_dim
    devices = lax.axis_size("seq")
    ring = devices // PROMPTS
    scale = 1.0 / math.sqrt(head_dim)

    to_prompt = []
    for owner in range(devices):
        plane, lane = divmod(owner, PROMPTS)
        reach = (0, 3, 1, 2)[lane]
        target = (plane + reach if plane % 2 else plane - reach) % ring
        to_prompt.append((owner, target * PROMPTS + owner // ring))
    to_owner = [(b, a) for a, b in to_prompt]

    def shift(x, steps):
        pairs = [(s, (s + PROMPTS * steps) % devices) for s in range(devices)]
        return lax.ppermute(x, "seq", pairs)

    own = lax.ppermute(jnp.stack([prefix_k[:, 0], prefix_v[:, 0]]), "seq", to_prompt)
    packed = pack(comp_q, comp_grad, comp_k, comp_v)
    own, packed = lax.optimization_barrier((own, packed))
    x = lax.all_to_all(packed, "head", split_axis=0, concat_axis=0, tiled=True)

    up, down = shift(own, 1), shift(own, -1)
    far_keys = shift(down[0], -3)
    far_values = shift(up[1], 3)
    up3, down3 = shift(up, 2), shift(down, -2)
    up2, down2 = shift(up, 1), shift(down, -1)

    near = [own, up, down]
    stats = near_stats(comp_len, x, near, group, scale)
    grads, totals = far_pass(
        comp_len, x, stats, [far_keys, far_values, up3, down3, up2, down2], group, scale
    )
    moved = [
        shift(grad, steps).astype(f32) for grad, steps in zip(grads, (3, -3, -2, 2, -1, 1))
    ]
    out, (own_grad, up_grad, down_grad) = near_pass(comp_len, x, totals, near, group, scale)
    far_dk, far_dv, up3, down3, up2, down2 = moved
    up_sum = up_grad + up2 + up3
    down_sum = down_grad + down2 + down3
    up_sum = up_sum + jnp.pad(far_dv[None], ((1, 0), (0, 0), (0, 0)))
    down_sum = down_sum + jnp.pad(far_dk[None], ((0, 1), (0, 0), (0, 0)))
    back = lax.all_to_all(out, "head", split_axis=0, concat_axis=0, tiled=True)
    up_sum = shift(up_sum.astype(bf16), -1)
    down_sum = shift(down_sum.astype(bf16), 1)
    summed = own_grad + up_sum.astype(f32) + down_sum.astype(f32)
    attn_out, grad_q, grad_k, grad_v = unpack(back, heads, width, head_dim)
    placed = lax.ppermute(summed.astype(bf16), "seq", to_owner).astype(f32)
    return (attn_out, grad_q, grad_k, grad_v, placed[0][:, None], placed[1][:, None])


def solution(mesh):
    tokens = P("seq", "head", None, None)
    prefix = P("seq", "head", None)
    return jax.shard_map(
        on_device,
        mesh=mesh,
        in_specs=(tokens, tokens, tokens, tokens, prefix, prefix, P()),
        out_specs=(tokens, tokens, tokens, tokens, prefix, prefix),
        check_vma=False,
    )
```

time: 438 us -> 95.9 us (0.22); the launches traced: 432 us -> 95.4 us
  waiting for transfers between devices: 285 us -> 24.9 us
  local copies, waits for them, and re-layouts: 40.5 us -> 3.27 us
  matrix products: 23.4 us -> 0 us
  Pallas kernels: 0 us -> 15.8 us
  between operations: 14.8 us -> 0.77 us
  other arithmetic: 13.9 us -> 1.11 us
  starting transfers between devices: 54.8 us -> 49.6 us
    unnamed x4 -> x0, waiting for transfers between devices: 191 us -> none
    all_gather x2 -> x0, waiting for transfers between devices: 84.6 us -> none  [the longest x1 49.7 us: on_device(): lax.all_gather(prefix_v, 'seq', axis=0, tiled=True)]
    all_to_all x8 -> x2, starting transfers between devices: 54.7 us -> 14.5 us  [the longest x1 7.26 us: on_device(): x = lax.all_to_all(packed, 'head', split_axis=0, concat_axis=0, tiled=True)]
    ppermute x0 -> x18, starting transfers between devices: none -> 35.1 us  [the longest x16 25.2 us: shift(): return lax.ppermute(x, 'seq', pairs)]
    ppermute x0 -> x18, waiting for transfers between devices: none -> 24.9 us  [the longest x16 14.4 us: shift(): return lax.ppermute(x, 'seq', pairs)]
    dot_general x6 -> x0, matrix products: 23.4 us -> none  [the longest x1 7.35 us: slot_pass(): jnp.einsum('thgd,khd->hgtk', cotangent, values, preferred_element_type=jn...]
    pallas_call x0 -> x5, Pallas kernels: none -> 15.8 us  [the longest x3 13.7 us: call(): pl.pallas_call(body, out_shape=outs, in_specs=[smem] + [vmem] * (len(ins)...]
    unnamed x50 -> x10, local copies, waits for them, and re-layouts: 15.8 us -> 2.54 us
  transfers between devices with their start and end apart: 11 -> 20, of which waited for: 7 -> 6; matrix products, arithmetic and copies ran while one was open for 11% -> 1% of each run, Pallas kernels for 0% -> 10%
where the time goes in v1:
time: 95.9 us; the launch traced here: 95.4 us
  starting transfers between devices  49.6 us (52%)
  waiting for transfers between devices  24.9 us (26%)
  Pallas kernels  15.8 us (16%)
  local copies, waits for them, and re-layouts  3.27 us (3%)
  other arithmetic  1.11 us (1%)
    ppermute x16, starting transfers between devices, shift(): return lax.ppermute(x, 'seq', pairs)  25.2 us
    ppermute x16, waiting for transfers between devices, shift(): return lax.ppermute(x, 'seq', pairs)  14.4 us
    pallas_call x3, Pallas kernels, call(): pl.pallas_call(body, out_shape=outs, in_specs=[smem] + [vmem] * (len(ins)...  13.7 us
    ppermute x1, waiting for transfers between devices, on_device(): placed = lax.ppermute(summed.astype(bf16), 'seq', to_owner).astype(f32)  10.4 us
    ppermute x1, starting transfers between devices, on_device(): lax.ppermute(jnp.stack([prefix_k[:, 0], prefix_v[:, 0]]), 'seq', to_prompt)  7.94 us
    all_to_all x1, starting transfers between devices, on_device(): x = lax.all_to_all(packed, 'head', split_axis=0, concat_axis=0, tiled=True)  7.26 us
    all_to_all x1, starting transfers between devices, on_device(): back = lax.all_to_all(out, 'head', split_axis=0, concat_axis=0, tiled=True)  7.24 us
    unnamed x10, local copies, waits for them, and re-layouts  2.54 us
  transfers between devices with their start and end apart: 20, of which 6 were waited for; matrix products, arithmetic and copies ran while one was open for 1% of the time, Pallas kernels for 10%

profile of v1, /device:TPU:24, one launch (start us, length us, event | category | flops | bytes accessed | tf_op | source)
XLA Modules:
  0.0 95.4 jit_solution(2629798545888264352)
XLA Ops:
  0.6 0.9 pad_maximum_fusion
  1.6 7.9 %collective-permute-start = (bf16[2,256,128]{2,1,0:T(8,128)(2,1)S(1)}, bf16[2,256,128]{2,1,0:T(8,128)(2,1)S(1)}, u32[]{:S(2)}, u32[]{:S(2)}) collective-permute-start(bf16[2,256,128]{2,1,0:T(8,128)(2,1)S(1)} %pad_maximum_fusion), channel_id=1, source_target_pairs={{0,0},{8,160},{16,224},{24,192},{32,32},{40,128},{48,64},{56,96},{... | collective-permute-start | bytes 393224 | tf_op jit(solution)/shard_map/ppermute | solution.py:375
  9.5 0.0 copy-start.1
  9.5 0.9 copy-done.1
  10.5 0.8 copy-done.2
  11.3 0.8 copy-done.3
  12.1 1.1 %shard_map.118 = bf16[192,1536]{1,0:T(8,128)(2,1)} custom-call(bf16[192,640]{1,0:T(8,128)(2,1)S(1)} %bitcast.30, bf16[192,640]{1,0:T(8,128)(2,1)S(1)} %bitcast.31, bf16[192,128]{1,0:T(8,128)(2,1)S(1)} %bitcast.32, bf16[192,128]{1,0:T(8,128)(2,1)S(1)} %bitcast.33), custom_call_target="tpu_custom_call" | custom-call | flops 294912 | bytes 1179648 | tf_op jit(solution)/shard_map/pallas_call | solution.py:47
  13.2 0.1 collective-permute-done.refs_0_
  13.3 2.6 %collective-permute-start.2 = (bf16[2,256,128]{2,1,0:T(8,128)(2,1)S(1)}, bf16[2,256,128]{2,1,0:T(8,128)(2,1)S(1)}, u32[]{:S(2)}, u32[]{:S(2)}) collective-permute-start(bf16[2,256,128]{2,1,0:T(8,128)(2,1)S(1)} %collective-permute-done.refs_0_), channel_id=1, source_target_pairs={{0,224},{8,232},{16,240},{24,248},{32,0},{40,8},{48,16},{56,24},{6... | collective-permute-start | bytes 393224 | tf_op jit(solution)/shard_map/ppermute | solution.py:373
  15.9 7.3 %all-to-all-start = ((bf16[8,24,1536]{2,1,0:T(8,128)(2,1)}), bf16[8,24,1536]{2,1,0:T(8,128)(2,1)S(1)}, u32[]{:S(2)}, u32[]{:S(2)}) async-start(bf16[8,24,1536]{2,1,0:T(8,128)(2,1)} %bitcast.6), calls=%async_computation | async-start | bytes 1179648 | tf_op jit(solution)/shard_map/all_to_all | solution.py:378
  23.2 0.0 collective-permute-start.1
  23.2 0.0 collective-permute-done.2.refs_2_
  23.2 1.7 %collective-permute-start.3 = (bf16[256,128]{1,0:T(8,128)(2,1)S(1)}, bf16[256,128]{1,0:T(8,128)(2,1)S(1)}, u32[]{:S(2)}, u32[]{:S(2)}) collective-permute-start(bf16[256,128]{1,0:T(8,128)(2,1)S(1)} %slice_bitcast_fusion.1), channel_id=1, source_target_pairs={{0,160},{8,168},{16,176},{24,184},{32,192},{40,200},{48,208},{56,2... | collective-permute-start | bytes 196616 | tf_op jit(solution)/shard_map/ppermute | solution.py:373
  24.8 1.7 %collective-permute-start.8 = (bf16[2,256,128]{2,1,0:T(8,128)(2,1)S(1)}, bf16[2,256,128]{2,1,0:T(8,128)(2,1)S(1)}, u32[]{:S(2)}, u32[]{:S(2)}) collective-permute-start(bf16[2,256,128]{2,1,0:T(8,128)(2,1)S(1)} %collective-permute-done.2.refs_2_), channel_id=1, source_target_pairs={{0,224},{8,232},{16,240},{24,248},{32,0},{40,8},{48,16},{56,24},{6... | collective-permute-start | bytes 393224 | tf_op jit(solution)/shard_map/ppermute | solution.py:373
  26.6 1.4 %collective-permute-start.6 = (bf16[2,256,128]{2,1,0:T(8,128)(2,1)S(1)}, bf16[2,256,128]{2,1,0:T(8,128)(2,1)S(1)}, u32[]{:S(2)}, u32[]{:S(2)}) collective-permute-start(bf16[2,256,128]{2,1,0:T(8,128)(2,1)S(1)} %collective-permute-done.2.refs_2_), channel_id=1, source_target_pairs={{0,192},{8,200},{16,208},{24,216},{32,224},{40,232},{48,240},{56,2... | collective-permute-start | bytes 393224 | tf_op jit(solution)/shard_map/ppermute | solution.py:373
  28.0 1.3 %collective-permute-done.1.refs_1_ = bf16[2,256,128]{2,1,0:T(8,128)(2,1)S(1)} collective-permute-done((bf16[2,256,128]{2,1,0:T(8,128)(2,1)S(1)}, bf16[2,256,128]{2,1,0:T(8,128)(2,1)S(1)}, u32[]{:S(2)}, u32[]{:S(2)}) %collective-permute-start.1) | collective-permute-done | bytes 131104 | tf_op jit(solution)/shard_map/ppermute | solution.py:373
  29.3 0.7 collective-permute-start.7
  30.0 0.9 collective-permute-start.5
  30.9 1.2 %collective-permute-done.3.refs_0_ = bf16[256,128]{1,0:T(8,128)(2,1)S(1)} collective-permute-done((bf16[256,128]{1,0:T(8,128)(2,1)S(1)}, bf16[256,128]{1,0:T(8,128)(2,1)S(1)}, u32[]{:S(2)}, u32[]{:S(2)}) %collective-permute-start.3) | collective-permute-done | bytes 65568 | tf_op jit(solution)/shard_map/ppermute | solution.py:373
  32.1 2.6 %collective-permute-start.4 = (bf16[256,128]{1,0:T(8,128)(2,1)S(1)}, bf16[256,128]{1,0:T(8,128)(2,1)S(1)}, u32[]{:S(2)}, u32[]{:S(2)}) collective-permute-start(bf16[256,128]{1,0:T(8,128)(2,1)S(1)} %slice_bitcast_fusion), channel_id=1, source_target_pairs={{0,96},{8,104},{16,112},{24,120},{32,128},{40,136},{48,144},{56,15... | collective-permute-start | bytes 196616 | tf_op jit(solution)/shard_map/ppermute | solution.py:373
  34.7 0.0 all-to-all-done
  34.7 2.3 %shard_map.119.stats_ref = f32[3,960]{1,0:T(4,128)S(1)} custom-call(s32[32]{0:T(128)S(1)} %copy-done.4, bf16[192,1536]{1,0:T(8,128)(2,1)S(1)} %bitcast.27, bf16[2,256,128]{2,1,0:T(8,128)(2,1)S(1)} %collective-permute-done.refs_0_, bf16[2,256,128]{2,1,0:T(8,128)(2,1)S(1)} %collective-permute-done.1.refs_1_, ...), custom_call_target="tpu_custom_call" | custom-call | flops 471859200 | bytes 994688 | tf_op jit(solution)/shard_map/pallas_call | solution.py:284
  37.1 6.3 %collective-permute-done.4.refs_1_ = bf16[256,128]{1,0:T(8,128)(2,1)S(1)} collective-permute-done((bf16[256,128]{1,0:T(8,128)(2,1)S(1)}, bf16[256,128]{1,0:T(8,128)(2,1)S(1)}, u32[]{:S(2)}, u32[]{:S(2)}) %collective-permute-start.4) | collective-permute-done | bytes 65568 | tf_op jit(solution)/shard_map/ppermute | solution.py:373
  43.4 0.0 collective-permute-done.8.refs_5_
  43.4 0.0 collective-permute-done.6.refs_3_
  43.4 0.0 collective-permute-done.7.refs_4_
  43.4 5.6 %shard_map.120 = (bf16[256,128]{1,0:T(8,128)(2,1)S(1)}, bf16[256,128]{1,0:T(8,128)(2,1)S(1)}, bf16[2,256,128]{2,1,0:T(8,128)(2,1)S(1)}, bf16[2,256,128]{2,1,0:T(...) custom-call(s32[32]{0:T(128)S(1)} %copy-done.4, ...), custom_call_target="tpu_custom_call" | custom-call | flops 1887436800 | bytes 2902912 | tf_op jit(solution)/shard_map/pallas_call | solution.py:284
  49.0 2.4 %collective-permute-start.11 = (bf16[256,128]{1,0:T(8,128)(2,1)S(1)}, bf16[256,128]{1,0:T(8,128)(2,1)S(1)}, u32[]{:S(2)}, u32[]{:S(2)}) collective-permute-start(bf16[256,128]{1,0:T(8,128)(2,1)S(1)} %get-tuple-element.39), channel_id=1, source_target_pairs={{0,160},{8,168},{16,176},{24,184},{32,192},{40,200},{48,208},{56,2... | collective-permute-start | bytes 196616 | tf_op jit(solution)/shard_map/ppermute | solution.py:373
  51.4 1.5 %collective-permute-start.15 = (bf16[256,128]{1,0:T(8,128)(2,1)S(1)}, bf16[256,128]{1,0:T(8,128)(2,1)S(1)}, u32[]{:S(2)}, u32[]{:S(2)}) collective-permute-start(bf16[256,128]{1,0:T(8,128)(2,1)S(1)} %get-tuple-element.43), channel_id=1, source_target_pairs={{0,96},{8,104},{16,112},{24,120},{32,128},{40,136},{48,144},{56,15... | collective-permute-start | bytes 196616 | tf_op jit(solution)/shard_map/ppermute | solution.py:373
  52.9 1.7 %collective-permute-start.9 = (bf16[2,256,128]{2,1,0:T(8,128)(2,1)S(1)}, bf16[2,256,128]{2,1,0:T(8,128)(2,1)S(1)}, u32[]{:S(2)}, u32[]{:S(2)}) collective-permute-start(bf16[2,256,128]{2,1,0:T(8,128)(2,1)S(1)} %get-tuple-element.37), channel_id=1, source_target_pairs={{0,224},{8,232},{16,240},{24,248},{32,0},{40,8},{48,16},{56,24},{6... | collective-permute-start | bytes 393224 | tf_op jit(solution)/shard_map/ppermute | solution.py:373
  54.6 3.1 %collective-permute-start.10 = (bf16[2,256,128]{2,1,0:T(8,128)(2,1)S(1)}, bf16[2,256,128]{2,1,0:T(8,128)(2,1)S(1)}, u32[]{:S(2)}, u32[]{:S(2)}) collective-permute-start(bf16[2,256,128]{2,1,0:T(8,128)(2,1)S(1)} %get-tuple-element.38), channel_id=1, source_target_pairs={{0,192},{8,200},{16,208},{24,216},{32,224},{40,232},{48,240},{56,2... | collective-permute-start | bytes 393224 | tf_op jit(solution)/shard_map/ppermute | solution.py:373
  57.8 2.0 %collective-permute-start.13 = (bf16[2,256,128]{2,1,0:T(8,128)(2,1)S(1)}, bf16[2,256,128]{2,1,0:T(8,128)(2,1)S(1)}, u32[]{:S(2)}, u32[]{:S(2)}) collective-permute-start(bf16[2,256,128]{2,1,0:T(8,128)(2,1)S(1)} %get-tuple-element.41), channel_id=1, source_target_pairs={{0,32},{8,40},{16,48},{24,56},{32,64},{40,72},{48,80},{56,88},{64,... | collective-permute-start | bytes 393224 | tf_op jit(solution)/shard_map/ppermute | solution.py:373
  59.8 5.8 %shard_map.121 = (bf16[192,1536]{1,0:T(8,128)(2,1)}, f32[2,256,128]{2,1,0:T(8,128)S(1)}, f32[2,256,128]{2,1,0:T(8,128)S(1)}, f32[2,256,128]{2,1,0:T(8,128)S(1)}) custom-call(s32[32]{0:T(128)S(1)} %copy-done.4, bf16[192,1536]{1,0:T(8,128)(2,1)S(1)} %bitcast.29, f32[2,960]{1,0:T(2,128)S(1)} %get-tuple-element.27.total_ref, ...), custom_call_target="tpu_custom_call" | custom-call | flops 1415577600 | bytes 3350144 | tf_op jit(solution)/shard_map/pallas_call | solution.py:284
  65.5 0.0 collective-permute-done.11
  65.6 0.0 collective-permute-done.10
  65.6 0.1 add_convert_fusion.2
  65.6 2.7 %collective-permute-start.12 = (bf16[2,256,128]{2,1,0:T(8,128)(2,1)S(1)}, bf16[2,256,128]{2,1,0:T(8,128)(2,1)S(1)}, u32[]{:S(2)}, u32[]{:S(2)}) collective-permute-start(bf16[2,256,128]{2,1,0:T(8,128)(2,1)S(1)} %add_convert_fusion.2), channel_id=1, source_target_pairs={{0,224},{8,232},{16,240},{24,248},{32,0},{40,8},{48,16},{56,24},{6... | collective-permute-start | bytes 393224 | tf_op jit(solution)/shard_map/ppermute | solution.py:373
  68.4 0.0 collective-permute-done.15
  68.4 5.6 %collective-permute-done.14 = bf16[2,256,128]{2,1,0:T(8,128)(2,1)S(1)} collective-permute-done((bf16[2,256,128]{2,1,0:T(8,128)(2,1)S(1)}, bf16[2,256,128]{2,1,0:T(8,128)(2,1)S(1)}, u32[]{:S(2)}, u32[]{:S(2)}) %collective-permute-start.14) | collective-permute-done | bytes 131104 | tf_op jit(solution)/shard_map/ppermute | solution.py:373
  73.9 0.1 add_convert_fusion.1
  74.0 0.1 collective-permute-start.16
  74.1 7.2 %all-to-all-start.1 = ((bf16[8,24,1536]{2,1,0:T(8,128)(2,1)}), bf16[8,24,1536]{2,1,0:T(8,128)(2,1)S(1)}, u32[]{:S(2)}, u32[]{:S(2)}) async-start(bf16[8,24,1536]{2,1,0:T(8,128)(2,1)} %bitcast.10), calls=%async_computation.1 | async-start | bytes 1179648 | tf_op jit(solution)/shard_map/all_to_all | solution.py:400
  81.4 0.0 collective-permute-done.12
  81.4 1.9 %collective-permute-start.17 = (bf16[2,256,128]{2,1,0:T(8,128)(2,1)S(1)}, bf16[2,256,128]{2,1,0:T(8,128)(2,1)S(1)}, u32[]{:S(2)}, u32[]{:S(2)}) collective-permute-start(bf16[2,256,128]{2,1,0:T(8,128)(2,1)S(1)} %add_convert_fusion), channel_id=1, source_target_pairs={{0,0},{160,8},{224,16},{192,24},{32,32},{128,40},{64,48},{96,56},{... | collective-permute-start | bytes 393224 | tf_op jit(solution)/shard_map/ppermute | solution.py:405
  83.3 10.4 %collective-permute-done.17 = bf16[2,256,128]{2,1,0:T(8,128)(2,1)S(1)} collective-permute-done((bf16[2,256,128]{2,1,0:T(8,128)(2,1)S(1)}, bf16[2,256,128]{2,1,0:T(8,128)(2,1)S(1)}, u32[]{:S(2)}, u32[]{:S(2)}) %collective-permute-start.17) | collective-permute-done | bytes 131104 | tf_op jit(solution)/shard_map/ppermute | solution.py:405
  93.7 0.7 fusion
  94.5 0.0 all-to-all-done.1
  94.5 1.0 %shard_map.122 = (bf16[192,640]{1,0:T(8,128)(2,1)}, bf16[192,640]{1,0:T(8,128)(2,1)}, bf16[192,128]{1,0:T(8,128)(2,1)}, bf16[192,128]{1,0:T(8,128)(2,1)}) custom-call(bf16[192,1536]{1,0:T(8,128)(2,1)S(1)} %bitcast.26), custom_call_target="tpu_custom_call" | custom-call | flops 294912 | bytes 1179648 | tf_op jit(solution)/shard_map/pallas_call | solution.py:87
  (14 shorter events, 0.1 us)
Async XLA Ops:
  0.6 8.9 %copy-start = (bf16[1,24,8,640]{3,2,1,0:T(8,128)(2,1)S(1)}, bf16[1,24,8,640]{3,2,1,0:T(8,128)(2,1)}, u32[]{:S(2)}) copy-start(bf16[1,24,8,640]{3,2,1,0:T(8,128)(2,1)} %param.7) | copy-start | bytes 737284
  1.6 11.7 %collective-permute-start = (bf16[2,256,128]{2,1,0:T(8,128)(2,1)S(1)}, bf16[2,256,128]{2,1,0:T(8,128)(2,1)S(1)}, u32[]{:S(2)}, u32[]{:S(2)}) collective-permute-start(bf16[2,256,128]{2,1,0:T(8,128)(2,1)S(1)} %pad_maximum_fusion), channel_id=1, source_target_pairs={{0,0},{8,160},{16,224},{24,192},{32,32},{40,128},{48,64},{56,96},{... | collective-permute-start | bytes 393224 | tf_op jit(solution)/shard_map/ppermute | solution.py:375
  9.5 0.9 copy-start.1
  10.5 0.8 copy-start.2
  11.3 0.8 copy-start.3
  13.3 9.9 %collective-permute-start.2 = (bf16[2,256,128]{2,1,0:T(8,128)(2,1)S(1)}, bf16[2,256,128]{2,1,0:T(8,128)(2,1)S(1)}, u32[]{:S(2)}, u32[]{:S(2)}) collective-permute-start(bf16[2,256,128]{2,1,0:T(8,128)(2,1)S(1)} %collective-permute-done.refs_0_), channel_id=1, source_target_pairs={{0,224},{8,232},{16,240},{24,248},{32,0},{40,8},{48,16},{56,24},{6... | collective-permute-start | bytes 393224 | tf_op jit(solution)/shard_map/ppermute | solution.py:373
  15.9 18.8 %all-to-all-start = ((bf16[8,24,1536]{2,1,0:T(8,128)(2,1)}), bf16[8,24,1536]{2,1,0:T(8,128)(2,1)S(1)}, u32[]{:S(2)}, u32[]{:S(2)}) async-start(bf16[8,24,1536]{2,1,0:T(8,128)(2,1)} %bitcast.6), calls=%async_computation | async-start | bytes 1179648 | tf_op jit(solution)/shard_map/all_to_all | solution.py:378
  23.2 6.2 %collective-permute-start.1 = (bf16[2,256,128]{2,1,0:T(8,128)(2,1)S(1)}, bf16[2,256,128]{2,1,0:T(8,128)(2,1)S(1)}, u32[]{:S(2)}, u32[]{:S(2)}) collective-permute-start(bf16[2,256,128]{2,1,0:T(8,128)(2,1)S(1)} %collective-permute-done.refs_0_), channel_id=1, source_target_pairs={{0,32},{8,40},{16,48},{24,56},{32,64},{40,72},{48,80},{56,88},{64,... | collective-permute-start | bytes 393224 | tf_op jit(solution)/shard_map/ppermute | solution.py:373
  23.2 8.9 %collective-permute-start.3 = (bf16[256,128]{1,0:T(8,128)(2,1)S(1)}, bf16[256,128]{1,0:T(8,128)(2,1)S(1)}, u32[]{:S(2)}, u32[]{:S(2)}) collective-permute-start(bf16[256,128]{1,0:T(8,128)(2,1)S(1)} %slice_bitcast_fusion.1), channel_id=1, source_target_pairs={{0,160},{8,168},{16,176},{24,184},{32,192},{40,200},{48,208},{56,2... | collective-permute-start | bytes 196616 | tf_op jit(solution)/shard_map/ppermute | solution.py:373
  24.8 18.6 %collective-permute-start.8 = (bf16[2,256,128]{2,1,0:T(8,128)(2,1)S(1)}, bf16[2,256,128]{2,1,0:T(8,128)(2,1)S(1)}, u32[]{:S(2)}, u32[]{:S(2)}) collective-permute-start(bf16[2,256,128]{2,1,0:T(8,128)(2,1)S(1)} %collective-permute-done.2.refs_2_), channel_id=1, source_target_pairs={{0,224},{8,232},{16,240},{24,248},{32,0},{40,8},{48,16},{56,24},{6... | collective-permute-start | bytes 393224 | tf_op jit(solution)/shard_map/ppermute | solution.py:373
  26.6 16.8 %collective-permute-start.6 = (bf16[2,256,128]{2,1,0:T(8,128)(2,1)S(1)}, bf16[2,256,128]{2,1,0:T(8,128)(2,1)S(1)}, u32[]{:S(2)}, u32[]{:S(2)}) collective-permute-start(bf16[2,256,128]{2,1,0:T(8,128)(2,1)S(1)} %collective-permute-done.2.refs_2_), channel_id=1, source_target_pairs={{0,192},{8,200},{16,208},{24,216},{32,224},{40,232},{48,240},{56,2... | collective-permute-start | bytes 393224 | tf_op jit(solution)/shard_map/ppermute | solution.py:373
  29.3 14.1 %collective-permute-start.7 = (bf16[2,256,128]{2,1,0:T(8,128)(2,1)S(1)}, bf16[2,256,128]{2,1,0:T(8,128)(2,1)S(1)}, u32[]{:S(2)}, u32[]{:S(2)}) collective-permute-start(bf16[2,256,128]{2,1,0:T(8,128)(2,1)S(1)} %collective-permute-done.1.refs_1_), channel_id=1, source_target_pairs={{0,32},{8,40},{16,48},{24,56},{32,64},{40,72},{48,80},{56,88},{64,... | collective-permute-start | bytes 393224 | tf_op jit(solution)/shard_map/ppermute | solution.py:373
  30.0 13.4 %collective-permute-start.5 = (bf16[2,256,128]{2,1,0:T(8,128)(2,1)S(1)}, bf16[2,256,128]{2,1,0:T(8,128)(2,1)S(1)}, u32[]{:S(2)}, u32[]{:S(2)}) collective-permute-start(bf16[2,256,128]{2,1,0:T(8,128)(2,1)S(1)} %collective-permute-done.1.refs_1_), channel_id=1, source_target_pairs={{0,64},{8,72},{16,80},{24,88},{32,96},{40,104},{48,112},{56,120},{... | collective-permute-start | bytes 393224 | tf_op jit(solution)/shard_map/ppermute | solution.py:373
  30.9 3.8 %copy-start.4 = (s32[32]{0:T(128)S(1)}, s32[32]{0:T(128)}, u32[]{:S(2)}) copy-start(s32[32]{0:T(128)} %len_ref.5) | copy-start | bytes 388
  32.1 11.3 %collective-permute-start.4 = (bf16[256,128]{1,0:T(8,128)(2,1)S(1)}, bf16[256,128]{1,0:T(8,128)(2,1)S(1)}, u32[]{:S(2)}, u32[]{:S(2)}) collective-permute-start(bf16[256,128]{1,0:T(8,128)(2,1)S(1)} %slice_bitcast_fusion), channel_id=1, source_target_pairs={{0,96},{8,104},{16,112},{24,120},{32,128},{40,136},{48,144},{56,15... | collective-permute-start | bytes 196616 | tf_op jit(solution)/shard_map/ppermute | solution.py:373
  49.0 16.6 %collective-permute-start.11 = (bf16[256,128]{1,0:T(8,128)(2,1)S(1)}, bf16[256,128]{1,0:T(8,128)(2,1)S(1)}, u32[]{:S(2)}, u32[]{:S(2)}) collective-permute-start(bf16[256,128]{1,0:T(8,128)(2,1)S(1)} %get-tuple-element.39), channel_id=1, source_target_pairs={{0,160},{8,168},{16,176},{24,184},{32,192},{40,200},{48,208},{56,2... | collective-permute-start | bytes 196616 | tf_op jit(solution)/shard_map/ppermute | solution.py:373
  51.4 16.9 %collective-permute-start.15 = (bf16[256,128]{1,0:T(8,128)(2,1)S(1)}, bf16[256,128]{1,0:T(8,128)(2,1)S(1)}, u32[]{:S(2)}, u32[]{:S(2)}) collective-permute-start(bf16[256,128]{1,0:T(8,128)(2,1)S(1)} %get-tuple-element.43), channel_id=1, source_target_pairs={{0,96},{8,104},{16,112},{24,120},{32,128},{40,136},{48,144},{56,15... | collective-permute-start | bytes 196616 | tf_op jit(solution)/shard_map/ppermute | solution.py:373
  52.9 12.7 %collective-permute-start.9 = (bf16[2,256,128]{2,1,0:T(8,128)(2,1)S(1)}, bf16[2,256,128]{2,1,0:T(8,128)(2,1)S(1)}, u32[]{:S(2)}, u32[]{:S(2)}) collective-permute-start(bf16[2,256,128]{2,1,0:T(8,128)(2,1)S(1)} %get-tuple-element.37), channel_id=1, source_target_pairs={{0,224},{8,232},{16,240},{24,248},{32,0},{40,8},{48,16},{56,24},{6... | collective-permute-start | bytes 393224 | tf_op jit(solution)/shard_map/ppermute | solution.py:373
  54.6 10.9 %collective-permute-start.10 = (bf16[2,256,128]{2,1,0:T(8,128)(2,1)S(1)}, bf16[2,256,128]{2,1,0:T(8,128)(2,1)S(1)}, u32[]{:S(2)}, u32[]{:S(2)}) collective-permute-start(bf16[2,256,128]{2,1,0:T(8,128)(2,1)S(1)} %get-tuple-element.38), channel_id=1, source_target_pairs={{0,192},{8,200},{16,208},{24,216},{32,224},{40,232},{48,240},{56,2... | collective-permute-start | bytes 393224 | tf_op jit(solution)/shard_map/ppermute | solution.py:373
  57.8 10.6 %collective-permute-start.13 = (bf16[2,256,128]{2,1,0:T(8,128)(2,1)S(1)}, bf16[2,256,128]{2,1,0:T(8,128)(2,1)S(1)}, u32[]{:S(2)}, u32[]{:S(2)}) collective-permute-start(bf16[2,256,128]{2,1,0:T(8,128)(2,1)S(1)} %get-tuple-element.41), channel_id=1, source_target_pairs={{0,32},{8,40},{16,48},{24,56},{32,64},{40,72},{48,80},{56,88},{64,... | collective-permute-start | bytes 393224 | tf_op jit(solution)/shard_map/ppermute | solution.py:373
  65.5 8.4 %collective-permute-start.14 = (bf16[2,256,128]{2,1,0:T(8,128)(2,1)S(1)}, bf16[2,256,128]{2,1,0:T(8,128)(2,1)S(1)}, u32[]{:S(2)}, u32[]{:S(2)}) collective-permute-start(bf16[2,256,128]{2,1,0:T(8,128)(2,1)S(1)} %get-tuple-element.42), channel_id=1, source_target_pairs={{0,64},{8,72},{16,80},{24,88},{32,96},{40,104},{48,112},{56,120},{... | collective-permute-start | bytes 393224 | tf_op jit(solution)/shard_map/ppermute | solution.py:373
  65.6 15.7 %collective-permute-start.12 = (bf16[2,256,128]{2,1,0:T(8,128)(2,1)S(1)}, bf16[2,256,128]{2,1,0:T(8,128)(2,1)S(1)}, u32[]{:S(2)}, u32[]{:S(2)}) collective-permute-start(bf16[2,256,128]{2,1,0:T(8,128)(2,1)S(1)} %add_convert_fusion.2), channel_id=1, source_target_pairs={{0,224},{8,232},{16,240},{24,248},{32,0},{40,8},{48,16},{56,24},{6... | collective-permute-start | bytes 393224 | tf_op jit(solution)/shard_map/ppermute | solution.py:373
  74.0 7.3 %collective-permute-start.16 = (bf16[2,256,128]{2,1,0:T(8,128)(2,1)S(1)}, bf16[2,256,128]{2,1,0:T(8,128)(2,1)S(1)}, u32[]{:S(2)}, u32[]{:S(2)}) collective-permute-start(bf16[2,256,128]{2,1,0:T(8,128)(2,1)S(1)} %add_convert_fusion.1), channel_id=1, source_target_pairs={{0,32},{8,40},{16,48},{24,56},{32,64},{40,72},{48,80},{56,88},{64,... | collective-permute-start | bytes 393224 | tf_op jit(solution)/shard_map/ppermute | solution.py:373
  74.1 20.3 %all-to-all-start.1 = ((bf16[8,24,1536]{2,1,0:T(8,128)(2,1)}), bf16[8,24,1536]{2,1,0:T(8,128)(2,1)S(1)}, u32[]{:S(2)}, u32[]{:S(2)}) async-start(bf16[8,24,1536]{2,1,0:T(8,128)(2,1)} %bitcast.10), calls=%async_computation.1 | async-start | bytes 1179648 | tf_op jit(solution)/shard_map/all_to_all | solution.py:400
  81.4 12.3 %collective-permute-start.17 = (bf16[2,256,128]{2,1,0:T(8,128)(2,1)S(1)}, bf16[2,256,128]{2,1,0:T(8,128)(2,1)S(1)}, u32[]{:S(2)}, u32[]{:S(2)}) collective-permute-start(bf16[2,256,128]{2,1,0:T(8,128)(2,1)S(1)} %add_convert_fusion), channel_id=1, source_target_pairs={{0,0},{160,8},{224,16},{192,24},{32,32},{128,40},{64,48},{96,56},{... | collective-permute-start | bytes 393224 | tf_op jit(solution)/shard_map/ppermute | solution.py:405

commit v2 on v1

--- a/solution.py
+++ b/solution.py
@@ -48,9 +48,9 @@
         functools.partial(pack_kernel, heads),
         out_shape=jax.ShapeDtypeStruct((rows, total), bf16),
         scratch_shapes=[VMEM((total // head_dim, rows, head_dim), f32)],
-        compiler_params=pltpu.CompilerParams(vmem_limit_bytes=LIMIT),
+        compiler_params=pltpu.CompilerParams(vmem_limit_bytes=7 * LIMIT),
         cost_estimate=pl.CostEstimate(
-            flops=rows * total, bytes_accessed=4 * rows * total, transcendentals=0
+            flops=int(2e9), bytes_accessed=4 * rows * total, transcendentals=0
         ),
     )(
         q.reshape(rows, width),
@@ -95,7 +95,7 @@
         scratch_shapes=[VMEM((total // head_dim, rows, head_dim), f32)],
         compiler_params=pltpu.CompilerParams(vmem_limit_bytes=LIMIT),
         cost_estimate=pl.CostEstimate(
-            flops=rows * total, bytes_accessed=4 * rows * total, transcendentals=0
+            flops=int(1e9), bytes_accessed=4 * rows * total, transcendentals=0
         ),
     )(x)
     return [piece.reshape(1, slots, heads, piece.shape[1]) for piece in outs]
@@ -142,47 +142,41 @@
     return x.astype(f32).T.astype(bf16)
 
 
-def near_stats_kernel(group, chunks, scale, len_ref, x_ref, *refs):
-    kv_refs, stats_ref, q_s, g_s = refs[:chunks], refs[chunks], refs[chunks + 1], refs[chunks + 2]
-    cap, head_dim = x_ref.shape[0], q_s.shape[1]
+def turn_kernel(far_k, far_v, low_ref, high_ref, keys_t, values_t):
+    span = far_k.shape[0]
+    k_refs = [far_k] + [r.at[i, 0] for r in (low_ref, high_ref) for i in range(2)]
+    v_refs = [far_v] + [r.at[i, 1] for r in (low_ref, high_ref) for i in range(2)]
+    for i in range(len(k_refs)):
+        keys_t[:, i * span:(i + 1) * span] = transposed(k_refs[i][...])
+        values_t[:, i * span:(i + 1) * span] = transposed(v_refs[i][...])
+
+
+def far_kernel(group, near, scale, len_ref, x_ref, *refs):
+    near_refs, refs = refs[:near], refs[near:]
+    (far_k, far_v, low_ref, high_ref, keys_t, values_t,
+     far_dk, far_dv, low_grad, high_grad, total_ref, ot_ref, qt_ref,
+     q_s, g_s, e_s, d_s, pb_s, sb_s, dk_s, dv_s) = refs
+    k_refs = [far_k] + [r.at[i, 0] for r in (low_ref, high_ref) for i in range(2)]
+    v_refs = [far_v] + [r.at[i, 1] for r in (low_ref, high_ref) for i in range(2)]
+    dk_refs = [far_dk] + [r.at[i, 0] for r in (low_grad, high_grad) for i in range(2)]
+    dv_refs = [far_dv] + [r.at[i, 1] for r in (low_grad, high_grad) for i in range(2)]
+    chunks = len(k_refs)
+    cap = x_ref.shape[0]
+    span, head_dim = far_k.shape
     width = group * head_dim
     length = len_ref[lax.axis_index("seq")]
     turn = scale * math.log2(math.e)
     stack_rows(x_ref, q_s, g_s, group)
     for start, stop, token in blocks_of(group * cap, cap):
+        size = stop - start
         q, g = q_s[start:stop, :], g_s[start:stop, :]
         state = None
-        for kv in kv_refs:
+        for kv in near_refs:
             _, state = merge(state, dot_t(kv[0], q), dot_t(kv[1], g), turn)
         own_k = x_ref[:, 2 * width:2 * width + head_dim]
         own_v = x_ref[:, 2 * width + head_dim:]
         seen = causal(token, length, cap)
         _, state = merge(state, dot_t(own_k, q), dot_t(own_v, g), turn, seen)
-        for i in range(3):
-            stats_ref[i:i + 1, start:stop] = state[i]
-
-
-def far_kernel(group, chunks, scale, len_ref, x_ref, stats_ref, *refs):
-    count = chunks + 1
-    shard_refs, grad_refs = refs[:count], refs[count:2 * count]
-    k_refs = [shard_refs[0]] + [r.at[0] for r in shard_refs[2:]]
-    v_refs = [shard_refs[1]] + [r.at[1] for r in shard_refs[2:]]
-    dk_refs = [grad_refs[0]] + [r.at[0] for r in grad_refs[2:]]
-    dv_refs = [grad_refs[1]] + [r.at[1] for r in grad_refs[2:]]
-    (total_ref, ot_ref, qt_ref,
-     q_s, g_s, keys_t, values_t, e_s, d_s, pb_s, sb_s, dk_s, dv_s) = refs[2 * count:]
-    cap = x_ref.shape[0]
-    span, head_dim = shard_refs[0].shape
-    length = len_ref[lax.axis_index("seq")]
-    turn = scale * math.log2(math.e)
-    stack_rows(x_ref, q_s, g_s, group)
-    for i in range(chunks):
-        keys_t[:, i * span:(i + 1) * span] = transposed(k_refs[i][...])
-        values_t[:, i * span:(i + 1) * span] = transposed(v_refs[i][...])
-    for start, stop, token in blocks_of(group * cap, cap):
-        size = stop - start
-        q, g = q_s[start:stop, :], g_s[start:stop, :]
-        state = tuple(stats_ref[i:i + 1, start:stop] for i in range(3))
         tops = []
         for i in range(chunks):
             d = dot_t(v_refs[i][...], g)
@@ -278,58 +272,50 @@
         )
 
 
-def call(body, products, keys, rows, head_dim, ins, outs, scratch, limit):
+def call(body, micros, ins, outs, scratch, limit, scalars=1):
     smem = pl.BlockSpec(memory_space=pltpu.SMEM)
     vmem = pl.BlockSpec(memory_space=pltpu.VMEM)
     return pl.pallas_call(
         body,
         out_shape=outs,
-        in_specs=[smem] + [vmem] * (len(ins) - 1),
+        in_specs=[smem] * scalars + [vmem] * (len(ins) - scalars),
         out_specs=[vmem] * len(outs),
         scratch_shapes=scratch,
         compiler_params=pltpu.CompilerParams(vmem_limit_bytes=limit * 1024 * 1024),
         cost_estimate=pl.CostEstimate(
-            flops=2 * products * rows * keys * head_dim,
+            flops=int(micros * 1.15e9),
             bytes_accessed=sum(x.size * x.dtype.itemsize for x in ins + outs),
-            transcendentals=rows * keys,
+            transcendentals=0,
         ),
     )(*ins)
 
 
-def near_stats(lengths, x, shards, group, scale):
+def turned(far):
+    span, head_dim = far[0].shape
+    return call(
+        turn_kernel, 6, list(far), [jax.ShapeDtypeStruct((head_dim, 5 * span), bf16)] * 2,
+        [], 8, scalars=0,
+    )
+
+
+def far_pass(lengths, x, near, far, far_t, group, scale):
     cap = x.shape[0]
-    _, span, head_dim = shards[0].shape
-    rows, keys = group * cap, len(shards) * span + cap
-    return call(
-        functools.partial(near_stats_kernel, group, len(shards), scale),
-        2, keys, rows, head_dim,
-        [lengths, x, *shards],
-        [jax.ShapeDtypeStruct((3, rows), f32)],
-        [VMEM((rows, head_dim), bf16)] * 2,
-        12,
-    )[0]
-
-
-def far_pass(lengths, x, stats, shards, group, scale):
-    cap = x.shape[0]
-    span, head_dim = shards[0].shape
-    chunks = len(shards) - 1
-    rows, keys = group * cap, chunks * span
+    span, head_dim = far[0].shape
+    rows, keys = group * cap, 5 * span
     outs = call(
-        functools.partial(far_kernel, group, chunks, scale),
-        6, keys, rows, head_dim,
-        [lengths, x, stats, *shards],
-        [jax.ShapeDtypeStruct(shard.shape, bf16) for shard in shards]
+        functools.partial(far_kernel, group, len(near), scale),
+        7,
+        [lengths, x, *near, *far, *far_t],
+        [jax.ShapeDtypeStruct(shard.shape, bf16) for shard in far]
         + [jax.ShapeDtypeStruct((2, rows), f32)]
         + [jax.ShapeDtypeStruct((head_dim, rows), f32)] * 2,
         [VMEM((rows, head_dim), bf16)] * 2
-        + [VMEM((head_dim, keys), bf16)] * 2
         + [VMEM((keys, 256), f32)] * 2
         + [VMEM((keys, 256), bf16)] * 2
         + [VMEM((keys, head_dim), f32)] * 2,
         24,
     )
-    return outs[:chunks + 1], outs[chunks + 1:]
+    return outs[:len(far)], outs[len(far):]
 
 
 def near_pass(lengths, x, totals, shards, group, scale):
@@ -338,7 +324,7 @@
     rows, keys = group * cap, len(shards) * span + cap
     outs = call(
         functools.partial(near_kernel, group, len(shards), scale),
-        6, keys, rows, head_dim,
+        6,
         [lengths, x, *totals, *shards],
         [jax.ShapeDtypeStruct((cap, packed), bf16)]
         + [jax.ShapeDtypeStruct((2, span, head_dim), f32)] * len(shards),
@@ -375,32 +361,28 @@
     own = lax.ppermute(jnp.stack([prefix_k[:, 0], prefix_v[:, 0]]), "seq", to_prompt)
     packed = pack(comp_q, comp_grad, comp_k, comp_v)
     own, packed = lax.optimization_barrier((own, packed))
+
+    up, down = shift(own, 1), shift(own, -1)
+    up, down, packed = lax.optimization_barrier((up, down, packed))
+    far_keys, far_values = shift(down[0], -3), shift(up[1], 3)
+    low = shift(jnp.stack([own, up]), 2)
+    high = shift(jnp.stack([own, down]), -2)
     x = lax.all_to_all(packed, "head", split_axis=0, concat_axis=0, tiled=True)
 
-    up, down = shift(own, 1), shift(own, -1)
-    far_keys = shift(down[0], -3)
-    far_values = shift(up[1], 3)
-    up3, down3 = shift(up, 2), shift(down, -2)
-    up2, down2 = shift(up, 1), shift(down, -1)
-
-    near = [own, up, down]
-    stats = near_stats(comp_len, x, near, group, scale)
-    grads, totals = far_pass(
-        comp_len, x, stats, [far_keys, far_values, up3, down3, up2, down2], group, scale
-    )
-    moved = [
-        shift(grad, steps).astype(f32) for grad, steps in zip(grads, (3, -3, -2, 2, -1, 1))
+    near, far = [own, up, down], [far_keys, far_values, low, high]
+    grads, totals = far_pass(comp_len, x, near, far, turned(far), group, scale)
+    far_dk, far_dv, low, high = [
+        shift(grad, steps) for grad, steps in zip(grads, (3, -3, -2, 2))
     ]
     out, (own_grad, up_grad, down_grad) = near_pass(comp_len, x, totals, near, group, scale)
-    far_dk, far_dv, up3, down3, up2, down2 = moved
-    up_sum = up_grad + up2 + up3
-    down_sum = down_grad + down2 + down3
-    up_sum = up_sum + jnp.pad(far_dv[None], ((1, 0), (0, 0), (0, 0)))
-    down_sum = down_sum + jnp.pad(far_dk[None], ((0, 1), (0, 0), (0, 0)))
+    far_dk, far_dv = far_dk.astype(f32)[None], far_dv.astype(f32)[None]
+    up_sum = up_grad + low[1].astype(f32) + jnp.pad(far_dv, ((1, 0), (0, 0), (0, 0)))
+    down_sum = down_grad + high[1].astype(f32) + jnp.pad(far_dk, ((0, 1), (0, 0), (0, 0)))
     back = lax.all_to_all(out, "head", split_axis=0, concat_axis=0, tiled=True)
     up_sum = shift(up_sum.astype(bf16), -1)
     down_sum = shift(down_sum.astype(bf16), 1)
-    summed = own_grad + up_sum.astype(f32) + down_sum.astype(f32)
+    summed = own_grad + low[0].astype(f32) + high[0].astype(f32)
+    summed = summed + up_sum.astype(f32) + down_sum.astype(f32)
     attn_out, grad_q, grad_k, grad_v = unpack(back, heads, width, head_dim)
     placed = lax.ppermute(summed.astype(bf16), "seq", to_owner).astype(f32)
     return (attn_out, grad_q, grad_k, grad_v, placed[0][:, None], placed[1][:, None])

time: 95.9 us -> 96.9 us (1.010)
  waiting for transfers between devices: 24.9 us -> 31.8 us
  starting transfers between devices: 49.6 us -> 44.8 us
  local copies, waits for them, and re-layouts: 3.27 us -> 1.38 us
    ppermute x16 -> x12, waiting for transfers between devices: 14.4 us -> 19 us  [shift(): return lax.ppermute(x, 'seq', pairs)]
    ppermute x16 -> x12, starting transfers between devices: 25.2 us -> 21.3 us  [shift(): return lax.ppermute(x, 'seq', pairs)]
    all_to_all x1, waiting for transfers between devices: 0.01 us -> 3.69 us  [on_device(): x = lax.all_to_all(packed, 'head', split_axis=0, concat_axis=0, tiled=True)]
    ppermute x1, waiting for transfers between devices: 10.4 us -> 7.57 us  [on_device(): placed = lax.ppermute(summed.astype(bf16), 'seq', to_owner).astype(f32)]
    unnamed x10 -> x2, local copies, waits for them, and re-layouts: 2.54 us -> 0.66 us
    ppermute x1, waiting for transfers between devices: 0.06 us -> 1.54 us  [on_device(): lax.ppermute(jnp.stack([prefix_k[:, 0], prefix_v[:, 0]]), 'seq', to_prompt)]
    pallas_call x1, Pallas kernels: 1.12 us -> 2.19 us  [pack(): pl.pallas_call(functools.partial(pack_kernel, heads), out_shape=jax.Shape...]
  transfers between devices with their start and end apart: 20 -> 16, of which waited for: 6 -> 9; matrix products, arithmetic and copies ran while one was open for 1% -> 0% of each run, Pallas kernels for 10% -> 10%
where the time goes in v2:
time: 96.9 us; the launch traced here: 96.6 us
  starting transfers between devices  44.8 us (46%)
  waiting for transfers between devices  31.8 us (33%)
  Pallas kernels  16.7 us (17%)
  local copies, waits for them, and re-layouts  1.38 us (1%)
  other arithmetic  1.09 us (1%)
    ppermute x12, starting transfers between devices, shift(): return lax.ppermute(x, 'seq', pairs)  21.3 us
    ppermute x12, waiting for transfers between devices, shift(): return lax.ppermute(x, 'seq', pairs)  19 us
    pallas_call x3, Pallas kernels, call(): pl.pallas_call(body, out_shape=outs, in_specs=[smem] * scalars + [vmem] *...  13.6 us
    ppermute x1, starting transfers between devices, on_device(): lax.ppermute(jnp.stack([prefix_k[:, 0], prefix_v[:, 0]]), 'seq', to_prompt)  7.94 us
    ppermute x1, waiting for transfers between devices, on_device(): placed = lax.ppermute(summed.astype(bf16), 'seq', to_owner).astype(f32)  7.57 us
    all_to_all x1, starting transfers between devices, on_device(): x = lax.all_to_all(packed, 'head', split_axis=0, concat_axis=0, tiled=True)  7.26 us
    all_to_all x1, starting transfers between devices, on_device(): back = lax.all_to_all(out, 'head', split_axis=0, concat_axis=0, tiled=True)  6.43 us
    all_to_all x1, waiting for transfers between devices, on_device(): x = lax.all_to_all(packed, 'head', split_axis=0, concat_axis=0, tiled=True)  3.69 us
  transfers between devices with their start and end apart: 16, of which 9 were waited for; matrix products, arithmetic and copies ran while one was open for 0% of the time, Pallas kernels for 10%

profile of v2, /device:TPU:24, one launch (start us, length us, event | category | flops | bytes accessed | tf_op | source)
XLA Modules:
  0.0 96.6 jit_solution(1305340014220291472)
XLA Ops:
  0.6 0.9 pad_maximum_fusion.2
  1.5 7.9 %collective-permute-start = (bf16[2,256,128]{2,1,0:T(8,128)(2,1)S(1)}, bf16[2,256,128]{2,1,0:T(8,128)(2,1)S(1)}, u32[]{:S(2)}, u32[]{:S(2)}) collective-permute-start(bf16[2,256,128]{2,1,0:T(8,128)(2,1)S(1)} %pad_maximum_fusion.2), channel_id=1, source_target_pairs={{0,0},{8,160},{16,224},{24,192},{32,32},{40,128},{48,64},{56,96},{... | collective-permute-start | bytes 393224 | tf_op jit(solution)/shard_map/ppermute | solution.py:361
  9.5 2.2 %shard_map.118 = bf16[192,1536]{1,0:T(8,128)(2,1)} custom-call(bf16[192,640]{1,0:T(8,128)(2,1)} %bitcast.61, bf16[192,640]{1,0:T(8,128)(2,1)} %bitcast.62, bf16[192,128]{1,0:T(8,128)(2,1)} %bitcast.63, bf16[192,128]{1,0:T(8,128)(2,1)} %bitcast.64), custom_call_target="tpu_custom_call" | custom-call | flops 2000000000 | bytes 1179648 | tf_op jit(solution)/shard_map/pallas_call | solution.py:47
  11.7 1.5 %collective-permute-done.refs_0_ = bf16[2,256,128]{2,1,0:T(8,128)(2,1)S(1)} collective-permute-done((bf16[2,256,128]{2,1,0:T(8,128)(2,1)S(1)}, bf16[2,256,128]{2,1,0:T(8,128)(2,1)S(1)}, u32[]{:S(2)}, u32[]{:S(2)}) %collective-permute-start) | collective-permute-done | bytes 131104 | tf_op jit(solution)/shard_map/ppermute | solution.py:361
  13.2 2.6 %collective-permute-start.2 = (bf16[2,256,128]{2,1,0:T(8,128)(2,1)S(1)}, bf16[2,256,128]{2,1,0:T(8,128)(2,1)S(1)}, u32[]{:S(2)}, u32[]{:S(2)}) collective-permute-start(bf16[2,256,128]{2,1,0:T(8,128)(2,1)S(1)} %collective-permute-done.refs_0_), channel_id=1, source_target_pairs={{0,224},{8,232},{16,240},{24,248},{32,0},{40,8},{48,16},{56,24},{6... | collective-permute-start | bytes 393224 | tf_op jit(solution)/shard_map/ppermute | solution.py:359
  15.8 0.0 collective-permute-start.1
  15.9 2.7 %collective-permute-done.2.refs_2_ = bf16[2,256,128]{2,1,0:T(8,128)(2,1)S(1)} collective-permute-done((bf16[2,256,128]{2,1,0:T(8,128)(2,1)S(1)}, bf16[2,256,128]{2,1,0:T(8,128)(2,1)S(1)}, u32[]{:S(2)}, u32[]{:S(2)}) %collective-permute-start.2) | collective-permute-done | bytes 131104 | tf_op jit(solution)/shard_map/ppermute | solution.py:359
  18.6 3.4 %collective-permute-done.1.refs_1_ = bf16[2,256,128]{2,1,0:T(8,128)(2,1)S(1)} collective-permute-done((bf16[2,256,128]{2,1,0:T(8,128)(2,1)S(1)}, bf16[2,256,128]{2,1,0:T(8,128)(2,1)S(1)}, u32[]{:S(2)}, u32[]{:S(2)}) %collective-permute-start.1) | collective-permute-done | bytes 131104 | tf_op jit(solution)/shard_map/ppermute | solution.py:359
  22.1 0.1 collective-permute-start.6
  22.2 2.9 %collective-permute-start.5 = (bf16[2,2,256,128]{3,2,1,0:T(8,128)(2,1)S(1)}, bf16[2,2,256,128]{3,2,1,0:T(8,128)(2,1)S(1)}, u32[]{:S(2)}, u32[]{:S(2)}) collective-permute-start(bf16[2,2,256,128]{3,2,1,0:T(8,128)(2,1)S(1)} %get-tuple-element.59), channel_id=1, source_target_pairs={{0,64},{8,72},{16,80},{24,88},{32,96},{40,104},{48,112},{56,120},{... | collective-permute-start | bytes 786440 | tf_op jit(solution)/shard_map/ppermute | solution.py:359
  25.1 0.2 collective-permute-start.3
  25.3 3.6 %collective-permute-start.4 = (bf16[256,128]{1,0:T(8,128)(2,1)S(1)}, bf16[256,128]{1,0:T(8,128)(2,1)S(1)}, u32[]{:S(2)}, u32[]{:S(2)}) collective-permute-start(bf16[256,128]{1,0:T(8,128)(2,1)S(1)} %slice_bitcast_fusion.4), channel_id=1, source_target_pairs={{0,96},{8,104},{16,112},{24,120},{32,128},{40,136},{48,144},{56,15... | collective-permute-start | bytes 196616 | tf_op jit(solution)/shard_map/ppermute | solution.py:359
  28.9 7.3 %all-to-all-start = ((bf16[8,24,1536]{2,1,0:T(8,128)(2,1)}), bf16[8,24,1536]{2,1,0:T(8,128)(2,1)S(1)}, u32[]{:S(2)}, u32[]{:S(2)}) async-start(bf16[8,24,1536]{2,1,0:T(8,128)(2,1)} %bitcast.6), calls=%async_computation | async-start | bytes 1179648 | tf_op jit(solution)/shard_map/all_to_all | solution.py:370
  36.2 0.6 collective-permute-done.3.far_k.refs_3_
  36.8 3.0 %collective-permute-done.4.far_v.refs_4_ = bf16[256,128]{1,0:T(8,128)(2,1)S(1)} collective-permute-done((bf16[256,128]{1,0:T(8,128)(2,1)S(1)}, bf16[256,128]{1,0:T(8,128)(2,1)S(1)}, u32[]{:S(2)}, u32[]{:S(2)}) %collective-permute-start.4) | collective-permute-done | bytes 65568 | tf_op jit(solution)/shard_map/ppermute | solution.py:359
  39.8 0.0 collective-permute-done.6.high_ref.refs_6_
  39.8 0.0 collective-permute-done.5.low_ref.refs_5_
  39.8 0.2 shard_map.119
  40.1 3.7 %all-to-all-done = bf16[8,24,1536]{2,1,0:T(8,128)(2,1)S(1)} async-done(((bf16[8,24,1536]{2,1,0:T(8,128)(2,1)}), bf16[8,24,1536]{2,1,0:T(8,128)(2,1)S(1)}, u32[]{:S(2)}, u32[]{:S(2)}) %all-to-all-start) | async-done | bytes 589856 | tf_op jit(solution)/shard_map/all_to_all | solution.py:370
  43.8 0.0 copy-start
  43.8 0.7 copy-done
  44.4 7.6 %shard_map.120 = (bf16[256,128]{1,0:T(8,128)(2,1)S(1)}, bf16[256,128]{1,0:T(8,128)(2,1)S(1)}, bf16[2,2,256,128]{3,2,1,0:T(8,128)(2,1)S(1)}, bf16[2,2,256,128]{3,...) custom-call(s32[32]{0:T(128)S(1)} %copy-done, ...), custom_call_target="tpu_custom_call" | custom-call | flops 8049999872 | bytes 3939968 | tf_op jit(solution)/shard_map/pallas_call | solution.py:278
  52.0 2.5 %collective-permute-start.9 = (bf16[256,128]{1,0:T(8,128)(2,1)S(1)}, bf16[256,128]{1,0:T(8,128)(2,1)S(1)}, u32[]{:S(2)}, u32[]{:S(2)}) collective-permute-start(bf16[256,128]{1,0:T(8,128)(2,1)S(1)} %get-tuple-element.47), channel_id=1, source_target_pairs={{0,160},{8,168},{16,176},{24,184},{32,192},{40,200},{48,208},{56,2... | collective-permute-start | bytes 196616 | tf_op jit(solution)/shard_map/ppermute | solution.py:359
  54.4 3.8 %collective-permute-start.7 = (bf16[2,2,256,128]{3,2,1,0:T(8,128)(2,1)S(1)}, bf16[2,2,256,128]{3,2,1,0:T(8,128)(2,1)S(1)}, u32[]{:S(2)}, u32[]{:S(2)}) collective-permute-start(bf16[2,2,256,128]{3,2,1,0:T(8,128)(2,1)S(1)} %get-tuple-element.44), channel_id=1, source_target_pairs={{0,192},{8,200},{16,208},{24,216},{32,224},{40,232},{48,240},{56,2... | collective-permute-start | bytes 786440 | tf_op jit(solution)/shard_map/ppermute | solution.py:359
  58.2 0.0 collective-permute-start.8
  58.2 5.8 %shard_map.121 = (bf16[192,1536]{1,0:T(8,128)(2,1)}, f32[2,256,128]{2,1,0:T(8,128)S(1)}, f32[2,256,128]{2,1,0:T(8,128)S(1)}, f32[2,256,128]{2,1,0:T(8,128)S(1)}) custom-call(s32[32]{0:T(128)S(1)} %copy-done, bf16[192,1536]{1,0:T(8,128)(2,1)S(1)} %bitcast.51, f32[2,960]{1,0:T(2,128)S(1)} %get-tuple-element.35.total_ref, ...), custom_call_target="tpu_custom_call" | custom-call | flops 6899999744 | bytes 3350144 | tf_op jit(solution)/shard_map/pallas_call | solution.py:278
  64.0 6.4 %all-to-all-start.1 = ((bf16[8,24,1536]{2,1,0:T(8,128)(2,1)}), bf16[8,24,1536]{2,1,0:T(8,128)(2,1)S(1)}, u32[]{:S(2)}, u32[]{:S(2)}) async-start(bf16[8,24,1536]{2,1,0:T(8,128)(2,1)} %bitcast.13), calls=%async_computation.1 | async-start | bytes 1179648 | tf_op jit(solution)/shard_map/all_to_all | solution.py:381
  70.4 1.8 %collective-permute-start.11 = (bf16[256,128]{1,0:T(8,128)(2,1)S(1)}, bf16[256,128]{1,0:T(8,128)(2,1)S(1)}, u32[]{:S(2)}, u32[]{:S(2)}) collective-permute-start(bf16[256,128]{1,0:T(8,128)(2,1)S(1)} %get-tuple-element.49), channel_id=1, source_target_pairs={{0,96},{8,104},{16,112},{24,120},{32,128},{40,136},{48,144},{56,15... | collective-permute-start | bytes 196616 | tf_op jit(solution)/shard_map/ppermute | solution.py:359
  72.2 0.0 collective-permute-done.9
  72.2 0.0 collective-permute-done.7
  72.3 3.7 %collective-permute-start.10 = (bf16[2,256,128]{2,1,0:T(8,128)(2,1)S(1)}, bf16[2,256,128]{2,1,0:T(8,128)(2,1)S(1)}, u32[]{:S(2)}, u32[]{:S(2)}) collective-permute-start(bf16[2,256,128]{2,1,0:T(8,128)(2,1)S(1)} %fusion.3), channel_id=1, source_target_pairs={{0,224},{8,232},{16,240},{24,248},{32,0},{40,8},{48,16},{56,24},{6... | collective-permute-start | bytes 393224 | tf_op jit(solution)/shard_map/ppermute | solution.py:359
  76.0 3.0 %collective-permute-done.11 = bf16[256,128]{1,0:T(8,128)(2,1)S(1)} collective-permute-done((bf16[256,128]{1,0:T(8,128)(2,1)S(1)}, bf16[256,128]{1,0:T(8,128)(2,1)S(1)}, u32[]{:S(2)}, u32[]{:S(2)}) %collective-permute-start.11) | collective-permute-done | bytes 65568 | tf_op jit(solution)/shard_map/ppermute | solution.py:359
  79.0 0.0 collective-permute-done.8
  79.0 0.1 collective-permute-start.12
  79.1 0.0 collective-permute-done.10
  79.1 6.2 %collective-permute-done.12 = bf16[2,256,128]{2,1,0:T(8,128)(2,1)S(1)} collective-permute-done((bf16[2,256,128]{2,1,0:T(8,128)(2,1)S(1)}, bf16[2,256,128]{2,1,0:T(8,128)(2,1)S(1)}, u32[]{:S(2)}, u32[]{:S(2)}) %collective-permute-start.12) | collective-permute-done | bytes 131104 | tf_op jit(solution)/shard_map/ppermute | solution.py:359
  85.3 0.1 fusion.6
  85.3 1.9 %collective-permute-start.13 = (bf16[2,256,128]{2,1,0:T(8,128)(2,1)S(1)}, bf16[2,256,128]{2,1,0:T(8,128)(2,1)S(1)}, u32[]{:S(2)}, u32[]{:S(2)}) collective-permute-start(bf16[2,256,128]{2,1,0:T(8,128)(2,1)S(1)} %fusion.6), channel_id=1, source_target_pairs={{0,0},{160,8},{224,16},{192,24},{32,32},{128,40},{64,48},{96,56},{... | collective-permute-start | bytes 393224 | tf_op jit(solution)/shard_map/ppermute | solution.py:387
  87.3 0.0 all-to-all-done.1
  87.3 1.0 %shard_map.122 = (bf16[192,640]{1,0:T(8,128)(2,1)}, bf16[192,640]{1,0:T(8,128)(2,1)}, bf16[192,128]{1,0:T(8,128)(2,1)}, bf16[192,128]{1,0:T(8,128)(2,1)}) custom-call(bf16[192,1536]{1,0:T(8,128)(2,1)S(1)} %bitcast.49), custom_call_target="tpu_custom_call" | custom-call | flops 1000000000 | bytes 1179648 | tf_op jit(solution)/shard_map/pallas_call | solution.py:87
  88.3 7.6 %collective-permute-done.13 = bf16[2,256,128]{2,1,0:T(8,128)(2,1)S(1)} collective-permute-done((bf16[2,256,128]{2,1,0:T(8,128)(2,1)S(1)}, bf16[2,256,128]{2,1,0:T(8,128)(2,1)S(1)}, u32[]{:S(2)}, u32[]{:S(2)}) %collective-permute-start.13) | collective-permute-done | bytes 131104 | tf_op jit(solution)/shard_map/ppermute | solution.py:387
  95.8 0.7 fusion.7
  (5 shorter events, 0.1 us)
Async XLA Ops:
  1.5 11.7 %collective-permute-start = (bf16[2,256,128]{2,1,0:T(8,128)(2,1)S(1)}, bf16[2,256,128]{2,1,0:T(8,128)(2,1)S(1)}, u32[]{:S(2)}, u32[]{:S(2)}) collective-permute-start(bf16[2,256,128]{2,1,0:T(8,128)(2,1)S(1)} %pad_maximum_fusion.2), channel_id=1, source_target_pairs={{0,0},{8,160},{16,224},{24,192},{32,32},{40,128},{48,64},{56,96},{... | collective-permute-start | bytes 393224 | tf_op jit(solution)/shard_map/ppermute | solution.py:361
  13.2 5.4 %collective-permute-start.2 = (bf16[2,256,128]{2,1,0:T(8,128)(2,1)S(1)}, bf16[2,256,128]{2,1,0:T(8,128)(2,1)S(1)}, u32[]{:S(2)}, u32[]{:S(2)}) collective-permute-start(bf16[2,256,128]{2,1,0:T(8,128)(2,1)S(1)} %collective-permute-done.refs_0_), channel_id=1, source_target_pairs={{0,224},{8,232},{16,240},{24,248},{32,0},{40,8},{48,16},{56,24},{6... | collective-permute-start | bytes 393224 | tf_op jit(solution)/shard_map/ppermute | solution.py:359
  15.8 6.2 %collective-permute-start.1 = (bf16[2,256,128]{2,1,0:T(8,128)(2,1)S(1)}, bf16[2,256,128]{2,1,0:T(8,128)(2,1)S(1)}, u32[]{:S(2)}, u32[]{:S(2)}) collective-permute-start(bf16[2,256,128]{2,1,0:T(8,128)(2,1)S(1)} %collective-permute-done.refs_0_), channel_id=1, source_target_pairs={{0,32},{8,40},{16,48},{24,56},{32,64},{40,72},{48,80},{56,88},{64,... | collective-permute-start | bytes 393224 | tf_op jit(solution)/shard_map/ppermute | solution.py:359
  22.1 17.7 %collective-permute-start.6 = (bf16[2,2,256,128]{3,2,1,0:T(8,128)(2,1)S(1)}, bf16[2,2,256,128]{3,2,1,0:T(8,128)(2,1)S(1)}, u32[]{:S(2)}, u32[]{:S(2)}) collective-permute-start(bf16[2,2,256,128]{3,2,1,0:T(8,128)(2,1)S(1)} %get-tuple-element.58), channel_id=1, source_target_pairs={{0,192},{8,200},{16,208},{24,216},{32,224},{40,232},{48,240},{56,2... | collective-permute-start | bytes 786440 | tf_op jit(solution)/shard_map/ppermute | solution.py:359
  22.2 17.7 %collective-permute-start.5 = (bf16[2,2,256,128]{3,2,1,0:T(8,128)(2,1)S(1)}, bf16[2,2,256,128]{3,2,1,0:T(8,128)(2,1)S(1)}, u32[]{:S(2)}, u32[]{:S(2)}) collective-permute-start(bf16[2,2,256,128]{3,2,1,0:T(8,128)(2,1)S(1)} %get-tuple-element.59), channel_id=1, source_target_pairs={{0,64},{8,72},{16,80},{24,88},{32,96},{40,104},{48,112},{56,120},{... | collective-permute-start | bytes 786440 | tf_op jit(solution)/shard_map/ppermute | solution.py:359
  25.1 11.7 %collective-permute-start.3 = (bf16[256,128]{1,0:T(8,128)(2,1)S(1)}, bf16[256,128]{1,0:T(8,128)(2,1)S(1)}, u32[]{:S(2)}, u32[]{:S(2)}) collective-permute-start(bf16[256,128]{1,0:T(8,128)(2,1)S(1)} %slice_bitcast_fusion.5), channel_id=1, source_target_pairs={{0,160},{8,168},{16,176},{24,184},{32,192},{40,200},{48,208},{56,2... | collective-permute-start | bytes 196616 | tf_op jit(solution)/shard_map/ppermute | solution.py:359
  25.3 14.5 %collective-permute-start.4 = (bf16[256,128]{1,0:T(8,128)(2,1)S(1)}, bf16[256,128]{1,0:T(8,128)(2,1)S(1)}, u32[]{:S(2)}, u32[]{:S(2)}) collective-permute-start(bf16[256,128]{1,0:T(8,128)(2,1)S(1)} %slice_bitcast_fusion.4), channel_id=1, source_target_pairs={{0,96},{8,104},{16,112},{24,120},{32,128},{40,136},{48,144},{56,15... | collective-permute-start | bytes 196616 | tf_op jit(solution)/shard_map/ppermute | solution.py:359
  28.9 14.8 %all-to-all-start = ((bf16[8,24,1536]{2,1,0:T(8,128)(2,1)}), bf16[8,24,1536]{2,1,0:T(8,128)(2,1)S(1)}, u32[]{:S(2)}, u32[]{:S(2)}) async-start(bf16[8,24,1536]{2,1,0:T(8,128)(2,1)} %bitcast.6), calls=%async_computation | async-start | bytes 1179648 | tf_op jit(solution)/shard_map/all_to_all | solution.py:370
  43.8 0.7 copy-start
  52.0 20.3 %collective-permute-start.9 = (bf16[256,128]{1,0:T(8,128)(2,1)S(1)}, bf16[256,128]{1,0:T(8,128)(2,1)S(1)}, u32[]{:S(2)}, u32[]{:S(2)}) collective-permute-start(bf16[256,128]{1,0:T(8,128)(2,1)S(1)} %get-tuple-element.47), channel_id=1, source_target_pairs={{0,160},{8,168},{16,176},{24,184},{32,192},{40,200},{48,208},{56,2... | collective-permute-start | bytes 196616 | tf_op jit(solution)/shard_map/ppermute | solution.py:359
  54.4 17.8 %collective-permute-start.7 = (bf16[2,2,256,128]{3,2,1,0:T(8,128)(2,1)S(1)}, bf16[2,2,256,128]{3,2,1,0:T(8,128)(2,1)S(1)}, u32[]{:S(2)}, u32[]{:S(2)}) collective-permute-start(bf16[2,2,256,128]{3,2,1,0:T(8,128)(2,1)S(1)} %get-tuple-element.44), channel_id=1, source_target_pairs={{0,192},{8,200},{16,208},{24,216},{32,224},{40,232},{48,240},{56,2... | collective-permute-start | bytes 786440 | tf_op jit(solution)/shard_map/ppermute | solution.py:359
  58.2 20.7 %collective-permute-start.8 = (bf16[2,2,256,128]{3,2,1,0:T(8,128)(2,1)S(1)}, bf16[2,2,256,128]{3,2,1,0:T(8,128)(2,1)S(1)}, u32[]{:S(2)}, u32[]{:S(2)}) collective-permute-start(bf16[2,2,256,128]{3,2,1,0:T(8,128)(2,1)S(1)} %get-tuple-element.45), channel_id=1, source_target_pairs={{0,64},{8,72},{16,80},{24,88},{32,96},{40,104},{48,112},{56,120},{... | collective-permute-start | bytes 786440 | tf_op jit(solution)/shard_map/ppermute | solution.py:359
  64.0 23.3 %all-to-all-start.1 = ((bf16[8,24,1536]{2,1,0:T(8,128)(2,1)}), bf16[8,24,1536]{2,1,0:T(8,128)(2,1)S(1)}, u32[]{:S(2)}, u32[]{:S(2)}) async-start(bf16[8,24,1536]{2,1,0:T(8,128)(2,1)} %bitcast.13), calls=%async_computation.1 | async-start | bytes 1179648 | tf_op jit(solution)/shard_map/all_to_all | solution.py:381
  70.4 8.5 %collective-permute-start.11 = (bf16[256,128]{1,0:T(8,128)(2,1)S(1)}, bf16[256,128]{1,0:T(8,128)(2,1)S(1)}, u32[]{:S(2)}, u32[]{:S(2)}) collective-permute-start(bf16[256,128]{1,0:T(8,128)(2,1)S(1)} %get-tuple-element.49), channel_id=1, source_target_pairs={{0,96},{8,104},{16,112},{24,120},{32,128},{40,136},{48,144},{56,15... | collective-permute-start | bytes 196616 | tf_op jit(solution)/shard_map/ppermute | solution.py:359
  72.3 6.8 %collective-permute-start.10 = (bf16[2,256,128]{2,1,0:T(8,128)(2,1)S(1)}, bf16[2,256,128]{2,1,0:T(8,128)(2,1)S(1)}, u32[]{:S(2)}, u32[]{:S(2)}) collective-permute-start(bf16[2,256,128]{2,1,0:T(8,128)(2,1)S(1)} %fusion.3), channel_id=1, source_target_pairs={{0,224},{8,232},{16,240},{24,248},{32,0},{40,8},{48,16},{56,24},{6... | collective-permute-start | bytes 393224 | tf_op jit(solution)/shard_map/ppermute | solution.py:359
  79.0 6.3 %collective-permute-start.12 = (bf16[2,256,128]{2,1,0:T(8,128)(2,1)S(1)}, bf16[2,256,128]{2,1,0:T(8,128)(2,1)S(1)}, u32[]{:S(2)}, u32[]{:S(2)}) collective-permute-start(bf16[2,256,128]{2,1,0:T(8,128)(2,1)S(1)} %fusion.1), channel_id=1, source_target_pairs={{0,32},{8,40},{16,48},{24,56},{32,64},{40,72},{48,80},{56,88},{64,... | collective-permute-start | bytes 393224 | tf_op jit(solution)/shard_map/ppermute | solution.py:359
  85.3 10.5 %collective-permute-start.13 = (bf16[2,256,128]{2,1,0:T(8,128)(2,1)S(1)}, bf16[2,256,128]{2,1,0:T(8,128)(2,1)S(1)}, u32[]{:S(2)}, u32[]{:S(2)}) collective-permute-start(bf16[2,256,128]{2,1,0:T(8,128)(2,1)S(1)} %fusion.6), channel_id=1, source_target_pairs={{0,0},{160,8},{224,16},{192,24},{32,32},{128,40},{64,48},{96,56},{... | collective-permute-start | bytes 393224 | tf_op jit(solution)/shard_map/ppermute | solution.py:387

commit v3 on v1

--- a/solution.py
+++ b/solution.py
@@ -48,9 +48,9 @@
         functools.partial(pack_kernel, heads),
         out_shape=jax.ShapeDtypeStruct((rows, total), bf16),
         scratch_shapes=[VMEM((total // head_dim, rows, head_dim), f32)],
-        compiler_params=pltpu.CompilerParams(vmem_limit_bytes=LIMIT),
+        compiler_params=pltpu.CompilerParams(vmem_limit_bytes=7 * LIMIT),
         cost_estimate=pl.CostEstimate(
-            flops=rows * total, bytes_accessed=4 * rows * total, transcendentals=0
+            flops=int(2e9), bytes_accessed=4 * rows * total, transcendentals=0
         ),
     )(
         q.reshape(rows, width),
@@ -95,7 +95,7 @@
         scratch_shapes=[VMEM((total // head_dim, rows, head_dim), f32)],
         compiler_params=pltpu.CompilerParams(vmem_limit_bytes=LIMIT),
         cost_estimate=pl.CostEstimate(
-            flops=rows * total, bytes_accessed=4 * rows * total, transcendentals=0
+            flops=int(1e9), bytes_accessed=4 * rows * total, transcendentals=0
         ),
     )(x)
     return [piece.reshape(1, slots, heads, piece.shape[1]) for piece in outs]
@@ -163,16 +163,13 @@
 
 
 def far_kernel(group, chunks, scale, len_ref, x_ref, stats_ref, *refs):
-    count = chunks + 1
-    shard_refs, grad_refs = refs[:count], refs[count:2 * count]
-    k_refs = [shard_refs[0]] + [r.at[0] for r in shard_refs[2:]]
-    v_refs = [shard_refs[1]] + [r.at[1] for r in shard_refs[2:]]
-    dk_refs = [grad_refs[0]] + [r.at[0] for r in grad_refs[2:]]
-    dv_refs = [grad_refs[1]] + [r.at[1] for r in grad_refs[2:]]
+    shard_refs, grad_refs = refs[:chunks], refs[chunks:2 * chunks]
+    k_refs, v_refs = [[r.at[i] for r in shard_refs] for i in range(2)]
+    dk_refs, dv_refs = [[r.at[i] for r in grad_refs] for i in range(2)]
     (total_ref, ot_ref, qt_ref,
-     q_s, g_s, keys_t, values_t, e_s, d_s, pb_s, sb_s, dk_s, dv_s) = refs[2 * count:]
+     q_s, g_s, keys_t, values_t, e_s, d_s, pb_s, sb_s, dk_s, dv_s) = refs[2 * chunks:]
     cap = x_ref.shape[0]
-    span, head_dim = shard_refs[0].shape
+    span, head_dim = shard_refs[0].shape[1:]
     length = len_ref[lax.axis_index("seq")]
     turn = scale * math.log2(math.e)
     stack_rows(x_ref, q_s, g_s, group)
@@ -278,7 +275,7 @@
         )
 
 
-def call(body, products, keys, rows, head_dim, ins, outs, scratch, limit):
+def call(body, micros, ins, outs, scratch, limit):
     smem = pl.BlockSpec(memory_space=pltpu.SMEM)
     vmem = pl.BlockSpec(memory_space=pltpu.VMEM)
     return pl.pallas_call(
@@ -289,9 +286,9 @@
         scratch_shapes=scratch,
         compiler_params=pltpu.CompilerParams(vmem_limit_bytes=limit * 1024 * 1024),
         cost_estimate=pl.CostEstimate(
-            flops=2 * products * rows * keys * head_dim,
+            flops=int(micros * 1.15e9),
             bytes_accessed=sum(x.size * x.dtype.itemsize for x in ins + outs),
-            transcendentals=rows * keys,
+            transcendentals=0,
         ),
     )(*ins)
 
@@ -299,10 +296,10 @@
 def near_stats(lengths, x, shards, group, scale):
     cap = x.shape[0]
     _, span, head_dim = shards[0].shape
-    rows, keys = group * cap, len(shards) * span + cap
+    rows = group * cap
     return call(
         functools.partial(near_stats_kernel, group, len(shards), scale),
-        2, keys, rows, head_dim,
+        1.5,
         [lengths, x, *shards],
         [jax.ShapeDtypeStruct((3, rows), f32)],
         [VMEM((rows, head_dim), bf16)] * 2,
@@ -312,12 +309,12 @@
 
 def far_pass(lengths, x, stats, shards, group, scale):
     cap = x.shape[0]
-    span, head_dim = shards[0].shape
-    chunks = len(shards) - 1
+    _, span, head_dim = shards[0].shape
+    chunks = len(shards)
     rows, keys = group * cap, chunks * span
     outs = call(
         functools.partial(far_kernel, group, chunks, scale),
-        6, keys, rows, head_dim,
+        7.6,
         [lengths, x, stats, *shards],
         [jax.ShapeDtypeStruct(shard.shape, bf16) for shard in shards]
         + [jax.ShapeDtypeStruct((2, rows), f32)]
@@ -329,7 +326,7 @@
         + [VMEM((keys, head_dim), f32)] * 2,
         24,
     )
-    return outs[:chunks + 1], outs[chunks + 1:]
+    return outs[:chunks], outs[chunks:]
 
 
 def near_pass(lengths, x, totals, shards, group, scale):
@@ -338,10 +335,10 @@
     rows, keys = group * cap, len(shards) * span + cap
     outs = call(
         functools.partial(near_kernel, group, len(shards), scale),
-        6, keys, rows, head_dim,
+        4,
         [lengths, x, *totals, *shards],
         [jax.ShapeDtypeStruct((cap, packed), bf16)]
-        + [jax.ShapeDtypeStruct((2, span, head_dim), f32)] * len(shards),
+        + [jax.ShapeDtypeStruct(shard.shape, f32) for shard in shards],
         [VMEM((rows, head_dim), bf16)] * 2
         + [VMEM((head_dim, keys), bf16)] * 2
         + [VMEM((keys, 256), bf16)] * 2
@@ -377,30 +374,28 @@
     own, packed = lax.optimization_barrier((own, packed))
     x = lax.all_to_all(packed, "head", split_axis=0, concat_axis=0, tiled=True)
 
-    up, down = shift(own, 1), shift(own, -1)
-    far_keys = shift(down[0], -3)
-    far_values = shift(up[1], 3)
-    up3, down3 = shift(up, 2), shift(down, -2)
-    up2, down2 = shift(up, 1), shift(down, -1)
-
-    near = [own, up, down]
-    stats = near_stats(comp_len, x, near, group, scale)
-    grads, totals = far_pass(
-        comp_len, x, stats, [far_keys, far_values, up3, down3, up2, down2], group, scale
-    )
-    moved = [
-        shift(grad, steps).astype(f32) for grad, steps in zip(grads, (3, -3, -2, 2, -1, 1))
-    ]
-    out, (own_grad, up_grad, down_grad) = near_pass(comp_len, x, totals, near, group, scale)
-    far_dk, far_dv, up3, down3, up2, down2 = moved
-    up_sum = up_grad + up2 + up3
-    down_sum = down_grad + down2 + down3
-    up_sum = up_sum + jnp.pad(far_dv[None], ((1, 0), (0, 0), (0, 0)))
-    down_sum = down_sum + jnp.pad(far_dk[None], ((0, 1), (0, 0), (0, 0)))
+    up, down = [own], [own]
+    for step in range(1, ring // 2 + 1):
+        up.append(shift(up[-1], 1))
+        if step < ring - step:
+            down.append(shift(down[-1], -1))
+
+    far, steps = [], []
+    for step in range(1, ring // 2 + 1):
+        far.append(up[step])
+        steps.append(-step)
+        if step < ring - step:
+            far.append(down[step])
+            steps.append(step)
+    stats = near_stats(comp_len, x, [own], group, scale)
+    grads, totals = far_pass(comp_len, x, stats, far, group, scale)
+    moved = [shift(grad, step) for grad, step in zip(grads, steps)]
+    out, (own_grad,) = near_pass(comp_len, x, totals, [own], group, scale)
+    own_grad, moved = lax.optimization_barrier((own_grad, moved))
+    summed = own_grad
+    for part in moved:
+        summed = summed + part.astype(f32)
     back = lax.all_to_all(out, "head", split_axis=0, concat_axis=0, tiled=True)
-    up_sum = shift(up_sum.astype(bf16), -1)
-    down_sum = shift(down_sum.astype(bf16), 1)
-    summed = own_grad + up_sum.astype(f32) + down_sum.astype(f32)
     attn_out, grad_q, grad_k, grad_v = unpack(back, heads, width, head_dim)
     placed = lax.ppermute(summed.astype(bf16), "seq", to_owner).astype(f32)
     return (attn_out, grad_q, grad_k, grad_v, placed[0][:, None], placed[1][:, None])

time: 95.9 us -> 92 us (0.959)
  starting transfers between devices: 49.6 us -> 44.7 us
  waiting for transfers between devices: 24.9 us -> 28.7 us
  local copies, waits for them, and re-layouts: 3.27 us -> 0.72 us
    ppermute x16 -> x14, starting transfers between devices: 25.2 us -> 20.8 us  [shift(): return lax.ppermute(x, 'seq', pairs)]
    unnamed x10 -> x2, local copies, waits for them, and re-layouts: 2.54 us -> 0.01 us
    ppermute x1, waiting for transfers between devices: 0.06 us -> 1.54 us  [on_device(): lax.ppermute(jnp.stack([prefix_k[:, 0], prefix_v[:, 0]]), 'seq', to_prompt)]
    ppermute x16 -> x14, waiting for transfers between devices: 14.4 us -> 15.8 us  [shift(): return lax.ppermute(x, 'seq', pairs)]
    pallas_call x1, Pallas kernels: 1.12 us -> 2.19 us  [pack(): pl.pallas_call(functools.partial(pack_kernel, heads), out_shape=jax.Shape...]
    pallas_call x3, Pallas kernels: 13.7 us -> 12.6 us  [call(): pl.pallas_call(body, out_shape=outs, in_specs=[smem] + [vmem] * (len(ins)...]
  transfers between devices with their start and end apart: 20 -> 18, of which waited for: 6 -> 8; matrix products, arithmetic and copies ran while one was open for 1% -> 1% of each run, Pallas kernels for 10% -> 8%
where the time goes in v3:
time: 92 us; the launch traced here: 91.6 us
  starting transfers between devices  44.7 us (49%)
  waiting for transfers between devices  28.7 us (31%)
  Pallas kernels  15.8 us (17%)
  other arithmetic  1.02 us (1%)
    ppermute x14, starting transfers between devices, shift(): return lax.ppermute(x, 'seq', pairs)  20.8 us
    ppermute x14, waiting for transfers between devices, shift(): return lax.ppermute(x, 'seq', pairs)  15.8 us
    pallas_call x3, Pallas kernels, call(): pl.pallas_call(body, out_shape=outs, in_specs=[smem] + [vmem] * (len(ins)...  12.6 us
    ppermute x1, waiting for transfers between devices, on_device(): placed = lax.ppermute(summed.astype(bf16), 'seq', to_owner).astype(f32)  11.3 us
    ppermute x1, starting transfers between devices, on_device(): lax.ppermute(jnp.stack([prefix_k[:, 0], prefix_v[:, 0]]), 'seq', to_prompt)  7.94 us
    all_to_all x1, starting transfers between devices, on_device(): x = lax.all_to_all(packed, 'head', split_axis=0, concat_axis=0, tiled=True)  7.26 us
    all_to_all x1, starting transfers between devices, on_device(): back = lax.all_to_all(out, 'head', split_axis=0, concat_axis=0, tiled=True)  6.8 us
    pallas_call x1, Pallas kernels, pack(): pl.pallas_call(functools.partial(pack_kernel, heads), out_shape=jax.Shape...  2.19 us
  transfers between devices with their start and end apart: 18, of which 8 were waited for; matrix products, arithmetic and copies ran while one was open for 1% of the time, Pallas kernels for 8%

profile of v3, /device:TPU:24, one launch (start us, length us, event | category | flops | bytes accessed | tf_op | source)
XLA Modules:
  0.0 91.6 jit_solution(16883928827254595618)
XLA Ops:
  0.6 0.9 pad_maximum_fusion
  1.5 7.9 %collective-permute-start = (bf16[2,256,128]{2,1,0:T(8,128)(2,1)S(1)}, bf16[2,256,128]{2,1,0:T(8,128)(2,1)S(1)}, u32[]{:S(2)}, u32[]{:S(2)}) collective-permute-start(bf16[2,256,128]{2,1,0:T(8,128)(2,1)S(1)} %pad_maximum_fusion), channel_id=1, source_target_pairs={{0,0},{8,160},{16,224},{24,192},{32,32},{40,128},{48,64},{56,96},{... | collective-permute-start | bytes 393224 | tf_op jit(solution)/shard_map/ppermute | solution.py:372
  9.5 2.2 %shard_map.118 = bf16[192,1536]{1,0:T(8,128)(2,1)} custom-call(bf16[192,640]{1,0:T(8,128)(2,1)} %bitcast.29, bf16[192,640]{1,0:T(8,128)(2,1)} %bitcast.30, bf16[192,128]{1,0:T(8,128)(2,1)} %bitcast.31, bf16[192,128]{1,0:T(8,128)(2,1)} %bitcast.32), custom_call_target="tpu_custom_call" | custom-call | flops 2000000000 | bytes 1179648 | tf_op jit(solution)/shard_map/pallas_call | solution.py:47
  11.7 1.5 %collective-permute-done.refs_0_ = bf16[2,256,128]{2,1,0:T(8,128)(2,1)S(1)} collective-permute-done((bf16[2,256,128]{2,1,0:T(8,128)(2,1)S(1)}, bf16[2,256,128]{2,1,0:T(8,128)(2,1)S(1)}, u32[]{:S(2)}, u32[]{:S(2)}) %collective-permute-start) | collective-permute-done | bytes 131104 | tf_op jit(solution)/shard_map/ppermute | solution.py:372
  13.2 7.3 %all-to-all-start = ((bf16[8,24,1536]{2,1,0:T(8,128)(2,1)}), bf16[8,24,1536]{2,1,0:T(8,128)(2,1)S(1)}, u32[]{:S(2)}, u32[]{:S(2)}) async-start(bf16[8,24,1536]{2,1,0:T(8,128)(2,1)} %bitcast.24), calls=%async_computation | async-start | bytes 1179648 | tf_op jit(solution)/shard_map/all_to_all | solution.py:375
  20.5 0.0 copy-start
  20.5 0.5 collective-permute-start.1
  21.0 2.7 %collective-permute-start.2 = (bf16[2,256,128]{2,1,0:T(8,128)(2,1)S(1)}, bf16[2,256,128]{2,1,0:T(8,128)(2,1)S(1)}, u32[]{:S(2)}, u32[]{:S(2)}) collective-permute-start(bf16[2,256,128]{2,1,0:T(8,128)(2,1)S(1)} %collective-permute-done.refs_0_), channel_id=1, source_target_pairs={{0,224},{8,232},{16,240},{24,248},{32,0},{40,8},{48,16},{56,24},{6... | collective-permute-start | bytes 393224 | tf_op jit(solution)/shard_map/ppermute | solution.py:370
  23.7 2.9 %collective-permute-done.1.refs_0_ = bf16[2,256,128]{2,1,0:T(8,128)(2,1)S(1)} collective-permute-done((bf16[2,256,128]{2,1,0:T(8,128)(2,1)S(1)}, bf16[2,256,128]{2,1,0:T(8,128)(2,1)S(1)}, u32[]{:S(2)}, u32[]{:S(2)}) %collective-permute-start.1) | collective-permute-done | bytes 131104 | tf_op jit(solution)/shard_map/ppermute | solution.py:370
  26.7 0.0 collective-permute-start.3
  26.7 0.0 collective-permute-done.2.refs_1_
  26.7 3.2 %collective-permute-start.4 = (bf16[2,256,128]{2,1,0:T(8,128)(2,1)S(1)}, bf16[2,256,128]{2,1,0:T(8,128)(2,1)S(1)}, u32[]{:S(2)}, u32[]{:S(2)}) collective-permute-start(bf16[2,256,128]{2,1,0:T(8,128)(2,1)S(1)} %collective-permute-done.2.refs_1_), channel_id=1, source_target_pairs={{0,224},{8,232},{16,240},{24,248},{32,0},{40,8},{48,16},{56,24},{6... | collective-permute-start | bytes 393224 | tf_op jit(solution)/shard_map/ppermute | solution.py:370
  29.9 2.9 %collective-permute-done.3.refs_2_ = bf16[2,256,128]{2,1,0:T(8,128)(2,1)S(1)} collective-permute-done((bf16[2,256,128]{2,1,0:T(8,128)(2,1)S(1)}, bf16[2,256,128]{2,1,0:T(8,128)(2,1)S(1)}, u32[]{:S(2)}, u32[]{:S(2)}) %collective-permute-start.3) | collective-permute-done | bytes 131104 | tf_op jit(solution)/shard_map/ppermute | solution.py:370
  32.8 0.0 collective-permute-start.5
  32.8 0.0 collective-permute-done.4.refs_3_
  32.8 3.2 %collective-permute-start.6 = (bf16[2,256,128]{2,1,0:T(8,128)(2,1)S(1)}, bf16[2,256,128]{2,1,0:T(8,128)(2,1)S(1)}, u32[]{:S(2)}, u32[]{:S(2)}) collective-permute-start(bf16[2,256,128]{2,1,0:T(8,128)(2,1)S(1)} %collective-permute-done.4.refs_3_), channel_id=1, source_target_pairs={{0,224},{8,232},{16,240},{24,248},{32,0},{40,8},{48,16},{56,24},{6... | collective-permute-start | bytes 393224 | tf_op jit(solution)/shard_map/ppermute | solution.py:370
  36.1 3.0 %collective-permute-done.5.refs_4_ = bf16[2,256,128]{2,1,0:T(8,128)(2,1)S(1)} collective-permute-done((bf16[2,256,128]{2,1,0:T(8,128)(2,1)S(1)}, bf16[2,256,128]{2,1,0:T(8,128)(2,1)S(1)}, u32[]{:S(2)}, u32[]{:S(2)}) %collective-permute-start.5) | collective-permute-done | bytes 131104 | tf_op jit(solution)/shard_map/ppermute | solution.py:370
  39.1 0.0 collective-permute-start.7
  39.1 0.0 all-to-all-done
  39.1 0.0 copy-done
  39.1 1.6 %shard_map.119.stats_ref = f32[3,960]{1,0:T(4,128)S(1)} custom-call(s32[32]{0:T(128)S(1)} %copy-done, bf16[192,1536]{1,0:T(8,128)(2,1)S(1)} %bitcast.20, bf16[2,256,128]{2,1,0:T(8,128)(2,1)S(1)} %collective-permute-done.refs_0_), custom_call_target="tpu_custom_call" | custom-call | flops 1724999936 | bytes 732544 | tf_op jit(solution)/shard_map/pallas_call | solution.py:281
  40.7 0.0 collective-permute-done.6.refs_5_
  40.7 4.6 %collective-permute-done.7.refs_6_ = bf16[2,256,128]{2,1,0:T(8,128)(2,1)S(1)} collective-permute-done((bf16[2,256,128]{2,1,0:T(8,128)(2,1)S(1)}, bf16[2,256,128]{2,1,0:T(8,128)(2,1)S(1)}, u32[]{:S(2)}, u32[]{:S(2)}) %collective-permute-start.7) | collective-permute-done | bytes 131104 | tf_op jit(solution)/shard_map/ppermute | solution.py:370
  45.3 7.3 %shard_map.120 = (bf16[2,256,128]{2,1,0:T(8,128)(2,1)S(1)}, bf16[2,256,128]{2,1,0:T(8,128)(2,1)S(1)}, bf16[2,256,128]{2,1,0:T(8,128)(2,1)S(1)}, bf16[2,256,128]{...) custom-call(s32[32]{0:T(128)S(1)} %copy-done, ...), custom_call_target="tpu_custom_call" | custom-call | flops 8739999744 | bytes 3427200 | tf_op jit(solution)/shard_map/pallas_call | solution.py:281
  52.6 0.5 collective-permute-start.8
  53.0 1.6 %collective-permute-start.9 = (bf16[2,256,128]{2,1,0:T(8,128)(2,1)S(1)}, bf16[2,256,128]{2,1,0:T(8,128)(2,1)S(1)}, u32[]{:S(2)}, u32[]{:S(2)}) collective-permute-start(bf16[2,256,128]{2,1,0:T(8,128)(2,1)S(1)} %get-tuple-element.44), channel_id=1, source_target_pairs={{0,32},{8,40},{16,48},{24,56},{32,64},{40,72},{48,80},{56,88},{64,... | collective-permute-start | bytes 393224 | tf_op jit(solution)/shard_map/ppermute | solution.py:370
  54.7 0.0 collective-permute-start.10
  54.7 2.9 %collective-permute-start.11 = (bf16[2,256,128]{2,1,0:T(8,128)(2,1)S(1)}, bf16[2,256,128]{2,1,0:T(8,128)(2,1)S(1)}, u32[]{:S(2)}, u32[]{:S(2)}) collective-permute-start(bf16[2,256,128]{2,1,0:T(8,128)(2,1)S(1)} %get-tuple-element.46), channel_id=1, source_target_pairs={{0,64},{8,72},{16,80},{24,88},{32,96},{40,104},{48,112},{56,120},{... | collective-permute-start | bytes 393224 | tf_op jit(solution)/shard_map/ppermute | solution.py:370
  57.6 1.6 %collective-permute-start.12 = (bf16[2,256,128]{2,1,0:T(8,128)(2,1)S(1)}, bf16[2,256,128]{2,1,0:T(8,128)(2,1)S(1)}, u32[]{:S(2)}, u32[]{:S(2)}) collective-permute-start(bf16[2,256,128]{2,1,0:T(8,128)(2,1)S(1)} %get-tuple-element.47), channel_id=1, source_target_pairs={{0,160},{8,168},{16,176},{24,184},{32,192},{40,200},{48,208},{56,2... | collective-permute-start | bytes 393224 | tf_op jit(solution)/shard_map/ppermute | solution.py:370
  59.2 1.6 %collective-permute-done.8 = bf16[2,256,128]{2,1,0:T(8,128)(2,1)S(1)} collective-permute-done((bf16[2,256,128]{2,1,0:T(8,128)(2,1)S(1)}, bf16[2,256,128]{2,1,0:T(8,128)(2,1)S(1)}, u32[]{:S(2)}, u32[]{:S(2)}) %collective-permute-start.8) | collective-permute-done | bytes 131104 | tf_op jit(solution)/shard_map/ppermute | solution.py:370
  60.8 2.4 %collective-permute-start.13 = (bf16[2,256,128]{2,1,0:T(8,128)(2,1)S(1)}, bf16[2,256,128]{2,1,0:T(8,128)(2,1)S(1)}, u32[]{:S(2)}, u32[]{:S(2)}) collective-permute-start(bf16[2,256,128]{2,1,0:T(8,128)(2,1)S(1)} %get-tuple-element.48), channel_id=1, source_target_pairs={{0,96},{8,104},{16,112},{24,120},{32,128},{40,136},{48,144},{56,15... | collective-permute-start | bytes 393224 | tf_op jit(solution)/shard_map/ppermute | solution.py:370
  63.2 0.0 collective-permute-done.9
  63.2 2.0 %collective-permute-start.14 = (bf16[2,256,128]{2,1,0:T(8,128)(2,1)S(1)}, bf16[2,256,128]{2,1,0:T(8,128)(2,1)S(1)}, u32[]{:S(2)}, u32[]{:S(2)}) collective-permute-start(bf16[2,256,128]{2,1,0:T(8,128)(2,1)S(1)} %get-tuple-element.49), channel_id=1, source_target_pairs={{0,128},{8,136},{16,144},{24,152},{32,160},{40,168},{48,176},{56,1... | collective-permute-start | bytes 393224 | tf_op jit(solution)/shard_map/ppermute | solution.py:370
  65.2 3.7 %shard_map.121 = (bf16[192,1536]{1,0:T(8,128)(2,1)}, f32[2,256,128]{2,1,0:T(8,128)S(1)}) custom-call(s32[32]{0:T(128)S(1)} %copy-done, bf16[192,1536]{1,0:T(8,128)(2,1)S(1)} %bitcast.22, f32[2,960]{1,0:T(2,128)S(1)} %get-tuple-element.34.total_ref, f32[128,960]{1,0:T(8,128)S(1)} %get-tuple-element.35.ot_ref, f32[128,960]{1,0:T(8,128)S(1)} %get-tuple-element.36.qt_ref, ...), custom_call_target="tpu_custom_call" | custom-call | flops 4600000000 | bytes 2563712 | tf_op jit(solution)/shard_map/pallas_call | solution.py:281
  69.0 6.8 %all-to-all-start.1 = ((bf16[8,24,1536]{2,1,0:T(8,128)(2,1)}), bf16[8,24,1536]{2,1,0:T(8,128)(2,1)S(1)}, u32[]{:S(2)}, u32[]{:S(2)}) async-start(bf16[8,24,1536]{2,1,0:T(8,128)(2,1)} %bitcast.8), calls=%async_computation.1 | async-start | bytes 1179648 | tf_op jit(solution)/shard_map/all_to_all | solution.py:398
  75.8 0.0 collective-permute-done.10
  75.8 0.0 collective-permute-done.11
  75.8 0.0 collective-permute-done.12
  75.8 0.0 collective-permute-done.13
  75.8 0.7 collective-permute-done.14
  76.5 0.1 add_convert_fusion
  76.7 1.9 %collective-permute-start.15 = (bf16[2,256,128]{2,1,0:T(8,128)(2,1)S(1)}, bf16[2,256,128]{2,1,0:T(8,128)(2,1)S(1)}, u32[]{:S(2)}, u32[]{:S(2)}) collective-permute-start(bf16[2,256,128]{2,1,0:T(8,128)(2,1)S(1)} %add_convert_fusion), channel_id=1, source_target_pairs={{0,0},{160,8},{224,16},{192,24},{32,32},{128,40},{64,48},{96,56},{... | collective-permute-start | bytes 393224 | tf_op jit(solution)/shard_map/ppermute | solution.py:400
  78.6 11.3 %collective-permute-done.15 = bf16[2,256,128]{2,1,0:T(8,128)(2,1)S(1)} collective-permute-done((bf16[2,256,128]{2,1,0:T(8,128)(2,1)S(1)}, bf16[2,256,128]{2,1,0:T(8,128)(2,1)S(1)}, u32[]{:S(2)}, u32[]{:S(2)}) %collective-permute-start.15) | collective-permute-done | bytes 131104 | tf_op jit(solution)/shard_map/ppermute | solution.py:400
  89.9 0.7 fusion
  90.6 0.0 all-to-all-done.1
  90.6 1.0 %shard_map.122 = (bf16[192,640]{1,0:T(8,128)(2,1)}, bf16[192,640]{1,0:T(8,128)(2,1)}, bf16[192,128]{1,0:T(8,128)(2,1)}, bf16[192,128]{1,0:T(8,128)(2,1)}) custom-call(bf16[192,1536]{1,0:T(8,128)(2,1)S(1)} %bitcast.23), custom_call_target="tpu_custom_call" | custom-call | flops 1000000000 | bytes 1179648 | tf_op jit(solution)/shard_map/pallas_call | solution.py:87
Async XLA Ops:
  1.5 11.7 %collective-permute-start = (bf16[2,256,128]{2,1,0:T(8,128)(2,1)S(1)}, bf16[2,256,128]{2,1,0:T(8,128)(2,1)S(1)}, u32[]{:S(2)}, u32[]{:S(2)}) collective-permute-start(bf16[2,256,128]{2,1,0:T(8,128)(2,1)S(1)} %pad_maximum_fusion), channel_id=1, source_target_pairs={{0,0},{8,160},{16,224},{24,192},{32,32},{40,128},{48,64},{56,96},{... | collective-permute-start | bytes 393224 | tf_op jit(solution)/shard_map/ppermute | solution.py:372
  13.2 25.9 %all-to-all-start = ((bf16[8,24,1536]{2,1,0:T(8,128)(2,1)}), bf16[8,24,1536]{2,1,0:T(8,128)(2,1)S(1)}, u32[]{:S(2)}, u32[]{:S(2)}) async-start(bf16[8,24,1536]{2,1,0:T(8,128)(2,1)} %bitcast.24), calls=%async_computation | async-start | bytes 1179648 | tf_op jit(solution)/shard_map/all_to_all | solution.py:375
  20.5 18.6 %copy-start = (s32[32]{0:T(128)S(1)}, s32[32]{0:T(128)}, u32[]{:S(2)}) copy-start(s32[32]{0:T(128)} %len_ref.5) | copy-start | bytes 388
  20.5 6.2 %collective-permute-start.1 = (bf16[2,256,128]{2,1,0:T(8,128)(2,1)S(1)}, bf16[2,256,128]{2,1,0:T(8,128)(2,1)S(1)}, u32[]{:S(2)}, u32[]{:S(2)}) collective-permute-start(bf16[2,256,128]{2,1,0:T(8,128)(2,1)S(1)} %collective-permute-done.refs_0_), channel_id=1, source_target_pairs={{0,32},{8,40},{16,48},{24,56},{32,64},{40,72},{48,80},{56,88},{64,... | collective-permute-start | bytes 393224 | tf_op jit(solution)/shard_map/ppermute | solution.py:370
  21.0 5.7 %collective-permute-start.2 = (bf16[2,256,128]{2,1,0:T(8,128)(2,1)S(1)}, bf16[2,256,128]{2,1,0:T(8,128)(2,1)S(1)}, u32[]{:S(2)}, u32[]{:S(2)}) collective-permute-start(bf16[2,256,128]{2,1,0:T(8,128)(2,1)S(1)} %collective-permute-done.refs_0_), channel_id=1, source_target_pairs={{0,224},{8,232},{16,240},{24,248},{32,0},{40,8},{48,16},{56,24},{6... | collective-permute-start | bytes 393224 | tf_op jit(solution)/shard_map/ppermute | solution.py:370
  26.7 6.2 %collective-permute-start.3 = (bf16[2,256,128]{2,1,0:T(8,128)(2,1)S(1)}, bf16[2,256,128]{2,1,0:T(8,128)(2,1)S(1)}, u32[]{:S(2)}, u32[]{:S(2)}) collective-permute-start(bf16[2,256,128]{2,1,0:T(8,128)(2,1)S(1)} %collective-permute-done.1.refs_0_), channel_id=1, source_target_pairs={{0,32},{8,40},{16,48},{24,56},{32,64},{40,72},{48,80},{56,88},{64,... | collective-permute-start | bytes 393224 | tf_op jit(solution)/shard_map/ppermute | solution.py:370
  26.7 6.2 %collective-permute-start.4 = (bf16[2,256,128]{2,1,0:T(8,128)(2,1)S(1)}, bf16[2,256,128]{2,1,0:T(8,128)(2,1)S(1)}, u32[]{:S(2)}, u32[]{:S(2)}) collective-permute-start(bf16[2,256,128]{2,1,0:T(8,128)(2,1)S(1)} %collective-permute-done.2.refs_1_), channel_id=1, source_target_pairs={{0,224},{8,232},{16,240},{24,248},{32,0},{40,8},{48,16},{56,24},{6... | collective-permute-start | bytes 393224 | tf_op jit(solution)/shard_map/ppermute | solution.py:370
  32.8 6.2 %collective-permute-start.5 = (bf16[2,256,128]{2,1,0:T(8,128)(2,1)S(1)}, bf16[2,256,128]{2,1,0:T(8,128)(2,1)S(1)}, u32[]{:S(2)}, u32[]{:S(2)}) collective-permute-start(bf16[2,256,128]{2,1,0:T(8,128)(2,1)S(1)} %collective-permute-done.3.refs_2_), channel_id=1, source_target_pairs={{0,32},{8,40},{16,48},{24,56},{32,64},{40,72},{48,80},{56,88},{64,... | collective-permute-start | bytes 393224 | tf_op jit(solution)/shard_map/ppermute | solution.py:370
  32.8 7.9 %collective-permute-start.6 = (bf16[2,256,128]{2,1,0:T(8,128)(2,1)S(1)}, bf16[2,256,128]{2,1,0:T(8,128)(2,1)S(1)}, u32[]{:S(2)}, u32[]{:S(2)}) collective-permute-start(bf16[2,256,128]{2,1,0:T(8,128)(2,1)S(1)} %collective-permute-done.4.refs_3_), channel_id=1, source_target_pairs={{0,224},{8,232},{16,240},{24,248},{32,0},{40,8},{48,16},{56,24},{6... | collective-permute-start | bytes 393224 | tf_op jit(solution)/shard_map/ppermute | solution.py:370
  39.1 6.2 %collective-permute-start.7 = (bf16[2,256,128]{2,1,0:T(8,128)(2,1)S(1)}, bf16[2,256,128]{2,1,0:T(8,128)(2,1)S(1)}, u32[]{:S(2)}, u32[]{:S(2)}) collective-permute-start(bf16[2,256,128]{2,1,0:T(8,128)(2,1)S(1)} %collective-permute-done.5.refs_4_), channel_id=1, source_target_pairs={{0,32},{8,40},{16,48},{24,56},{32,64},{40,72},{48,80},{56,88},{64,... | collective-permute-start | bytes 393224 | tf_op jit(solution)/shard_map/ppermute | solution.py:370
  52.6 8.2 %collective-permute-start.8 = (bf16[2,256,128]{2,1,0:T(8,128)(2,1)S(1)}, bf16[2,256,128]{2,1,0:T(8,128)(2,1)S(1)}, u32[]{:S(2)}, u32[]{:S(2)}) collective-permute-start(bf16[2,256,128]{2,1,0:T(8,128)(2,1)S(1)} %get-tuple-element.43), channel_id=1, source_target_pairs={{0,224},{8,232},{16,240},{24,248},{32,0},{40,8},{48,16},{56,24},{6... | collective-permute-start | bytes 393224 | tf_op jit(solution)/shard_map/ppermute | solution.py:370
  53.0 10.2 %collective-permute-start.9 = (bf16[2,256,128]{2,1,0:T(8,128)(2,1)S(1)}, bf16[2,256,128]{2,1,0:T(8,128)(2,1)S(1)}, u32[]{:S(2)}, u32[]{:S(2)}) collective-permute-start(bf16[2,256,128]{2,1,0:T(8,128)(2,1)S(1)} %get-tuple-element.44), channel_id=1, source_target_pairs={{0,32},{8,40},{16,48},{24,56},{32,64},{40,72},{48,80},{56,88},{64,... | collective-permute-start | bytes 393224 | tf_op jit(solution)/shard_map/ppermute | solution.py:370
  54.7 21.1 %collective-permute-start.10 = (bf16[2,256,128]{2,1,0:T(8,128)(2,1)S(1)}, bf16[2,256,128]{2,1,0:T(8,128)(2,1)S(1)}, u32[]{:S(2)}, u32[]{:S(2)}) collective-permute-start(bf16[2,256,128]{2,1,0:T(8,128)(2,1)S(1)} %get-tuple-element.45), channel_id=1, source_target_pairs={{0,192},{8,200},{16,208},{24,216},{32,224},{40,232},{48,240},{56,2... | collective-permute-start | bytes 393224 | tf_op jit(solution)/shard_map/ppermute | solution.py:370
  54.7 21.1 %collective-permute-start.11 = (bf16[2,256,128]{2,1,0:T(8,128)(2,1)S(1)}, bf16[2,256,128]{2,1,0:T(8,128)(2,1)S(1)}, u32[]{:S(2)}, u32[]{:S(2)}) collective-permute-start(bf16[2,256,128]{2,1,0:T(8,128)(2,1)S(1)} %get-tuple-element.46), channel_id=1, source_target_pairs={{0,64},{8,72},{16,80},{24,88},{32,96},{40,104},{48,112},{56,120},{... | collective-permute-start | bytes 393224 | tf_op jit(solution)/shard_map/ppermute | solution.py:370
  57.6 18.2 %collective-permute-start.12 = (bf16[2,256,128]{2,1,0:T(8,128)(2,1)S(1)}, bf16[2,256,128]{2,1,0:T(8,128)(2,1)S(1)}, u32[]{:S(2)}, u32[]{:S(2)}) collective-permute-start(bf16[2,256,128]{2,1,0:T(8,128)(2,1)S(1)} %get-tuple-element.47), channel_id=1, source_target_pairs={{0,160},{8,168},{16,176},{24,184},{32,192},{40,200},{48,208},{56,2... | collective-permute-start | bytes 393224 | tf_op jit(solution)/shard_map/ppermute | solution.py:370
  60.8 15.0 %collective-permute-start.13 = (bf16[2,256,128]{2,1,0:T(8,128)(2,1)S(1)}, bf16[2,256,128]{2,1,0:T(8,128)(2,1)S(1)}, u32[]{:S(2)}, u32[]{:S(2)}) collective-permute-start(bf16[2,256,128]{2,1,0:T(8,128)(2,1)S(1)} %get-tuple-element.48), channel_id=1, source_target_pairs={{0,96},{8,104},{16,112},{24,120},{32,128},{40,136},{48,144},{56,15... | collective-permute-start | bytes 393224 | tf_op jit(solution)/shard_map/ppermute | solution.py:370
  63.2 13.3 %collective-permute-start.14 = (bf16[2,256,128]{2,1,0:T(8,128)(2,1)S(1)}, bf16[2,256,128]{2,1,0:T(8,128)(2,1)S(1)}, u32[]{:S(2)}, u32[]{:S(2)}) collective-permute-start(bf16[2,256,128]{2,1,0:T(8,128)(2,1)S(1)} %get-tuple-element.49), channel_id=1, source_target_pairs={{0,128},{8,136},{16,144},{24,152},{32,160},{40,168},{48,176},{56,1... | collective-permute-start | bytes 393224 | tf_op jit(solution)/shard_map/ppermute | solution.py:370
  69.0 21.7 %all-to-all-start.1 = ((bf16[8,24,1536]{2,1,0:T(8,128)(2,1)}), bf16[8,24,1536]{2,1,0:T(8,128)(2,1)S(1)}, u32[]{:S(2)}, u32[]{:S(2)}) async-start(bf16[8,24,1536]{2,1,0:T(8,128)(2,1)} %bitcast.8), calls=%async_computation.1 | async-start | bytes 1179648 | tf_op jit(solution)/shard_map/all_to_all | solution.py:398
  76.7 13.3 %collective-permute-start.15 = (bf16[2,256,128]{2,1,0:T(8,128)(2,1)S(1)}, bf16[2,256,128]{2,1,0:T(8,128)(2,1)S(1)}, u32[]{:S(2)}, u32[]{:S(2)}) collective-permute-start(bf16[2,256,128]{2,1,0:T(8,128)(2,1)S(1)} %add_convert_fusion), channel_id=1, source_target_pairs={{0,0},{160,8},{224,16},{192,24},{32,32},{128,40},{64,48},{96,56},{... | collective-permute-start | bytes 393224 | tf_op jit(solution)/shard_map/ppermute | solution.py:400

commit v4 on v3

--- a/solution.py
+++ b/solution.py
@@ -275,13 +275,13 @@
         )
 
 
-def call(body, micros, ins, outs, scratch, limit):
+def call(body, micros, ins, outs, scratch, limit, scalars=1):
     smem = pl.BlockSpec(memory_space=pltpu.SMEM)
     vmem = pl.BlockSpec(memory_space=pltpu.VMEM)
     return pl.pallas_call(
         body,
         out_shape=outs,
-        in_specs=[smem] + [vmem] * (len(ins) - 1),
+        in_specs=[smem] * scalars + [vmem] * (len(ins) - scalars),
         out_specs=[vmem] * len(outs),
         scratch_shapes=scratch,
         compiler_params=pltpu.CompilerParams(vmem_limit_bytes=limit * 1024 * 1024),
@@ -349,6 +349,19 @@
     return outs[0], outs[1:]
 
 
+def sum_kernel(own_ref, *refs):
+    total = own_ref[...]
+    for ref in refs[:-1]:
+        total = total + ref[...].astype(f32)
+    refs[-1][...] = total.astype(bf16)
+
+
+def add_parts(own, parts):
+    return call(
+        sum_kernel, 12, [own, *parts], [jax.ShapeDtypeStruct(own.shape, bf16)], [], 8, scalars=0
+    )[0]
+
+
 def on_device(comp_q, comp_k, comp_v, comp_grad, prefix_k, prefix_v, comp_len):
     _, slots, heads, width = comp_q.shape
     head_dim = comp_k.shape[3]
@@ -366,12 +379,13 @@
     to_owner = [(b, a) for a, b in to_prompt]
 
     def shift(x, steps):
-        pairs = [(s, (s + PROMPTS * steps) % devices) for s in range(devices)]
+        way = (PROMPTS * steps, -PROMPTS * steps)
+        pairs = [(s, (s + way[s % 2]) % devices) for s in range(devices)]
         return lax.ppermute(x, "seq", pairs)
 
     own = lax.ppermute(jnp.stack([prefix_k[:, 0], prefix_v[:, 0]]), "seq", to_prompt)
     packed = pack(comp_q, comp_grad, comp_k, comp_v)
-    own, packed = lax.optimization_barrier((own, packed))
+    own, _ = lax.optimization_barrier((own, packed))
     x = lax.all_to_all(packed, "head", split_axis=0, concat_axis=0, tiled=True)
 
     up, down = [own], [own]
@@ -391,13 +405,14 @@
     grads, totals = far_pass(comp_len, x, stats, far, group, scale)
     moved = [shift(grad, step) for grad, step in zip(grads, steps)]
     out, (own_grad,) = near_pass(comp_len, x, totals, [own], group, scale)
-    own_grad, moved = lax.optimization_barrier((own_grad, moved))
-    summed = own_grad
-    for part in moved:
-        summed = summed + part.astype(f32)
+    summed = add_parts(own_grad, moved)
     back = lax.all_to_all(out, "head", split_axis=0, concat_axis=0, tiled=True)
     attn_out, grad_q, grad_k, grad_v = unpack(back, heads, width, head_dim)
-    placed = lax.ppermute(summed.astype(bf16), "seq", to_owner).astype(f32)
+    placed = lax.ppermute(summed, "seq", to_owner)
+    placed, (attn_out, grad_q, grad_k, grad_v) = lax.optimization_barrier(
+        (placed, (attn_out, grad_q, grad_k, grad_v))
+    )
+    placed = placed.astype(f32)
     return (attn_out, grad_q, grad_k, grad_v, placed[0][:, None], placed[1][:, None])
 
 

time: 92 us -> 87.3 us (0.949)
  waiting for transfers between devices: 28.7 us -> 20.6 us
  starting transfers between devices: 44.7 us -> 47.7 us
    ppermute x1, waiting for transfers between devices: 11.3 us -> 1.7 us  [on_device(): placed = lax.ppermute(summed, 'seq', to_owner)]
    all_to_all x1, waiting for transfers between devices: 0.01 us -> 5.47 us  [on_device(): back = lax.all_to_all(out, 'head', split_axis=0, concat_axis=0, tiled=True)]
    ppermute x14, starting transfers between devices: 20.8 us -> 23.5 us  [shift(): return lax.ppermute(x, 'seq', pairs)]
    ppermute x14, waiting for transfers between devices: 15.8 us -> 13.5 us  [shift(): return lax.ppermute(x, 'seq', pairs)]
    ppermute x1, waiting for transfers between devices: 1.54 us -> 0.01 us  [on_device(): lax.ppermute(jnp.stack([prefix_k[:, 0], prefix_v[:, 0]]), 'seq', to_prompt)]
    pallas_call x3 -> x4, Pallas kernels: 12.6 us -> 12.7 us  [call(): pl.pallas_call(body, out_shape=outs, in_specs=[smem] * scalars + [vmem] *...]
  transfers between devices with their start and end apart: 18 -> 18, of which waited for: 8 -> 7; matrix products, arithmetic and copies ran while one was open for 1% -> 0% of each run, Pallas kernels for 8% -> 10%
where the time goes in v4:
time: 87.3 us; the launch traced here: 86.6 us
  starting transfers between devices  47.7 us (55%)
  waiting for transfers between devices  20.6 us (24%)
  Pallas kernels  15.9 us (18%)
  other arithmetic  0.89 us (1%)
    ppermute x14, starting transfers between devices, shift(): return lax.ppermute(x, 'seq', pairs)  23.5 us
    ppermute x14, waiting for transfers between devices, shift(): return lax.ppermute(x, 'seq', pairs)  13.5 us
    pallas_call x4, Pallas kernels, call(): pl.pallas_call(body, out_shape=outs, in_specs=[smem] * scalars + [vmem] *...  12.7 us
    ppermute x1, starting transfers between devices, on_device(): lax.ppermute(jnp.stack([prefix_k[:, 0], prefix_v[:, 0]]), 'seq', to_prompt)  7.94 us
    all_to_all x1, starting transfers between devices, on_device(): x = lax.all_to_all(packed, 'head', split_axis=0, concat_axis=0, tiled=True)  7.26 us
    all_to_all x1, starting transfers between devices, on_device(): back = lax.all_to_all(out, 'head', split_axis=0, concat_axis=0, tiled=True)  7.05 us
    all_to_all x1, waiting for transfers between devices, on_device(): back = lax.all_to_all(out, 'head', split_axis=0, concat_axis=0, tiled=True)  5.47 us
    pallas_call x1, Pallas kernels, pack(): pl.pallas_call(functools.partial(pack_kernel, heads), out_shape=jax.Shape...  2.19 us
  transfers between devices with their start and end apart: 18, of which 7 were waited for; matrix products, arithmetic and copies ran while one was open for 0% of the time, Pallas kernels for 10%

profile of v4, /device:TPU:24, one launch (start us, length us, event | category | flops | bytes accessed | tf_op | source)
XLA Modules:
  0.0 86.6 jit_solution(14703062019668060951)
XLA Ops:
  0.6 0.9 %pad_maximum_fusion = bf16[2,256,128]{2,1,0:T(8,128)(2,1)S(1)} fusion(bf16[1,256,128]{2,1,0:T(8,128)(2,1)} %bitcast.27, bf16[1,256,128]{2,1,0:T(8,128)(2,1)} %bitcast.28), kind=kLoop, calls=%fused_computation | loop fusion | flops 65536 | bytes 262144 | tf_op jit(solution)/shard_map/stack | solution.py:386
  1.5 7.9 %collective-permute-start = (bf16[2,256,128]{2,1,0:T(8,128)(2,1)S(1)}, bf16[2,256,128]{2,1,0:T(8,128)(2,1)S(1)}, u32[]{:S(2)}, u32[]{:S(2)}) collective-permute-start(bf16[2,256,128]{2,1,0:T(8,128)(2,1)S(1)} %pad_maximum_fusion), channel_id=1, source_target_pairs={{0,0},{8,160},{16,224},{24,192},{32,32},{40,128},{48,64},{56,96},{... | collective-permute-start | bytes 393224 | tf_op jit(solution)/shard_map/ppermute | solution.py:386
  9.5 2.2 %shard_map.118 = bf16[192,1536]{1,0:T(8,128)(2,1)} custom-call(bf16[192,640]{1,0:T(8,128)(2,1)} %bitcast.29, bf16[192,640]{1,0:T(8,128)(2,1)} %bitcast.30, bf16[192,128]{1,0:T(8,128)(2,1)} %bitcast.31, bf16[192,128]{1,0:T(8,128)(2,1)} %bitcast.32), custom_call_target="tpu_custom_call" | custom-call | flops 2000000000 | bytes 1179648 | tf_op jit(solution)/shard_map/pallas_call | solution.py:47
  11.7 7.3 %all-to-all-start = ((bf16[8,24,1536]{2,1,0:T(8,128)(2,1)}), bf16[8,24,1536]{2,1,0:T(8,128)(2,1)S(1)}, u32[]{:S(2)}, u32[]{:S(2)}) async-start(bf16[8,24,1536]{2,1,0:T(8,128)(2,1)} %bitcast.24), calls=%async_computation | async-start | bytes 1179648 | tf_op jit(solution)/shard_map/all_to_all | solution.py:389
  18.9 0.0 copy-start
  18.9 0.0 collective-permute-done.refs_0_
  18.9 0.1 collective-permute-start.1
  19.0 3.2 %collective-permute-start.2 = (bf16[2,256,128]{2,1,0:T(8,128)(2,1)S(1)}, bf16[2,256,128]{2,1,0:T(8,128)(2,1)S(1)}, u32[]{:S(2)}, u32[]{:S(2)}) collective-permute-start(bf16[2,256,128]{2,1,0:T(8,128)(2,1)S(1)} %collective-permute-done.refs_0_), channel_id=1, source_target_pairs={{0,224},{8,40},{16,240},{24,56},{32,0},{40,72},{48,16},{56,88},{64... | collective-permute-start | bytes 393224 | tf_op jit(solution)/shard_map/ppermute | solution.py:384
  22.3 3.5 %collective-permute-done.1.refs_0_ = bf16[2,256,128]{2,1,0:T(8,128)(2,1)S(1)} collective-permute-done((bf16[2,256,128]{2,1,0:T(8,128)(2,1)S(1)}, bf16[2,256,128]{2,1,0:T(8,128)(2,1)S(1)}, u32[]{:S(2)}, u32[]{:S(2)}) %collective-permute-start.1) | collective-permute-done | bytes 131104 | tf_op jit(solution)/shard_map/ppermute | solution.py:384
  25.7 0.0 collective-permute-start.3
  25.7 0.0 collective-permute-done.2.refs_1_
  25.7 3.2 %collective-permute-start.4 = (bf16[2,256,128]{2,1,0:T(8,128)(2,1)S(1)}, bf16[2,256,128]{2,1,0:T(8,128)(2,1)S(1)}, u32[]{:S(2)}, u32[]{:S(2)}) collective-permute-start(bf16[2,256,128]{2,1,0:T(8,128)(2,1)S(1)} %collective-permute-done.2.refs_1_), channel_id=1, source_target_pairs={{0,224},{8,40},{16,240},{24,56},{32,0},{40,72},{48,16},{56,88},{64... | collective-permute-start | bytes 393224 | tf_op jit(solution)/shard_map/ppermute | solution.py:384
  29.0 2.9 %collective-permute-done.3.refs_2_ = bf16[2,256,128]{2,1,0:T(8,128)(2,1)S(1)} collective-permute-done((bf16[2,256,128]{2,1,0:T(8,128)(2,1)S(1)}, bf16[2,256,128]{2,1,0:T(8,128)(2,1)S(1)}, u32[]{:S(2)}, u32[]{:S(2)}) %collective-permute-start.3) | collective-permute-done | bytes 131104 | tf_op jit(solution)/shard_map/ppermute | solution.py:384
  31.9 0.0 collective-permute-start.5
  31.9 0.7 collective-permute-done.4.refs_3_
  32.6 3.7 %collective-permute-start.6 = (bf16[2,256,128]{2,1,0:T(8,128)(2,1)S(1)}, bf16[2,256,128]{2,1,0:T(8,128)(2,1)S(1)}, u32[]{:S(2)}, u32[]{:S(2)}) collective-permute-start(bf16[2,256,128]{2,1,0:T(8,128)(2,1)S(1)} %collective-permute-done.4.refs_3_), channel_id=1, source_target_pairs={{0,224},{8,40},{16,240},{24,56},{32,0},{40,72},{48,16},{56,88},{64... | collective-permute-start | bytes 393224 | tf_op jit(solution)/shard_map/ppermute | solution.py:384
  36.3 1.8 %collective-permute-done.5.refs_4_ = bf16[2,256,128]{2,1,0:T(8,128)(2,1)S(1)} collective-permute-done((bf16[2,256,128]{2,1,0:T(8,128)(2,1)S(1)}, bf16[2,256,128]{2,1,0:T(8,128)(2,1)S(1)}, u32[]{:S(2)}, u32[]{:S(2)}) %collective-permute-start.5) | collective-permute-done | bytes 131104 | tf_op jit(solution)/shard_map/ppermute | solution.py:384
  38.1 0.0 collective-permute-start.7
  38.1 0.0 all-to-all-done
  38.1 0.0 copy-done
  38.1 1.6 %shard_map.119.stats_ref = f32[3,960]{1,0:T(4,128)S(1)} custom-call(s32[32]{0:T(128)S(1)} %copy-done, bf16[192,1536]{1,0:T(8,128)(2,1)S(1)} %bitcast.20, bf16[2,256,128]{2,1,0:T(8,128)(2,1)S(1)} %collective-permute-done.refs_0_), custom_call_target="tpu_custom_call" | custom-call | flops 1724999936 | bytes 732544 | tf_op jit(solution)/shard_map/pallas_call | solution.py:281
  39.7 0.0 collective-permute-done.6.refs_5_
  39.7 4.6 %collective-permute-done.7.refs_6_ = bf16[2,256,128]{2,1,0:T(8,128)(2,1)S(1)} collective-permute-done((bf16[2,256,128]{2,1,0:T(8,128)(2,1)S(1)}, bf16[2,256,128]{2,1,0:T(8,128)(2,1)S(1)}, u32[]{:S(2)}, u32[]{:S(2)}) %collective-permute-start.7) | collective-permute-done | bytes 131104 | tf_op jit(solution)/shard_map/ppermute | solution.py:384
  44.3 7.3 %shard_map.120 = (bf16[2,256,128]{2,1,0:T(8,128)(2,1)S(1)}, bf16[2,256,128]{2,1,0:T(8,128)(2,1)S(1)}, bf16[2,256,128]{2,1,0:T(8,128)(2,1)S(1)}, bf16[2,256,128]{...) custom-call(s32[32]{0:T(128)S(1)} %copy-done, ...), custom_call_target="tpu_custom_call" | custom-call | flops 8739999744 | bytes 3427200 | tf_op jit(solution)/shard_map/pallas_call | solution.py:281
  51.6 0.1 collective-permute-start.8
  51.6 2.0 %collective-permute-start.9 = (bf16[2,256,128]{2,1,0:T(8,128)(2,1)S(1)}, bf16[2,256,128]{2,1,0:T(8,128)(2,1)S(1)}, u32[]{:S(2)}, u32[]{:S(2)}) collective-permute-start(bf16[2,256,128]{2,1,0:T(8,128)(2,1)S(1)} %get-tuple-element.34), channel_id=1, source_target_pairs={{0,32},{8,232},{16,48},{24,248},{32,64},{40,8},{48,80},{56,24},{64... | collective-permute-start | bytes 393224 | tf_op jit(solution)/shard_map/ppermute | solution.py:384
  53.7 0.0 collective-permute-start.10
  53.7 2.9 %collective-permute-start.11 = (bf16[2,256,128]{2,1,0:T(8,128)(2,1)S(1)}, bf16[2,256,128]{2,1,0:T(8,128)(2,1)S(1)}, u32[]{:S(2)}, u32[]{:S(2)}) collective-permute-start(bf16[2,256,128]{2,1,0:T(8,128)(2,1)S(1)} %get-tuple-element.36), channel_id=1, source_target_pairs={{0,64},{8,200},{16,80},{24,216},{32,96},{40,232},{48,112},{56,248}... | collective-permute-start | bytes 393224 | tf_op jit(solution)/shard_map/ppermute | solution.py:384
  56.6 1.0 %collective-permute-start.12 = (bf16[2,256,128]{2,1,0:T(8,128)(2,1)S(1)}, bf16[2,256,128]{2,1,0:T(8,128)(2,1)S(1)}, u32[]{:S(2)}, u32[]{:S(2)}) collective-permute-start(bf16[2,256,128]{2,1,0:T(8,128)(2,1)S(1)} %get-tuple-element.37), channel_id=1, source_target_pairs={{0,160},{8,104},{16,176},{24,120},{32,192},{40,136},{48,208},{56,1... | collective-permute-start | bytes 393224 | tf_op jit(solution)/shard_map/ppermute | solution.py:384
  57.5 0.0 collective-permute-done.8.refs_0_
  57.5 2.9 %collective-permute-start.13 = (bf16[2,256,128]{2,1,0:T(8,128)(2,1)S(1)}, bf16[2,256,128]{2,1,0:T(8,128)(2,1)S(1)}, u32[]{:S(2)}, u32[]{:S(2)}) collective-permute-start(bf16[2,256,128]{2,1,0:T(8,128)(2,1)S(1)} %get-tuple-element.38), channel_id=1, source_target_pairs={{0,96},{8,168},{16,112},{24,184},{32,128},{40,200},{48,144},{56,21... | collective-permute-start | bytes 393224 | tf_op jit(solution)/shard_map/ppermute | solution.py:384
  60.4 0.0 collective-permute-done.9.refs_1_
  60.4 4.4 %collective-permute-start.14 = (bf16[2,256,128]{2,1,0:T(8,128)(2,1)S(1)}, bf16[2,256,128]{2,1,0:T(8,128)(2,1)S(1)}, u32[]{:S(2)}, u32[]{:S(2)}) collective-permute-start(bf16[2,256,128]{2,1,0:T(8,128)(2,1)S(1)} %get-tuple-element.39), channel_id=1, source_target_pairs={{0,128},{8,136},{16,144},{24,152},{32,160},{40,168},{48,176},{56,1... | collective-permute-start | bytes 393224 | tf_op jit(solution)/shard_map/ppermute | solution.py:384
  64.8 3.7 %shard_map.121 = (bf16[192,1536]{1,0:T(8,128)(2,1)}, f32[2,256,128]{2,1,0:T(8,128)S(1)}) custom-call(s32[32]{0:T(128)S(1)} %copy-done, bf16[192,1536]{1,0:T(8,128)(2,1)S(1)} %bitcast.22, f32[2,960]{1,0:T(2,128)S(1)} %get-tuple-element.29.total_ref, f32[128,960]{1,0:T(8,128)S(1)} %get-tuple-element.30.ot_ref, f32[128,960]{1,0:T(8,128)S(1)} %get-tuple-element.31.qt_ref, ...), custom_call_target="tpu_custom_call" | custom-call | flops 4600000000 | bytes 2563712 | tf_op jit(solution)/shard_map/pallas_call | solution.py:281
  68.5 7.0 %all-to-all-start.1 = ((bf16[8,24,1536]{2,1,0:T(8,128)(2,1)}), bf16[8,24,1536]{2,1,0:T(8,128)(2,1)S(1)}, u32[]{:S(2)}, u32[]{:S(2)}) async-start(bf16[8,24,1536]{2,1,0:T(8,128)(2,1)} %bitcast.8), calls=%async_computation.1 | async-start | bytes 1179648 | tf_op jit(solution)/shard_map/all_to_all | solution.py:409
  75.6 0.0 collective-permute-done.10.refs_2_
  75.6 0.0 collective-permute-done.11.refs_3_
  75.6 0.0 collective-permute-done.12.refs_4_
  75.6 0.0 collective-permute-done.13.refs_5_
  75.6 0.0 collective-permute-done.14.refs_6_
  75.6 0.1 shard_map.122
  75.8 1.9 %collective-permute-start.15 = (bf16[2,256,128]{2,1,0:T(8,128)(2,1)S(1)}, bf16[2,256,128]{2,1,0:T(8,128)(2,1)S(1)}, u32[]{:S(2)}, u32[]{:S(2)}) collective-permute-start(bf16[2,256,128]{2,1,0:T(8,128)(2,1)S(1)} %shard_map.122), channel_id=1, source_target_pairs={{0,0},{160,8},{224,16},{192,24},{32,32},{128,40},{64,48},{96,56},{... | collective-permute-start | bytes 393224 | tf_op jit(solution)/shard_map/ppermute | solution.py:411
  77.7 5.5 %all-to-all-done.1 = bf16[8,24,1536]{2,1,0:T(8,128)(2,1)S(1)} async-done(((bf16[8,24,1536]{2,1,0:T(8,128)(2,1)}), bf16[8,24,1536]{2,1,0:T(8,128)(2,1)S(1)}, u32[]{:S(2)}, u32[]{:S(2)}) %all-to-all-start.1) | async-done | bytes 589856 | tf_op jit(solution)/shard_map/all_to_all | solution.py:409
  83.2 1.0 %shard_map.123 = (bf16[192,640]{1,0:T(8,128)(2,1)}, bf16[192,640]{1,0:T(8,128)(2,1)}, bf16[192,128]{1,0:T(8,128)(2,1)}, bf16[192,128]{1,0:T(8,128)(2,1)}) custom-call(bf16[192,1536]{1,0:T(8,128)(2,1)S(1)} %bitcast.23), custom_call_target="tpu_custom_call" | custom-call | flops 1000000000 | bytes 1179648 | tf_op jit(solution)/shard_map/pallas_call | solution.py:87
  84.1 1.7 %collective-permute-done.15 = bf16[2,256,128]{2,1,0:T(8,128)(2,1)S(1)} collective-permute-done((bf16[2,256,128]{2,1,0:T(8,128)(2,1)S(1)}, bf16[2,256,128]{2,1,0:T(8,128)(2,1)S(1)}, u32[]{:S(2)}, u32[]{:S(2)}) %collective-permute-start.15) | collective-permute-done | bytes 131104 | tf_op jit(solution)/shard_map/ppermute | solution.py:411
  85.8 0.7 fusion
Async XLA Ops:
  1.5 17.4 %collective-permute-start = (bf16[2,256,128]{2,1,0:T(8,128)(2,1)S(1)}, bf16[2,256,128]{2,1,0:T(8,128)(2,1)S(1)}, u32[]{:S(2)}, u32[]{:S(2)}) collective-permute-start(bf16[2,256,128]{2,1,0:T(8,128)(2,1)S(1)} %pad_maximum_fusion), channel_id=1, source_target_pairs={{0,0},{8,160},{16,224},{24,192},{32,32},{40,128},{48,64},{56,96},{... | collective-permute-start | bytes 393224 | tf_op jit(solution)/shard_map/ppermute | solution.py:386
  11.7 26.4 %all-to-all-start = ((bf16[8,24,1536]{2,1,0:T(8,128)(2,1)}), bf16[8,24,1536]{2,1,0:T(8,128)(2,1)S(1)}, u32[]{:S(2)}, u32[]{:S(2)}) async-start(bf16[8,24,1536]{2,1,0:T(8,128)(2,1)} %bitcast.24), calls=%async_computation | async-start | bytes 1179648 | tf_op jit(solution)/shard_map/all_to_all | solution.py:389
  18.9 19.2 %copy-start = (s32[32]{0:T(128)S(1)}, s32[32]{0:T(128)}, u32[]{:S(2)}) copy-start(s32[32]{0:T(128)} %len_ref.5) | copy-start | bytes 388
  18.9 6.8 %collective-permute-start.1 = (bf16[2,256,128]{2,1,0:T(8,128)(2,1)S(1)}, bf16[2,256,128]{2,1,0:T(8,128)(2,1)S(1)}, u32[]{:S(2)}, u32[]{:S(2)}) collective-permute-start(bf16[2,256,128]{2,1,0:T(8,128)(2,1)S(1)} %collective-permute-done.refs_0_), channel_id=1, source_target_pairs={{0,32},{8,232},{16,48},{24,248},{32,64},{40,8},{48,80},{56,24},{64... | collective-permute-start | bytes 393224 | tf_op jit(solution)/shard_map/ppermute | solution.py:384
  19.0 6.7 %collective-permute-start.2 = (bf16[2,256,128]{2,1,0:T(8,128)(2,1)S(1)}, bf16[2,256,128]{2,1,0:T(8,128)(2,1)S(1)}, u32[]{:S(2)}, u32[]{:S(2)}) collective-permute-start(bf16[2,256,128]{2,1,0:T(8,128)(2,1)S(1)} %collective-permute-done.refs_0_), channel_id=1, source_target_pairs={{0,224},{8,40},{16,240},{24,56},{32,0},{40,72},{48,16},{56,88},{64... | collective-permute-start | bytes 393224 | tf_op jit(solution)/shard_map/ppermute | solution.py:384
  25.7 6.2 %collective-permute-start.3 = (bf16[2,256,128]{2,1,0:T(8,128)(2,1)S(1)}, bf16[2,256,128]{2,1,0:T(8,128)(2,1)S(1)}, u32[]{:S(2)}, u32[]{:S(2)}) collective-permute-start(bf16[2,256,128]{2,1,0:T(8,128)(2,1)S(1)} %collective-permute-done.1.refs_0_), channel_id=1, source_target_pairs={{0,32},{8,232},{16,48},{24,248},{32,64},{40,8},{48,80},{56,24},{64... | collective-permute-start | bytes 393224 | tf_op jit(solution)/shard_map/ppermute | solution.py:384
  25.7 6.9 %collective-permute-start.4 = (bf16[2,256,128]{2,1,0:T(8,128)(2,1)S(1)}, bf16[2,256,128]{2,1,0:T(8,128)(2,1)S(1)}, u32[]{:S(2)}, u32[]{:S(2)}) collective-permute-start(bf16[2,256,128]{2,1,0:T(8,128)(2,1)S(1)} %collective-permute-done.2.refs_1_), channel_id=1, source_target_pairs={{0,224},{8,40},{16,240},{24,56},{32,0},{40,72},{48,16},{56,88},{64... | collective-permute-start | bytes 393224 | tf_op jit(solution)/shard_map/ppermute | solution.py:384
  31.9 6.2 %collective-permute-start.5 = (bf16[2,256,128]{2,1,0:T(8,128)(2,1)S(1)}, bf16[2,256,128]{2,1,0:T(8,128)(2,1)S(1)}, u32[]{:S(2)}, u32[]{:S(2)}) collective-permute-start(bf16[2,256,128]{2,1,0:T(8,128)(2,1)S(1)} %collective-permute-done.3.refs_2_), channel_id=1, source_target_pairs={{0,32},{8,232},{16,48},{24,248},{32,64},{40,8},{48,80},{56,24},{64... | collective-permute-start | bytes 393224 | tf_op jit(solution)/shard_map/ppermute | solution.py:384
  32.6 7.1 %collective-permute-start.6 = (bf16[2,256,128]{2,1,0:T(8,128)(2,1)S(1)}, bf16[2,256,128]{2,1,0:T(8,128)(2,1)S(1)}, u32[]{:S(2)}, u32[]{:S(2)}) collective-permute-start(bf16[2,256,128]{2,1,0:T(8,128)(2,1)S(1)} %collective-permute-done.4.refs_3_), channel_id=1, source_target_pairs={{0,224},{8,40},{16,240},{24,56},{32,0},{40,72},{48,16},{56,88},{64... | collective-permute-start | bytes 393224 | tf_op jit(solution)/shard_map/ppermute | solution.py:384
  38.1 6.2 %collective-permute-start.7 = (bf16[2,256,128]{2,1,0:T(8,128)(2,1)S(1)}, bf16[2,256,128]{2,1,0:T(8,128)(2,1)S(1)}, u32[]{:S(2)}, u32[]{:S(2)}) collective-permute-start(bf16[2,256,128]{2,1,0:T(8,128)(2,1)S(1)} %collective-permute-done.5.refs_4_), channel_id=1, source_target_pairs={{0,32},{8,232},{16,48},{24,248},{32,64},{40,8},{48,80},{56,24},{64... | collective-permute-start | bytes 393224 | tf_op jit(solution)/shard_map/ppermute | solution.py:384
  51.6 6.0 %collective-permute-start.8 = (bf16[2,256,128]{2,1,0:T(8,128)(2,1)S(1)}, bf16[2,256,128]{2,1,0:T(8,128)(2,1)S(1)}, u32[]{:S(2)}, u32[]{:S(2)}) collective-permute-start(bf16[2,256,128]{2,1,0:T(8,128)(2,1)S(1)} %get-tuple-element.33), channel_id=1, source_target_pairs={{0,224},{8,40},{16,240},{24,56},{32,0},{40,72},{48,16},{56,88},{64... | collective-permute-start | bytes 393224 | tf_op jit(solution)/shard_map/ppermute | solution.py:384
  51.6 8.8 %collective-permute-start.9 = (bf16[2,256,128]{2,1,0:T(8,128)(2,1)S(1)}, bf16[2,256,128]{2,1,0:T(8,128)(2,1)S(1)}, u32[]{:S(2)}, u32[]{:S(2)}) collective-permute-start(bf16[2,256,128]{2,1,0:T(8,128)(2,1)S(1)} %get-tuple-element.34), channel_id=1, source_target_pairs={{0,32},{8,232},{16,48},{24,248},{32,64},{40,8},{48,80},{56,24},{64... | collective-permute-start | bytes 393224 | tf_op jit(solution)/shard_map/ppermute | solution.py:384
  53.7 21.9 %collective-permute-start.10 = (bf16[2,256,128]{2,1,0:T(8,128)(2,1)S(1)}, bf16[2,256,128]{2,1,0:T(8,128)(2,1)S(1)}, u32[]{:S(2)}, u32[]{:S(2)}) collective-permute-start(bf16[2,256,128]{2,1,0:T(8,128)(2,1)S(1)} %get-tuple-element.35), channel_id=1, source_target_pairs={{0,192},{8,72},{16,208},{24,88},{32,224},{40,104},{48,240},{56,120... | collective-permute-start | bytes 393224 | tf_op jit(solution)/shard_map/ppermute | solution.py:384
  53.7 21.9 %collective-permute-start.11 = (bf16[2,256,128]{2,1,0:T(8,128)(2,1)S(1)}, bf16[2,256,128]{2,1,0:T(8,128)(2,1)S(1)}, u32[]{:S(2)}, u32[]{:S(2)}) collective-permute-start(bf16[2,256,128]{2,1,0:T(8,128)(2,1)S(1)} %get-tuple-element.36), channel_id=1, source_target_pairs={{0,64},{8,200},{16,80},{24,216},{32,96},{40,232},{48,112},{56,248}... | collective-permute-start | bytes 393224 | tf_op jit(solution)/shard_map/ppermute | solution.py:384
  56.6 19.0 %collective-permute-start.12 = (bf16[2,256,128]{2,1,0:T(8,128)(2,1)S(1)}, bf16[2,256,128]{2,1,0:T(8,128)(2,1)S(1)}, u32[]{:S(2)}, u32[]{:S(2)}) collective-permute-start(bf16[2,256,128]{2,1,0:T(8,128)(2,1)S(1)} %get-tuple-element.37), channel_id=1, source_target_pairs={{0,160},{8,104},{16,176},{24,120},{32,192},{40,136},{48,208},{56,1... | collective-permute-start | bytes 393224 | tf_op jit(solution)/shard_map/ppermute | solution.py:384
  57.5 18.1 %collective-permute-start.13 = (bf16[2,256,128]{2,1,0:T(8,128)(2,1)S(1)}, bf16[2,256,128]{2,1,0:T(8,128)(2,1)S(1)}, u32[]{:S(2)}, u32[]{:S(2)}) collective-permute-start(bf16[2,256,128]{2,1,0:T(8,128)(2,1)S(1)} %get-tuple-element.38), channel_id=1, source_target_pairs={{0,96},{8,168},{16,112},{24,184},{32,128},{40,200},{48,144},{56,21... | collective-permute-start | bytes 393224 | tf_op jit(solution)/shard_map/ppermute | solution.py:384
  60.4 15.2 %collective-permute-start.14 = (bf16[2,256,128]{2,1,0:T(8,128)(2,1)S(1)}, bf16[2,256,128]{2,1,0:T(8,128)(2,1)S(1)}, u32[]{:S(2)}, u32[]{:S(2)}) collective-permute-start(bf16[2,256,128]{2,1,0:T(8,128)(2,1)S(1)} %get-tuple-element.39), channel_id=1, source_target_pairs={{0,128},{8,136},{16,144},{24,152},{32,160},{40,168},{48,176},{56,1... | collective-permute-start | bytes 393224 | tf_op jit(solution)/shard_map/ppermute | solution.py:384
  68.5 14.6 %all-to-all-start.1 = ((bf16[8,24,1536]{2,1,0:T(8,128)(2,1)}), bf16[8,24,1536]{2,1,0:T(8,128)(2,1)S(1)}, u32[]{:S(2)}, u32[]{:S(2)}) async-start(bf16[8,24,1536]{2,1,0:T(8,128)(2,1)} %bitcast.8), calls=%async_computation.1 | async-start | bytes 1179648 | tf_op jit(solution)/shard_map/all_to_all | solution.py:409
  75.8 10.1 %collective-permute-start.15 = (bf16[2,256,128]{2,1,0:T(8,128)(2,1)S(1)}, bf16[2,256,128]{2,1,0:T(8,128)(2,1)S(1)}, u32[]{:S(2)}, u32[]{:S(2)}) collective-permute-start(bf16[2,256,128]{2,1,0:T(8,128)(2,1)S(1)} %shard_map.122), channel_id=1, source_target_pairs={{0,0},{160,8},{224,16},{192,24},{32,32},{128,40},{64,48},{96,56},{... | collective-permute-start | bytes 393224 | tf_op jit(solution)/shard_map/ppermute | solution.py:411

commit v5 on v4

--- a/solution.py
+++ b/solution.py
@@ -163,13 +163,14 @@
 
 
 def far_kernel(group, chunks, scale, len_ref, x_ref, stats_ref, *refs):
-    shard_refs, grad_refs = refs[:chunks], refs[chunks:2 * chunks]
-    k_refs, v_refs = [[r.at[i] for r in shard_refs] for i in range(2)]
-    dk_refs, dv_refs = [[r.at[i] for r in grad_refs] for i in range(2)]
+    pairs = chunks // 2
+    shard_refs, grad_refs = refs[:pairs], refs[pairs:2 * pairs]
+    k_refs, v_refs = [[r.at[j, i] for r in shard_refs for j in range(2)] for i in range(2)]
+    dk_refs, dv_refs = [[r.at[j, i] for r in grad_refs for j in range(2)] for i in range(2)]
     (total_ref, ot_ref, qt_ref,
-     q_s, g_s, keys_t, values_t, e_s, d_s, pb_s, sb_s, dk_s, dv_s) = refs[2 * chunks:]
+     q_s, g_s, keys_t, values_t, e_s, d_s, pb_s, sb_s, dk_s, dv_s) = refs[2 * pairs:]
     cap = x_ref.shape[0]
-    span, head_dim = shard_refs[0].shape[1:]
+    span, head_dim = shard_refs[0].shape[2:]
     length = len_ref[lax.axis_index("seq")]
     turn = scale * math.log2(math.e)
     stack_rows(x_ref, q_s, g_s, group)
@@ -299,7 +300,7 @@
     rows = group * cap
     return call(
         functools.partial(near_stats_kernel, group, len(shards), scale),
-        1.5,
+        2,
         [lengths, x, *shards],
         [jax.ShapeDtypeStruct((3, rows), f32)],
         [VMEM((rows, head_dim), bf16)] * 2,
@@ -309,12 +310,12 @@
 
 def far_pass(lengths, x, stats, shards, group, scale):
     cap = x.shape[0]
-    _, span, head_dim = shards[0].shape
-    chunks = len(shards)
+    span, head_dim = shards[0].shape[2:]
+    chunks = 2 * len(shards)
     rows, keys = group * cap, chunks * span
     outs = call(
         functools.partial(far_kernel, group, chunks, scale),
-        7.6,
+        6.5,
         [lengths, x, stats, *shards],
         [jax.ShapeDtypeStruct(shard.shape, bf16) for shard in shards]
         + [jax.ShapeDtypeStruct((2, rows), f32)]
@@ -326,7 +327,7 @@
         + [VMEM((keys, head_dim), f32)] * 2,
         24,
     )
-    return outs[:chunks], outs[chunks:]
+    return outs[:len(shards)], outs[len(shards):]
 
 
 def near_pass(lengths, x, totals, shards, group, scale):
@@ -335,7 +336,7 @@
     rows, keys = group * cap, len(shards) * span + cap
     outs = call(
         functools.partial(near_kernel, group, len(shards), scale),
-        4,
+        5,
         [lengths, x, *totals, *shards],
         [jax.ShapeDtypeStruct((cap, packed), bf16)]
         + [jax.ShapeDtypeStruct(shard.shape, f32) for shard in shards],
@@ -349,17 +350,19 @@
     return outs[0], outs[1:]
 
 
-def sum_kernel(own_ref, *refs):
-    total = own_ref[...]
-    for ref in refs[:-1]:
-        total = total + ref[...].astype(f32)
-    refs[-1][...] = total.astype(bf16)
-
-
-def add_parts(own, parts):
+def sum_kernel(count, *refs):
+    for i in range(count):
+        total = refs[i][...]
+        for ref in refs[count:-count]:
+            total = total + ref[i].astype(f32)
+        refs[i - count][...] = total.astype(bf16)
+
+
+def add_parts(held, parts):
     return call(
-        sum_kernel, 12, [own, *parts], [jax.ShapeDtypeStruct(own.shape, bf16)], [], 8, scalars=0
-    )[0]
+        functools.partial(sum_kernel, len(held)), 12, [*held, *parts],
+        [jax.ShapeDtypeStruct(part.shape, bf16) for part in held], [], 8, scalars=0,
+    )
 
 
 def on_device(comp_q, comp_k, comp_v, comp_grad, prefix_k, prefix_v, comp_len):
@@ -370,49 +373,48 @@
     ring = devices // PROMPTS
     scale = 1.0 / math.sqrt(head_dim)
 
-    to_prompt = []
+    holders = []
     for owner in range(devices):
         plane, lane = divmod(owner, PROMPTS)
         reach = (0, 3, 1, 2)[lane]
-        target = (plane + reach if plane % 2 else plane - reach) % ring
-        to_prompt.append((owner, target * PROMPTS + owner // ring))
-    to_owner = [(b, a) for a, b in to_prompt]
+        holders.append((plane + reach if plane % 2 else plane - reach) % ring)
+
+    def spread(steps):
+        return [
+            (owner, (holder + steps) % ring * PROMPTS + owner // ring)
+            for owner, holder in enumerate(holders)
+        ]
+
+    def collect(x, steps):
+        return lax.ppermute(x, "seq", [(b, a) for a, b in spread(steps)])
 
     def shift(x, steps):
         way = (PROMPTS * steps, -PROMPTS * steps)
         pairs = [(s, (s + way[s % 2]) % devices) for s in range(devices)]
         return lax.ppermute(x, "seq", pairs)
 
-    own = lax.ppermute(jnp.stack([prefix_k[:, 0], prefix_v[:, 0]]), "seq", to_prompt)
+    half = ring // 2
+    prefix = jnp.stack([prefix_k[:, 0], prefix_v[:, 0]])
+    own, across = [lax.ppermute(prefix, "seq", spread(steps)) for steps in (0, half)]
     packed = pack(comp_q, comp_grad, comp_k, comp_v)
-    own, _ = lax.optimization_barrier((own, packed))
+    own, across, _ = lax.optimization_barrier((own, across, packed))
     x = lax.all_to_all(packed, "head", split_axis=0, concat_axis=0, tiled=True)
 
-    up, down = [own], [own]
-    for step in range(1, ring // 2 + 1):
-        up.append(shift(up[-1], 1))
-        if step < ring - step:
-            down.append(shift(down[-1], -1))
-
-    far, steps = [], []
-    for step in range(1, ring // 2 + 1):
-        far.append(up[step])
-        steps.append(-step)
-        if step < ring - step:
-            far.append(down[step])
-            steps.append(step)
-    stats = near_stats(comp_len, x, [own], group, scale)
+    held, steps = [own, across], (1, -1, 2)
+    both = jnp.stack(held)
+    far = [shift(both, step) for step in steps]
+    stats = near_stats(comp_len, x, held, group, scale)
     grads, totals = far_pass(comp_len, x, stats, far, group, scale)
-    moved = [shift(grad, step) for grad, step in zip(grads, steps)]
-    out, (own_grad,) = near_pass(comp_len, x, totals, [own], group, scale)
-    summed = add_parts(own_grad, moved)
+    moved = [shift(grad, -step) for grad, step in zip(grads, steps)]
+    out, held_grads = near_pass(comp_len, x, totals, held, group, scale)
+    own, across = add_parts(held_grads, moved)
     back = lax.all_to_all(out, "head", split_axis=0, concat_axis=0, tiled=True)
     attn_out, grad_q, grad_k, grad_v = unpack(back, heads, width, head_dim)
-    placed = lax.ppermute(summed, "seq", to_owner)
-    placed, (attn_out, grad_q, grad_k, grad_v) = lax.optimization_barrier(
-        (placed, (attn_out, grad_q, grad_k, grad_v))
-    )
-    placed = placed.astype(f32)
+    own, across = collect(own, 0), collect(across, half)
+    own, across, (attn_out, grad_q, grad_k, grad_v) = lax.optimization_barrier(
+        (own, across, (attn_out, grad_q, grad_k, grad_v))
+    )
+    placed = [own[i].astype(f32) + across[i].astype(f32) for i in range(2)]
     return (attn_out, grad_q, grad_k, grad_v, placed[0][:, None], placed[1][:, None])
 
 

time: 87.3 us -> 81.5 us (0.934)
  starting transfers between devices: 47.7 us -> 37.3 us
  waiting for transfers between devices: 20.6 us -> 24.9 us
    ppermute x14 -> x6, starting transfers between devices: 23.5 us -> 7.72 us  [shift(): return lax.ppermute(x, 'seq', pairs)]
    ppermute x2 -> x4, waiting for transfers between devices: 1.7 us -> 14.3 us  [the longest x2 8 us: collect(): return lax.ppermute(x, 'seq', [(b, a) for a, b in spread(steps)])]
    ppermute x2 -> x4, starting transfers between devices: 9.87 us -> 15.6 us  [the longest x2 9.06 us: on_device(): lax.ppermute(prefix, 'seq', spread(steps))]
    ppermute x14 -> x6, waiting for transfers between devices: 13.5 us -> 8.75 us  [shift(): return lax.ppermute(x, 'seq', pairs)]
    all_to_all x1, waiting for transfers between devices: 5.47 us -> 1.77 us  [on_device(): back = lax.all_to_all(out, 'head', split_axis=0, concat_axis=0, tiled=True)]
  transfers between devices with their start and end apart: 18 -> 12, of which waited for: 7 -> 7; matrix products, arithmetic and copies ran while one was open for 0% -> 0% of each run, Pallas kernels for 10% -> 10%
where the time goes in v5:
time: 81.5 us; the launch traced here: 80.1 us
  starting transfers between devices  37.3 us (46%)
  waiting for transfers between devices  24.9 us (31%)
  Pallas kernels  16.4 us (20%)
    pallas_call x4, Pallas kernels, call(): pl.pallas_call(body, out_shape=outs, in_specs=[smem] * scalars + [vmem] *...  13.3 us
    ppermute x2, starting transfers between devices, on_device(): lax.ppermute(prefix, 'seq', spread(steps))  9.06 us
    ppermute x6, waiting for transfers between devices, shift(): return lax.ppermute(x, 'seq', pairs)  8.75 us
    ppermute x2, waiting for transfers between devices, collect(): return lax.ppermute(x, 'seq', [(b, a) for a, b in spread(steps)])  8 us
    ppermute x6, starting transfers between devices, shift(): return lax.ppermute(x, 'seq', pairs)  7.72 us
    all_to_all x1, starting transfers between devices, on_device(): x = lax.all_to_all(packed, 'head', split_axis=0, concat_axis=0, tiled=True)  7.39 us
    all_to_all x1, starting transfers between devices, on_device(): back = lax.all_to_all(out, 'head', split_axis=0, concat_axis=0, tiled=True)  6.58 us
    ppermute x2, starting transfers between devices, collect(): return lax.ppermute(x, 'seq', [(b, a) for a, b in spread(steps)])  6.56 us
  transfers between devices with their start and end apart: 12, of which 7 were waited for; matrix products, arithmetic and copies ran while one was open for 0% of the time, Pallas kernels for 10%

profile of v5, /device:TPU:24, one launch (start us, length us, event | category | flops | bytes accessed | tf_op | source)
XLA Modules:
  0.0 80.1 jit_solution(3245074267509497513)
XLA Ops:
  0.6 2.2 %shard_map.118 = bf16[192,1536]{1,0:T(8,128)(2,1)} custom-call(bf16[192,640]{1,0:T(8,128)(2,1)} %bitcast.33, bf16[192,640]{1,0:T(8,128)(2,1)} %bitcast.34, bf16[192,128]{1,0:T(8,128)(2,1)} %bitcast.35, bf16[192,128]{1,0:T(8,128)(2,1)} %bitcast.36), custom_call_target="tpu_custom_call" | custom-call | flops 2000000000 | bytes 1179648 | tf_op jit(solution)/shard_map/pallas_call | solution.py:47
  2.8 0.0 copy-start.1
  2.8 0.0 copy-start.2
  2.8 7.4 %all-to-all-start = ((bf16[8,24,1536]{2,1,0:T(8,128)(2,1)}), bf16[8,24,1536]{2,1,0:T(8,128)(2,1)S(1)}, u32[]{:S(2)}, u32[]{:S(2)}) async-start(bf16[8,24,1536]{2,1,0:T(8,128)(2,1)} %bitcast.28), calls=%async_computation | async-start | bytes 1179648 | tf_op jit(solution)/shard_map/all_to_all | solution.py:401
  10.2 0.0 copy-done.1
  10.2 0.0 copy-done.2
  10.3 4.9 %collective-permute-start.1 = (bf16[2,256,128]{2,1,0:T(8,128)(2,1)S(1)}, bf16[2,256,128]{2,1,0:T(8,128)(2,1)S(1)}, u32[]{:S(2)}, u32[]{:S(2)}) collective-permute-start(bf16[2,256,128]{2,1,0:T(8,128)(2,1)S(1)} %pad_maximum_fusion.1), channel_id=1, source_target_pairs={{0,128},{8,32},{16,96},{24,64},{32,160},{40,0},{48,192},{56,224},{... | collective-permute-start | bytes 393224 | tf_op jit(solution)/shard_map/ppermute | solution.py:398
  15.1 4.2 %collective-permute-start = (bf16[2,256,128]{2,1,0:T(8,128)(2,1)S(1)}, bf16[2,256,128]{2,1,0:T(8,128)(2,1)S(1)}, u32[]{:S(2)}, u32[]{:S(2)}) collective-permute-start(bf16[2,256,128]{2,1,0:T(8,128)(2,1)S(1)} %pad_maximum_fusion.1), channel_id=1, source_target_pairs={{0,0},{8,160},{16,224},{24,192},{32,32},{40,128},{48,64},{56,96},{... | collective-permute-start | bytes 393224 | tf_op jit(solution)/shard_map/ppermute | solution.py:398
  19.3 1.8 %collective-permute-done.1.refs_1_ = bf16[2,256,128]{2,1,0:T(8,128)(2,1)S(1)} collective-permute-done((bf16[2,256,128]{2,1,0:T(8,128)(2,1)S(1)}, bf16[2,256,128]{2,1,0:T(8,128)(2,1)S(1)}, u32[]{:S(2)}, u32[]{:S(2)}) %collective-permute-start.1) | collective-permute-done | bytes 131104 | tf_op jit(solution)/shard_map/ppermute | solution.py:398
  21.1 4.5 %collective-permute-done.refs_0_ = bf16[2,256,128]{2,1,0:T(8,128)(2,1)S(1)} collective-permute-done((bf16[2,256,128]{2,1,0:T(8,128)(2,1)S(1)}, bf16[2,256,128]{2,1,0:T(8,128)(2,1)S(1)}, u32[]{:S(2)}, u32[]{:S(2)}) %collective-permute-start) | collective-permute-done | bytes 131104 | tf_op jit(solution)/shard_map/ppermute | solution.py:398
  25.7 0.0 copy-start
  25.7 1.3 %collective-permute-start.4 = (bf16[2,2,256,128]{3,2,1,0:T(8,128)(2,1)S(1)}, bf16[2,2,256,128]{3,2,1,0:T(8,128)(2,1)S(1)}, u32[]{:S(2)}, u32[]{:S(2)}) collective-permute-start(bf16[2,2,256,128]{3,2,1,0:T(8,128)(2,1)S(1)} %pad_maximum_fusion), channel_id=1, source_target_pairs={{0,64},{8,200},{16,80},{24,216},{32,96},{40,232},{48,112},{56,248}... | collective-permute-start | bytes 786440 | tf_op jit(solution)/shard_map/ppermute | solution.py:394
  27.0 4.3 %collective-permute-start.3 = (bf16[2,2,256,128]{3,2,1,0:T(8,128)(2,1)S(1)}, bf16[2,2,256,128]{3,2,1,0:T(8,128)(2,1)S(1)}, u32[]{:S(2)}, u32[]{:S(2)}) collective-permute-start(bf16[2,2,256,128]{3,2,1,0:T(8,128)(2,1)S(1)} %pad_maximum_fusion), channel_id=1, source_target_pairs={{0,224},{8,40},{16,240},{24,56},{32,0},{40,72},{48,16},{56,88},{64... | collective-permute-start | bytes 786440 | tf_op jit(solution)/shard_map/ppermute | solution.py:394
  31.3 0.0 collective-permute-start.2
  31.3 0.0 all-to-all-done
  31.3 0.0 copy-done
  31.3 2.0 %shard_map.119.stats_ref = f32[3,960]{1,0:T(4,128)S(1)} custom-call(s32[32]{0:T(128)S(1)} %copy-done, bf16[192,1536]{1,0:T(8,128)(2,1)S(1)} %bitcast.22, bf16[2,256,128]{2,1,0:T(8,128)(2,1)S(1)} %collective-permute-done.refs_0_, bf16[2,256,128]{2,1,0:T(8,128)(2,1)S(1)} %collective-permute-done.1.refs_1_), custom_call_target="tpu_custom_call" | custom-call | flops 2300000000 | bytes 863616 | tf_op jit(solution)/shard_map/pallas_call | solution.py:282
  33.3 2.9 %collective-permute-done.4.refs_2_ = bf16[2,2,256,128]{3,2,1,0:T(8,128)(2,1)S(1)} collective-permute-done((bf16[2,2,256,128]{3,2,1,0:T(8,128)(2,1)S(1)}, bf16[2,2,256,128]{3,2,1,0:T(8,128)(2,1)S(1)}, u32[]{:S(2)}, u32[]{:S(2)}) %collective-permute-start.4) | collective-permute-done | bytes 262176 | tf_op jit(solution)/shard_map/ppermute | solution.py:394
  36.2 2.8 %collective-permute-done.3.refs_1_ = bf16[2,2,256,128]{3,2,1,0:T(8,128)(2,1)S(1)} collective-permute-done((bf16[2,2,256,128]{3,2,1,0:T(8,128)(2,1)S(1)}, bf16[2,2,256,128]{3,2,1,0:T(8,128)(2,1)S(1)}, u32[]{:S(2)}, u32[]{:S(2)}) %collective-permute-start.3) | collective-permute-done | bytes 262176 | tf_op jit(solution)/shard_map/ppermute | solution.py:394
  39.0 3.1 %collective-permute-done.2.refs_0_ = bf16[2,2,256,128]{3,2,1,0:T(8,128)(2,1)S(1)} collective-permute-done((bf16[2,2,256,128]{3,2,1,0:T(8,128)(2,1)S(1)}, bf16[2,2,256,128]{3,2,1,0:T(8,128)(2,1)S(1)}, u32[]{:S(2)}, u32[]{:S(2)}) %collective-permute-start.2) | collective-permute-done | bytes 262176 | tf_op jit(solution)/shard_map/ppermute | solution.py:394
  42.1 6.4 %shard_map.120 = (bf16[2,2,256,128]{3,2,1,0:T(8,128)(2,1)S(1)}, bf16[2,2,256,128]{3,2,1,0:T(8,128)(2,1)S(1)}, bf16[2,2,256,128]{3,2,1,0:T(8,128)(2,1)S(1)}, f32[...) custom-call(s32[32]{0:T(128)S(1)} %copy-done, bf16[192,1536]{1,0:T(8,128)(2,1)S(1)} %bitcast.23, ...), custom_call_target="tpu_custom_call" | custom-call | flops 7474999808 | bytes 3165056 | tf_op jit(solution)/shard_map/pallas_call | solution.py:282
  48.5 0.1 collective-permute-start.5
  48.6 2.0 %collective-permute-start.6 = (bf16[2,2,256,128]{3,2,1,0:T(8,128)(2,1)S(1)}, bf16[2,2,256,128]{3,2,1,0:T(8,128)(2,1)S(1)}, u32[]{:S(2)}, u32[]{:S(2)}) collective-permute-start(bf16[2,2,256,128]{3,2,1,0:T(8,128)(2,1)S(1)} %get-tuple-element.37), channel_id=1, source_target_pairs={{0,32},{8,232},{16,48},{24,248},{32,64},{40,8},{48,80},{56,24},{64... | collective-permute-start | bytes 786440 | tf_op jit(solution)/shard_map/ppermute | solution.py:394
  50.6 0.0 collective-permute-start.7
  50.6 4.7 %shard_map.121 = (bf16[192,1536]{1,0:T(8,128)(2,1)}, f32[2,256,128]{2,1,0:T(8,128)S(1)}, f32[2,256,128]{2,1,0:T(8,128)S(1)}) custom-call(s32[32]{0:T(128)S(1)} %copy-done, bf16[192,1536]{1,0:T(8,128)(2,1)S(1)} %bitcast.24, f32[2,960]{1,0:T(2,128)S(1)} %get-tuple-element.31.total_ref, f32[128,960]{1,0:T(8,128)S(1)} %get-tuple-element.32.ot_ref, ...), custom_call_target="tpu_custom_call" | custom-call | flops 5750000128 | bytes 2956928 | tf_op jit(solution)/shard_map/pallas_call | solution.py:282
  55.3 6.6 %all-to-all-start.1 = ((bf16[8,24,1536]{2,1,0:T(8,128)(2,1)}), bf16[8,24,1536]{2,1,0:T(8,128)(2,1)S(1)}, u32[]{:S(2)}, u32[]{:S(2)}) async-start(bf16[8,24,1536]{2,1,0:T(8,128)(2,1)} %bitcast.10), calls=%async_computation.1 | async-start | bytes 1179648 | tf_op jit(solution)/shard_map/all_to_all | solution.py:411
  61.9 0.0 collective-permute-done.5.refs_2_
  61.9 0.0 collective-permute-done.6.refs_3_
  61.9 0.0 collective-permute-done.7.refs_4_
  61.9 0.1 shard_map.122
  62.1 4.5 %collective-permute-start.8 = (bf16[2,256,128]{2,1,0:T(8,128)(2,1)S(1)}, bf16[2,256,128]{2,1,0:T(8,128)(2,1)S(1)}, u32[]{:S(2)}, u32[]{:S(2)}) collective-permute-start(bf16[2,256,128]{2,1,0:T(8,128)(2,1)S(1)} %get-tuple-element.39), channel_id=1, source_target_pairs={{0,0},{160,8},{224,16},{192,24},{32,32},{128,40},{64,48},{96,56},{... | collective-permute-start | bytes 393224 | tf_op jit(solution)/shard_map/ppermute | solution.py:389
  66.6 2.1 %collective-permute-start.9 = (bf16[2,256,128]{2,1,0:T(8,128)(2,1)S(1)}, bf16[2,256,128]{2,1,0:T(8,128)(2,1)S(1)}, u32[]{:S(2)}, u32[]{:S(2)}) collective-permute-start(bf16[2,256,128]{2,1,0:T(8,128)(2,1)S(1)} %get-tuple-element.40), channel_id=1, source_target_pairs={{128,0},{32,8},{96,16},{64,24},{160,32},{0,40},{192,48},{224,56},{... | collective-permute-start | bytes 393224 | tf_op jit(solution)/shard_map/ppermute | solution.py:389
  68.6 1.8 %all-to-all-done.1 = bf16[8,24,1536]{2,1,0:T(8,128)(2,1)S(1)} async-done(((bf16[8,24,1536]{2,1,0:T(8,128)(2,1)}), bf16[8,24,1536]{2,1,0:T(8,128)(2,1)S(1)}, u32[]{:S(2)}, u32[]{:S(2)}) %all-to-all-start.1) | async-done | bytes 589856 | tf_op jit(solution)/shard_map/all_to_all | solution.py:411
  70.4 1.0 %shard_map.123 = (bf16[192,640]{1,0:T(8,128)(2,1)}, bf16[192,640]{1,0:T(8,128)(2,1)}, bf16[192,128]{1,0:T(8,128)(2,1)}, bf16[192,128]{1,0:T(8,128)(2,1)}) custom-call(bf16[192,1536]{1,0:T(8,128)(2,1)S(1)} %bitcast.25), custom_call_target="tpu_custom_call" | custom-call | flops 1000000000 | bytes 1179648 | tf_op jit(solution)/shard_map/pallas_call | solution.py:87
  71.4 8.0 %collective-permute-done.8 = bf16[2,256,128]{2,1,0:T(8,128)(2,1)S(1)} collective-permute-done((bf16[2,256,128]{2,1,0:T(8,128)(2,1)S(1)}, bf16[2,256,128]{2,1,0:T(8,128)(2,1)S(1)}, u32[]{:S(2)}, u32[]{:S(2)}) %collective-permute-start.8) | collective-permute-done | bytes 131104 | tf_op jit(solution)/shard_map/ppermute | solution.py:389
  79.4 0.0 collective-permute-done.9
  79.4 0.7 convert_add_fusion
  (2 shorter events, 0.0 us)
Async XLA Ops:
  2.8 7.4 %copy-start.1 = (bf16[256,1,128]{2,0,1:T(8,128)(2,1)S(1)}, bf16[256,1,128]{2,0,1:T(8,128)(2,1)}, u32[]{:S(2)}) copy-start(bf16[256,1,128]{2,0,1:T(8,128)(2,1)} %param.12) | copy-start | bytes 196612
  2.8 7.4 %copy-start.2 = (bf16[256,1,128]{2,0,1:T(8,128)(2,1)S(1)}, bf16[256,1,128]{2,0,1:T(8,128)(2,1)}, u32[]{:S(2)}) copy-start(bf16[256,1,128]{2,0,1:T(8,128)(2,1)} %param.11) | copy-start | bytes 196612
  2.8 28.5 %all-to-all-start = ((bf16[8,24,1536]{2,1,0:T(8,128)(2,1)}), bf16[8,24,1536]{2,1,0:T(8,128)(2,1)S(1)}, u32[]{:S(2)}, u32[]{:S(2)}) async-start(bf16[8,24,1536]{2,1,0:T(8,128)(2,1)} %bitcast.28), calls=%async_computation | async-start | bytes 1179648 | tf_op jit(solution)/shard_map/all_to_all | solution.py:401
  10.3 10.9 %collective-permute-start.1 = (bf16[2,256,128]{2,1,0:T(8,128)(2,1)S(1)}, bf16[2,256,128]{2,1,0:T(8,128)(2,1)S(1)}, u32[]{:S(2)}, u32[]{:S(2)}) collective-permute-start(bf16[2,256,128]{2,1,0:T(8,128)(2,1)S(1)} %pad_maximum_fusion.1), channel_id=1, source_target_pairs={{0,128},{8,32},{16,96},{24,64},{32,160},{40,0},{48,192},{56,224},{... | collective-permute-start | bytes 393224 | tf_op jit(solution)/shard_map/ppermute | solution.py:398
  15.1 10.5 %collective-permute-start = (bf16[2,256,128]{2,1,0:T(8,128)(2,1)S(1)}, bf16[2,256,128]{2,1,0:T(8,128)(2,1)S(1)}, u32[]{:S(2)}, u32[]{:S(2)}) collective-permute-start(bf16[2,256,128]{2,1,0:T(8,128)(2,1)S(1)} %pad_maximum_fusion.1), channel_id=1, source_target_pairs={{0,0},{8,160},{16,224},{24,192},{32,32},{40,128},{48,64},{56,96},{... | collective-permute-start | bytes 393224 | tf_op jit(solution)/shard_map/ppermute | solution.py:398
  25.7 5.6 %copy-start = (s32[32]{0:T(128)S(1)}, s32[32]{0:T(128)}, u32[]{:S(2)}) copy-start(s32[32]{0:T(128)} %len_ref.5) | copy-start | bytes 388
  25.7 10.5 %collective-permute-start.4 = (bf16[2,2,256,128]{3,2,1,0:T(8,128)(2,1)S(1)}, bf16[2,2,256,128]{3,2,1,0:T(8,128)(2,1)S(1)}, u32[]{:S(2)}, u32[]{:S(2)}) collective-permute-start(bf16[2,2,256,128]{3,2,1,0:T(8,128)(2,1)S(1)} %pad_maximum_fusion), channel_id=1, source_target_pairs={{0,64},{8,200},{16,80},{24,216},{32,96},{40,232},{48,112},{56,248}... | collective-permute-start | bytes 786440 | tf_op jit(solution)/shard_map/ppermute | solution.py:394
  27.0 12.0 %collective-permute-start.3 = (bf16[2,2,256,128]{3,2,1,0:T(8,128)(2,1)S(1)}, bf16[2,2,256,128]{3,2,1,0:T(8,128)(2,1)S(1)}, u32[]{:S(2)}, u32[]{:S(2)}) collective-permute-start(bf16[2,2,256,128]{3,2,1,0:T(8,128)(2,1)S(1)} %pad_maximum_fusion), channel_id=1, source_target_pairs={{0,224},{8,40},{16,240},{24,56},{32,0},{40,72},{48,16},{56,88},{64... | collective-permute-start | bytes 786440 | tf_op jit(solution)/shard_map/ppermute | solution.py:394
  31.3 10.7 %collective-permute-start.2 = (bf16[2,2,256,128]{3,2,1,0:T(8,128)(2,1)S(1)}, bf16[2,2,256,128]{3,2,1,0:T(8,128)(2,1)S(1)}, u32[]{:S(2)}, u32[]{:S(2)}) collective-permute-start(bf16[2,2,256,128]{3,2,1,0:T(8,128)(2,1)S(1)} %pad_maximum_fusion), channel_id=1, source_target_pairs={{0,32},{8,232},{16,48},{24,248},{32,64},{40,8},{48,80},{56,24},{64... | collective-permute-start | bytes 786440 | tf_op jit(solution)/shard_map/ppermute | solution.py:394
  48.5 13.4 %collective-permute-start.5 = (bf16[2,2,256,128]{3,2,1,0:T(8,128)(2,1)S(1)}, bf16[2,2,256,128]{3,2,1,0:T(8,128)(2,1)S(1)}, u32[]{:S(2)}, u32[]{:S(2)}) collective-permute-start(bf16[2,2,256,128]{3,2,1,0:T(8,128)(2,1)S(1)} %get-tuple-element.36), channel_id=1, source_target_pairs={{0,224},{8,40},{16,240},{24,56},{32,0},{40,72},{48,16},{56,88},{64... | collective-permute-start | bytes 786440 | tf_op jit(solution)/shard_map/ppermute | solution.py:394
  48.6 13.3 %collective-permute-start.6 = (bf16[2,2,256,128]{3,2,1,0:T(8,128)(2,1)S(1)}, bf16[2,2,256,128]{3,2,1,0:T(8,128)(2,1)S(1)}, u32[]{:S(2)}, u32[]{:S(2)}) collective-permute-start(bf16[2,2,256,128]{3,2,1,0:T(8,128)(2,1)S(1)} %get-tuple-element.37), channel_id=1, source_target_pairs={{0,32},{8,232},{16,48},{24,248},{32,64},{40,8},{48,80},{56,24},{64... | collective-permute-start | bytes 786440 | tf_op jit(solution)/shard_map/ppermute | solution.py:394
  50.6 11.3 %collective-permute-start.7 = (bf16[2,2,256,128]{3,2,1,0:T(8,128)(2,1)S(1)}, bf16[2,2,256,128]{3,2,1,0:T(8,128)(2,1)S(1)}, u32[]{:S(2)}, u32[]{:S(2)}) collective-permute-start(bf16[2,2,256,128]{3,2,1,0:T(8,128)(2,1)S(1)} %get-tuple-element.38), channel_id=1, source_target_pairs={{0,192},{8,72},{16,208},{24,88},{32,224},{40,104},{48,240},{56,120... | collective-permute-start | bytes 786440 | tf_op jit(solution)/shard_map/ppermute | solution.py:394
  55.3 15.1 %all-to-all-start.1 = ((bf16[8,24,1536]{2,1,0:T(8,128)(2,1)}), bf16[8,24,1536]{2,1,0:T(8,128)(2,1)S(1)}, u32[]{:S(2)}, u32[]{:S(2)}) async-start(bf16[8,24,1536]{2,1,0:T(8,128)(2,1)} %bitcast.10), calls=%async_computation.1 | async-start | bytes 1179648 | tf_op jit(solution)/shard_map/all_to_all | solution.py:411
  62.1 17.3 %collective-permute-start.8 = (bf16[2,256,128]{2,1,0:T(8,128)(2,1)S(1)}, bf16[2,256,128]{2,1,0:T(8,128)(2,1)S(1)}, u32[]{:S(2)}, u32[]{:S(2)}) collective-permute-start(bf16[2,256,128]{2,1,0:T(8,128)(2,1)S(1)} %get-tuple-element.39), channel_id=1, source_target_pairs={{0,0},{160,8},{224,16},{192,24},{32,32},{128,40},{64,48},{96,56},{... | collective-permute-start | bytes 393224 | tf_op jit(solution)/shard_map/ppermute | solution.py:389
  66.6 12.8 %collective-permute-start.9 = (bf16[2,256,128]{2,1,0:T(8,128)(2,1)S(1)}, bf16[2,256,128]{2,1,0:T(8,128)(2,1)S(1)}, u32[]{:S(2)}, u32[]{:S(2)}) collective-permute-start(bf16[2,256,128]{2,1,0:T(8,128)(2,1)S(1)} %get-tuple-element.40), channel_id=1, source_target_pairs={{128,0},{32,8},{96,16},{64,24},{160,32},{0,40},{192,48},{224,56},{... | collective-permute-start | bytes 393224 | tf_op jit(solution)/shard_map/ppermute | solution.py:389

commit v6 on v5

--- a/solution.py
+++ b/solution.py
@@ -350,6 +350,18 @@
     return outs[0], outs[1:]
 
 
+def pair_kernel(first_ref, second_ref, out_ref):
+    out_ref[0] = first_ref[...]
+    out_ref[1] = second_ref[...]
+
+
+def pair_up(held):
+    shape = (len(held),) + held[0].shape
+    return call(
+        pair_kernel, 12, list(held), [jax.ShapeDtypeStruct(shape, bf16)], [], 8, scalars=0
+    )[0]
+
+
 def sum_kernel(count, *refs):
     for i in range(count):
         total = refs[i][...]
@@ -401,7 +413,7 @@
     x = lax.all_to_all(packed, "head", split_axis=0, concat_axis=0, tiled=True)
 
     held, steps = [own, across], (1, -1, 2)
-    both = jnp.stack(held)
+    both = pair_up(held)
     far = [shift(both, step) for step in steps]
     stats = near_stats(comp_len, x, held, group, scale)
     grads, totals = far_pass(comp_len, x, stats, far, group, scale)

time: 81.5 us -> 75.9 us (0.931)
  waiting for transfers between devices: 24.9 us -> 17.8 us
  other arithmetic: 0.77 us -> 1.61 us
    ppermute x2, waiting for transfers between devices: 6.34 us -> 0.01 us  [on_device(): lax.ppermute(prefix, 'seq', spread(steps))]
    all_to_all x1, waiting for transfers between devices: 0.01 us -> 5.14 us  [on_device(): x = lax.all_to_all(packed, 'head', split_axis=0, concat_axis=0, tiled=True)]
    ppermute x6, waiting for transfers between devices: 8.75 us -> 4.64 us  [shift(): return lax.ppermute(x, 'seq', pairs)]
    ppermute x6, starting transfers between devices: 7.72 us -> 6.08 us  [shift(): return lax.ppermute(x, 'seq', pairs)]
    ppermute x2, starting transfers between devices: 6.56 us -> 7.85 us  [collect(): return lax.ppermute(x, 'seq', [(b, a) for a, b in spread(steps)])]
    ppermute x2, waiting for transfers between devices: 8 us -> 7.03 us  [collect(): return lax.ppermute(x, 'seq', [(b, a) for a, b in spread(steps)])]
    another operation x1, other arithmetic: 0.02 us -> 0.89 us  [on_device(): prefix = jnp.stack([prefix_k[:, 0], prefix_v[:, 0]])]
    pallas_call x4 -> x5, Pallas kernels: 13.3 us -> 13.3 us  [call(): pl.pallas_call(body, out_shape=outs, in_specs=[smem] * scalars + [vmem] *...]
  transfers between devices with their start and end apart: 12 -> 12, of which waited for: 7 -> 5; matrix products, arithmetic and copies ran while one was open for 0% -> 0% of each run, Pallas kernels for 10% -> 13%
where the time goes in v6:
time: 75.9 us; the launch traced here: 74.6 us
  starting transfers between devices  38 us (50%)
  waiting for transfers between devices  17.8 us (23%)
  Pallas kernels  16.4 us (22%)
  other arithmetic  1.61 us (2%)
    pallas_call x5, Pallas kernels, call(): pl.pallas_call(body, out_shape=outs, in_specs=[smem] * scalars + [vmem] *...  13.3 us
    ppermute x2, starting transfers between devices, on_device(): lax.ppermute(prefix, 'seq', spread(steps))  9.62 us
    ppermute x2, starting transfers between devices, collect(): return lax.ppermute(x, 'seq', [(b, a) for a, b in spread(steps)])  7.85 us
    all_to_all x1, starting transfers between devices, on_device(): x = lax.all_to_all(packed, 'head', split_axis=0, concat_axis=0, tiled=True)  7.26 us
    all_to_all x1, starting transfers between devices, on_device(): back = lax.all_to_all(out, 'head', split_axis=0, concat_axis=0, tiled=True)  7.19 us
    ppermute x2, waiting for transfers between devices, collect(): return lax.ppermute(x, 'seq', [(b, a) for a, b in spread(steps)])  7.03 us
    ppermute x6, starting transfers between devices, shift(): return lax.ppermute(x, 'seq', pairs)  6.08 us
    all_to_all x1, waiting for transfers between devices, on_device(): x = lax.all_to_all(packed, 'head', split_axis=0, concat_axis=0, tiled=True)  5.14 us
  transfers between devices with their start and end apart: 12, of which 5 were waited for; matrix products, arithmetic and copies ran while one was open for 0% of the time, Pallas kernels for 13%

profile of v6, /device:TPU:24, one launch (start us, length us, event | category | flops | bytes accessed | tf_op | source)
XLA Modules:
  0.0 74.6 jit_solution(11467502483411405369)
XLA Ops:
  0.6 0.9 %pad_maximum_fusion = bf16[2,256,128]{2,1,0:T(8,128)(2,1)S(1)} fusion(bf16[1,256,128]{2,1,0:T(8,128)(2,1)} %bitcast.27, bf16[1,256,128]{2,1,0:T(8,128)(2,1)} %bitcast.28), kind=kLoop, calls=%fused_computation | loop fusion | flops 65536 | bytes 262144 | tf_op jit(solution)/shard_map/stack | solution.py:409
  1.5 4.9 %collective-permute-start.1 = (bf16[2,256,128]{2,1,0:T(8,128)(2,1)S(1)}, bf16[2,256,128]{2,1,0:T(8,128)(2,1)S(1)}, u32[]{:S(2)}, u32[]{:S(2)}) collective-permute-start(bf16[2,256,128]{2,1,0:T(8,128)(2,1)S(1)} %pad_maximum_fusion), channel_id=1, source_target_pairs={{0,128},{8,32},{16,96},{24,64},{32,160},{40,0},{48,192},{56,224},{... | collective-permute-start | bytes 393224 | tf_op jit(solution)/shard_map/ppermute | solution.py:410
  6.4 4.7 %collective-permute-start = (bf16[2,256,128]{2,1,0:T(8,128)(2,1)S(1)}, bf16[2,256,128]{2,1,0:T(8,128)(2,1)S(1)}, u32[]{:S(2)}, u32[]{:S(2)}) collective-permute-start(bf16[2,256,128]{2,1,0:T(8,128)(2,1)S(1)} %pad_maximum_fusion), channel_id=1, source_target_pairs={{0,0},{8,160},{16,224},{24,192},{32,32},{40,128},{48,64},{56,96},{... | collective-permute-start | bytes 393224 | tf_op jit(solution)/shard_map/ppermute | solution.py:410
  11.1 2.2 %shard_map.118 = bf16[192,1536]{1,0:T(8,128)(2,1)} custom-call(bf16[192,640]{1,0:T(8,128)(2,1)} %bitcast.29, bf16[192,640]{1,0:T(8,128)(2,1)} %bitcast.30, bf16[192,128]{1,0:T(8,128)(2,1)} %bitcast.31, bf16[192,128]{1,0:T(8,128)(2,1)} %bitcast.32), custom_call_target="tpu_custom_call" | custom-call | flops 2000000000 | bytes 1179648 | tf_op jit(solution)/shard_map/pallas_call | solution.py:47
  13.3 7.3 %all-to-all-start = ((bf16[8,24,1536]{2,1,0:T(8,128)(2,1)}), bf16[8,24,1536]{2,1,0:T(8,128)(2,1)S(1)}, u32[]{:S(2)}, u32[]{:S(2)}) async-start(bf16[8,24,1536]{2,1,0:T(8,128)(2,1)} %bitcast.24), calls=%async_computation | async-start | bytes 1179648 | tf_op jit(solution)/shard_map/all_to_all | solution.py:413
  20.6 0.0 collective-permute-done.1.refs_1_.second_ref
  20.6 0.0 collective-permute-done.refs_0_.first_ref
  20.6 0.0 copy-start
  20.6 0.3 collective-permute-start.4
  20.9 3.7 %collective-permute-start.3 = (bf16[2,2,256,128]{3,2,1,0:T(8,128)(2,1)S(1)}, bf16[2,2,256,128]{3,2,1,0:T(8,128)(2,1)S(1)}, u32[]{:S(2)}, u32[]{:S(2)}) collective-permute-start(bf16[2,2,256,128]{3,2,1,0:T(8,128)(2,1)S(1)} %shard_map.120), channel_id=1, source_target_pairs={{0,224},{8,40},{16,240},{24,56},{32,0},{40,72},{48,16},{56,88},{64... | collective-permute-start | bytes 786440 | tf_op jit(solution)/shard_map/ppermute | solution.py:406
  24.6 0.0 collective-permute-start.2
  24.6 5.1 %all-to-all-done = bf16[8,24,1536]{2,1,0:T(8,128)(2,1)S(1)} async-done(((bf16[8,24,1536]{2,1,0:T(8,128)(2,1)}), bf16[8,24,1536]{2,1,0:T(8,128)(2,1)S(1)}, u32[]{:S(2)}, u32[]{:S(2)}) %all-to-all-start) | async-done | bytes 589856 | tf_op jit(solution)/shard_map/all_to_all | solution.py:413
  29.7 0.0 copy-done
  29.7 2.0 %shard_map.119.stats_ref = f32[3,960]{1,0:T(4,128)S(1)} custom-call(s32[32]{0:T(128)S(1)} %copy-done, bf16[192,1536]{1,0:T(8,128)(2,1)S(1)} %bitcast.20, bf16[2,256,128]{2,1,0:T(8,128)(2,1)S(1)} %collective-permute-done.refs_0_.first_ref, bf16[2,256,128]{2,1,0:T(8,128)(2,1)S(1)} %collective-permute-done.1.refs_1_.second_ref), custom_call_target="tpu_custom_call" | custom-call | flops 2300000000 | bytes 863616 | tf_op jit(solution)/shard_map/pallas_call | solution.py:282
  31.7 1.5 %collective-permute-done.4.refs_2_ = bf16[2,2,256,128]{3,2,1,0:T(8,128)(2,1)S(1)} collective-permute-done((bf16[2,2,256,128]{3,2,1,0:T(8,128)(2,1)S(1)}, bf16[2,2,256,128]{3,2,1,0:T(8,128)(2,1)S(1)}, u32[]{:S(2)}, u32[]{:S(2)}) %collective-permute-start.4) | collective-permute-done | bytes 262176 | tf_op jit(solution)/shard_map/ppermute | solution.py:406
  33.2 0.0 collective-permute-done.3.refs_1_
  33.2 3.1 %collective-permute-done.2.refs_0_ = bf16[2,2,256,128]{3,2,1,0:T(8,128)(2,1)S(1)} collective-permute-done((bf16[2,2,256,128]{3,2,1,0:T(8,128)(2,1)S(1)}, bf16[2,2,256,128]{3,2,1,0:T(8,128)(2,1)S(1)}, u32[]{:S(2)}, u32[]{:S(2)}) %collective-permute-start.2) | collective-permute-done | bytes 262176 | tf_op jit(solution)/shard_map/ppermute | solution.py:406
  36.3 6.4 %shard_map.121 = (bf16[2,2,256,128]{3,2,1,0:T(8,128)(2,1)S(1)}, bf16[2,2,256,128]{3,2,1,0:T(8,128)(2,1)S(1)}, bf16[2,2,256,128]{3,2,1,0:T(8,128)(2,1)S(1)}, f32[...) custom-call(s32[32]{0:T(128)S(1)} %copy-done, bf16[192,1536]{1,0:T(8,128)(2,1)S(1)} %bitcast.21, ...), custom_call_target="tpu_custom_call" | custom-call | flops 7474999808 | bytes 3165056 | tf_op jit(solution)/shard_map/pallas_call | solution.py:282
  42.8 0.4 collective-permute-start.5
  43.2 1.7 %collective-permute-start.6 = (bf16[2,2,256,128]{3,2,1,0:T(8,128)(2,1)S(1)}, bf16[2,2,256,128]{3,2,1,0:T(8,128)(2,1)S(1)}, u32[]{:S(2)}, u32[]{:S(2)}) collective-permute-start(bf16[2,2,256,128]{3,2,1,0:T(8,128)(2,1)S(1)} %get-tuple-element.37), channel_id=1, source_target_pairs={{0,32},{8,232},{16,48},{24,248},{32,64},{40,8},{48,80},{56,24},{64... | collective-permute-start | bytes 786440 | tf_op jit(solution)/shard_map/ppermute | solution.py:406
  44.9 0.0 collective-permute-start.7
  44.9 4.7 %shard_map.122 = (bf16[192,1536]{1,0:T(8,128)(2,1)}, f32[2,256,128]{2,1,0:T(8,128)S(1)}, f32[2,256,128]{2,1,0:T(8,128)S(1)}) custom-call(s32[32]{0:T(128)S(1)} %copy-done, bf16[192,1536]{1,0:T(8,128)(2,1)S(1)} %bitcast.22, f32[2,960]{1,0:T(2,128)S(1)} %get-tuple-element.31.total_ref, f32[128,960]{1,0:T(8,128)S(1)} %get-tuple-element.32.ot_ref, ...), custom_call_target="tpu_custom_call" | custom-call | flops 5750000128 | bytes 2956928 | tf_op jit(solution)/shard_map/pallas_call | solution.py:282
  49.6 7.2 %all-to-all-start.1 = ((bf16[8,24,1536]{2,1,0:T(8,128)(2,1)}), bf16[8,24,1536]{2,1,0:T(8,128)(2,1)S(1)}, u32[]{:S(2)}, u32[]{:S(2)}) async-start(bf16[8,24,1536]{2,1,0:T(8,128)(2,1)} %bitcast.8), calls=%async_computation.1 | async-start | bytes 1179648 | tf_op jit(solution)/shard_map/all_to_all | solution.py:423
  56.8 0.0 collective-permute-done.5.refs_2_
  56.8 0.0 collective-permute-done.6.refs_3_
  56.8 0.0 collective-permute-done.7.refs_4_
  56.9 0.1 shard_map.123
  57.0 3.4 %collective-permute-start.8 = (bf16[2,256,128]{2,1,0:T(8,128)(2,1)S(1)}, bf16[2,256,128]{2,1,0:T(8,128)(2,1)S(1)}, u32[]{:S(2)}, u32[]{:S(2)}) collective-permute-start(bf16[2,256,128]{2,1,0:T(8,128)(2,1)S(1)} %get-tuple-element.39), channel_id=1, source_target_pairs={{0,0},{160,8},{224,16},{192,24},{32,32},{128,40},{64,48},{96,56},{... | collective-permute-start | bytes 393224 | tf_op jit(solution)/shard_map/ppermute | solution.py:401
  60.4 4.4 %collective-permute-start.9 = (bf16[2,256,128]{2,1,0:T(8,128)(2,1)S(1)}, bf16[2,256,128]{2,1,0:T(8,128)(2,1)S(1)}, u32[]{:S(2)}, u32[]{:S(2)}) collective-permute-start(bf16[2,256,128]{2,1,0:T(8,128)(2,1)S(1)} %get-tuple-element.40), channel_id=1, source_target_pairs={{128,0},{32,8},{96,16},{64,24},{160,32},{0,40},{192,48},{224,56},{... | collective-permute-start | bytes 393224 | tf_op jit(solution)/shard_map/ppermute | solution.py:401
  64.8 1.0 %all-to-all-done.1 = bf16[8,24,1536]{2,1,0:T(8,128)(2,1)S(1)} async-done(((bf16[8,24,1536]{2,1,0:T(8,128)(2,1)}), bf16[8,24,1536]{2,1,0:T(8,128)(2,1)S(1)}, u32[]{:S(2)}, u32[]{:S(2)}) %all-to-all-start.1) | async-done | bytes 589856 | tf_op jit(solution)/shard_map/all_to_all | solution.py:423
  65.9 1.0 %shard_map.124 = (bf16[192,640]{1,0:T(8,128)(2,1)}, bf16[192,640]{1,0:T(8,128)(2,1)}, bf16[192,128]{1,0:T(8,128)(2,1)}, bf16[192,128]{1,0:T(8,128)(2,1)}) custom-call(bf16[192,1536]{1,0:T(8,128)(2,1)S(1)} %bitcast.23), custom_call_target="tpu_custom_call" | custom-call | flops 1000000000 | bytes 1179648 | tf_op jit(solution)/shard_map/pallas_call | solution.py:87
  66.8 7.0 %collective-permute-done.8 = bf16[2,256,128]{2,1,0:T(8,128)(2,1)S(1)} collective-permute-done((bf16[2,256,128]{2,1,0:T(8,128)(2,1)S(1)}, bf16[2,256,128]{2,1,0:T(8,128)(2,1)S(1)}, u32[]{:S(2)}, u32[]{:S(2)}) %collective-permute-start.8) | collective-permute-done | bytes 131104 | tf_op jit(solution)/shard_map/ppermute | solution.py:401
  73.9 0.0 collective-permute-done.9
  73.9 0.7 convert_add_fusion
  (1 shorter events, 0.0 us)
Async XLA Ops:
  1.5 19.1 %collective-permute-start.1 = (bf16[2,256,128]{2,1,0:T(8,128)(2,1)S(1)}, bf16[2,256,128]{2,1,0:T(8,128)(2,1)S(1)}, u32[]{:S(2)}, u32[]{:S(2)}) collective-permute-start(bf16[2,256,128]{2,1,0:T(8,128)(2,1)S(1)} %pad_maximum_fusion), channel_id=1, source_target_pairs={{0,128},{8,32},{16,96},{24,64},{32,160},{40,0},{48,192},{56,224},{... | collective-permute-start | bytes 393224 | tf_op jit(solution)/shard_map/ppermute | solution.py:410
  6.4 14.2 %collective-permute-start = (bf16[2,256,128]{2,1,0:T(8,128)(2,1)S(1)}, bf16[2,256,128]{2,1,0:T(8,128)(2,1)S(1)}, u32[]{:S(2)}, u32[]{:S(2)}) collective-permute-start(bf16[2,256,128]{2,1,0:T(8,128)(2,1)S(1)} %pad_maximum_fusion), channel_id=1, source_target_pairs={{0,0},{8,160},{16,224},{24,192},{32,32},{40,128},{48,64},{56,96},{... | collective-permute-start | bytes 393224 | tf_op jit(solution)/shard_map/ppermute | solution.py:410
  13.3 16.4 %all-to-all-start = ((bf16[8,24,1536]{2,1,0:T(8,128)(2,1)}), bf16[8,24,1536]{2,1,0:T(8,128)(2,1)S(1)}, u32[]{:S(2)}, u32[]{:S(2)}) async-start(bf16[8,24,1536]{2,1,0:T(8,128)(2,1)} %bitcast.24), calls=%async_computation | async-start | bytes 1179648 | tf_op jit(solution)/shard_map/all_to_all | solution.py:413
  20.6 9.1 %copy-start = (s32[32]{0:T(128)S(1)}, s32[32]{0:T(128)}, u32[]{:S(2)}) copy-start(s32[32]{0:T(128)} %len_ref.5) | copy-start | bytes 388
  20.6 12.6 %collective-permute-start.4 = (bf16[2,2,256,128]{3,2,1,0:T(8,128)(2,1)S(1)}, bf16[2,2,256,128]{3,2,1,0:T(8,128)(2,1)S(1)}, u32[]{:S(2)}, u32[]{:S(2)}) collective-permute-start(bf16[2,2,256,128]{3,2,1,0:T(8,128)(2,1)S(1)} %shard_map.120), channel_id=1, source_target_pairs={{0,64},{8,200},{16,80},{24,216},{32,96},{40,232},{48,112},{56,248}... | collective-permute-start | bytes 786440 | tf_op jit(solution)/shard_map/ppermute | solution.py:406
  20.9 12.3 %collective-permute-start.3 = (bf16[2,2,256,128]{3,2,1,0:T(8,128)(2,1)S(1)}, bf16[2,2,256,128]{3,2,1,0:T(8,128)(2,1)S(1)}, u32[]{:S(2)}, u32[]{:S(2)}) collective-permute-start(bf16[2,2,256,128]{3,2,1,0:T(8,128)(2,1)S(1)} %shard_map.120), channel_id=1, source_target_pairs={{0,224},{8,40},{16,240},{24,56},{32,0},{40,72},{48,16},{56,88},{64... | collective-permute-start | bytes 786440 | tf_op jit(solution)/shard_map/ppermute | solution.py:406
  24.6 11.7 %collective-permute-start.2 = (bf16[2,2,256,128]{3,2,1,0:T(8,128)(2,1)S(1)}, bf16[2,2,256,128]{3,2,1,0:T(8,128)(2,1)S(1)}, u32[]{:S(2)}, u32[]{:S(2)}) collective-permute-start(bf16[2,2,256,128]{3,2,1,0:T(8,128)(2,1)S(1)} %shard_map.120), channel_id=1, source_target_pairs={{0,32},{8,232},{16,48},{24,248},{32,64},{40,8},{48,80},{56,24},{64... | collective-permute-start | bytes 786440 | tf_op jit(solution)/shard_map/ppermute | solution.py:406
  42.8 14.0 %collective-permute-start.5 = (bf16[2,2,256,128]{3,2,1,0:T(8,128)(2,1)S(1)}, bf16[2,2,256,128]{3,2,1,0:T(8,128)(2,1)S(1)}, u32[]{:S(2)}, u32[]{:S(2)}) collective-permute-start(bf16[2,2,256,128]{3,2,1,0:T(8,128)(2,1)S(1)} %get-tuple-element.36), channel_id=1, source_target_pairs={{0,224},{8,40},{16,240},{24,56},{32,0},{40,72},{48,16},{56,88},{64... | collective-permute-start | bytes 786440 | tf_op jit(solution)/shard_map/ppermute | solution.py:406
  43.2 13.7 %collective-permute-start.6 = (bf16[2,2,256,128]{3,2,1,0:T(8,128)(2,1)S(1)}, bf16[2,2,256,128]{3,2,1,0:T(8,128)(2,1)S(1)}, u32[]{:S(2)}, u32[]{:S(2)}) collective-permute-start(bf16[2,2,256,128]{3,2,1,0:T(8,128)(2,1)S(1)} %get-tuple-element.37), channel_id=1, source_target_pairs={{0,32},{8,232},{16,48},{24,248},{32,64},{40,8},{48,80},{56,24},{64... | collective-permute-start | bytes 786440 | tf_op jit(solution)/shard_map/ppermute | solution.py:406
  44.9 12.0 %collective-permute-start.7 = (bf16[2,2,256,128]{3,2,1,0:T(8,128)(2,1)S(1)}, bf16[2,2,256,128]{3,2,1,0:T(8,128)(2,1)S(1)}, u32[]{:S(2)}, u32[]{:S(2)}) collective-permute-start(bf16[2,2,256,128]{3,2,1,0:T(8,128)(2,1)S(1)} %get-tuple-element.38), channel_id=1, source_target_pairs={{0,192},{8,72},{16,208},{24,88},{32,224},{40,104},{48,240},{56,120... | collective-permute-start | bytes 786440 | tf_op jit(solution)/shard_map/ppermute | solution.py:406
  49.6 16.2 %all-to-all-start.1 = ((bf16[8,24,1536]{2,1,0:T(8,128)(2,1)}), bf16[8,24,1536]{2,1,0:T(8,128)(2,1)S(1)}, u32[]{:S(2)}, u32[]{:S(2)}) async-start(bf16[8,24,1536]{2,1,0:T(8,128)(2,1)} %bitcast.8), calls=%async_computation.1 | async-start | bytes 1179648 | tf_op jit(solution)/shard_map/all_to_all | solution.py:423
  57.0 16.9 %collective-permute-start.8 = (bf16[2,256,128]{2,1,0:T(8,128)(2,1)S(1)}, bf16[2,256,128]{2,1,0:T(8,128)(2,1)S(1)}, u32[]{:S(2)}, u32[]{:S(2)}) collective-permute-start(bf16[2,256,128]{2,1,0:T(8,128)(2,1)S(1)} %get-tuple-element.39), channel_id=1, source_target_pairs={{0,0},{160,8},{224,16},{192,24},{32,32},{128,40},{64,48},{96,56},{... | collective-permute-start | bytes 393224 | tf_op jit(solution)/shard_map/ppermute | solution.py:401
  60.4 13.5 %collective-permute-start.9 = (bf16[2,256,128]{2,1,0:T(8,128)(2,1)S(1)}, bf16[2,256,128]{2,1,0:T(8,128)(2,1)S(1)}, u32[]{:S(2)}, u32[]{:S(2)}) collective-permute-start(bf16[2,256,128]{2,1,0:T(8,128)(2,1)S(1)} %get-tuple-element.40), channel_id=1, source_target_pairs={{128,0},{32,8},{96,16},{64,24},{160,32},{0,40},{192,48},{224,56},{... | collective-permute-start | bytes 393224 | tf_op jit(solution)/shard_map/ppermute | solution.py:401
